TPU v7x, 32 devices: a whole 2x2x4 slice. The times are simulated.
32 devices in a mesh: owner: 4 (over y, core), tensor: 8 (over z, x).
Axes of the slice: x: 2, y: 2, z: 4, core: 2. Of those that a mesh axis runs over, the one named last changes fastest.
Arguments:
- hidden: bfloat16 [128, 2048], P('owner', 'tensor'), may hold values from -6 to 6
- attention_gain: bfloat16 [2048], replicated, may hold values from 0.5 to 1.5
- query_weight: bfloat16 [9216, 2048], P('tensor'), may hold values from -1 to 1
- out_weight: bfloat16 [2048, 8192], P('tensor'), may hold values from -1.796875 to 1.796875
- root_cache: bfloat16 [32768, 576], P('tensor'), may hold values from -4 to 4
- group_cache: bfloat16 [48, 1024, 576], P('owner', 'tensor'), may hold values from -4 to 4
- group_length: int32 [48], P('owner'), may hold values from 128 to 1024, as said below
- suffix_cache: bfloat16 [128, 512, 576], P('owner', 'tensor'), may hold values from -4 to 4
- suffix_length: int32 [128], P('owner'), may hold values from 1 to 512, as said below
- group_of: int32 [128], P('owner'), may hold values from 0 to 47, as said below
- mixture_gain: bfloat16 [2048], replicated, may hold values from 0.5 to 1.5
- routes: int32 [128, 6], P('owner'), may hold values from 0 to 31, all different within a row; in each aligned block of 32 rows (0 to 31, 32 to 63, ...) at most 12 rows name the same one
- route_weight: float32 [128, 6], P('owner'), may hold values from 0.1 to 1
- expert_gate: bfloat16 [32, 1408, 2048], P(('owner', 'tensor')), may hold values from -0.125 to 0.125
- expert_up: bfloat16 [32, 1408, 2048], P(('owner', 'tensor')), may hold values from -0.125 to 0.125
- expert_down: bfloat16 [32, 1408, 2048], P(('owner', 'tensor')), may hold values from -0.15625 to 0.15625
- shared_gate: bfloat16 [2816, 2048], P('tensor'), may hold values from -0.125 to 0.125
- shared_up: bfloat16 [2816, 2048], P('tensor'), may hold values from -0.125 to 0.125
- shared_down: bfloat16 [2816, 2048], P('tensor'), may hold values from -0.109375 to 0.109375
Outputs:
- layer_out: bfloat16 [128, 2048], P('owner', 'tensor')
Inputs may be any that keep to these rules, and one draw needn't show every extreme that they name: `group_of`: the groups of owner o are o * 12 to (o + 1) * 12 - 1. Among the requests of one owner (rows o * 32 to (o + 1) * 32 - 1), at most 16 have their group on any one owner, and some owner gets exactly 16 of them. `group_length`: some group prompt uses all 1024 positions. `suffix_length`: some request uses all 512 suffix positions. `routes`: each row names 6 different experts; among the rows of one owner no expert is named more than 12 times, and that is reached.
All inputs are finite; a program needn't handle non-finite values.
Results may differ from a plain program's by a relative error of at most 0.012.
The roundings to bfloat16 on the way count: a program that leaves them out, or rounds other values in their place, can miss the bound.
Values may be sent and summed in bfloat16 or wider, within the bound.
No kernel may reach another device: no remote copies, remote signals or barrier semaphores. Data moves between devices by JAX's collectives and lax.ppermute only.
A program may use at most 128 MiB of HBM per device.

v0:
```python
import jax
import jax.numpy as jnp
from jax import lax
from jax.sharding import PartitionSpec as P

H = 16
LAT = 512
KVW = 576
EXP_OWN = 8
GROUP_OWN = 12


score_scale = 192.0 ** (-0.5)
lowest = -1e30
epsilon = 1e-06


def combined_all(x, axis, combine):
    everything = jax.tree.map(lambda part: lax.all_gather(part, axis), x)
    first = jax.tree.map(lambda part: part[0], everything)

    def turn(k, so_far):
        return combine(so_far, jax.tree.map(lambda part: part[k], everything))

    return lax.fori_loop(1, lax.axis_size(axis), turn, first)


def rms_rows(values, gain_vector):
    values = values.astype(jnp.float32)
    scaled = values * lax.rsqrt(jnp.mean(values * values, axis=-1, keepdims=True) + epsilon)
    return scaled * gain_vector.astype(jnp.float32)


def block_weights(scores, usable):
    masked = jnp.where(usable, scores, lowest)
    peak_score = jnp.max(masked, axis=-1, keepdims=True)
    weights = jnp.where(usable, jnp.exp(masked - peak_score), 0.0)
    return (peak_score[..., 0], weights, jnp.sum(weights, axis=-1))


def finish(peak_score, numerator, total_mass):
    present = total_mass > 0.0
    safe_total = jnp.where(present, total_mass, 1.0)
    return (
        numerator / safe_total[..., None],
        jnp.where(present, peak_score + jnp.log(safe_total), lowest),
    )


def join_partials(first, second):
    first_out, first_mass = first
    second_out, second_mass = second
    peak_mass = jnp.maximum(first_mass, second_mass)
    first_weight = jnp.exp(first_mass - peak_mass)
    second_weight = jnp.exp(second_mass - peak_mass)
    total_weight = first_weight + second_weight
    joined = (
        first_weight[..., None] * first_out + second_weight[..., None] * second_out
    ) / total_weight[..., None]
    return (joined, peak_mass + jnp.log(total_weight))


def group_partial(query_rows, cache_block, usable):
    scores = (
        jnp.einsum(
            "...hc,...pc->...hp", query_rows, cache_block, preferred_element_type=jnp.float32
        )
        * score_scale
    )
    peak_score, weights, total_mass = block_weights(scores, usable[..., None, :])
    numerator = jnp.einsum(
        "...hp,...pl->...hl",
        weights.astype(jnp.bfloat16),
        cache_block[..., :LAT],
        preferred_element_type=jnp.float32,
    )
    block_out, log_mass = finish(peak_score, numerator, total_mass)
    return (block_out.astype(jnp.bfloat16), log_mass)


def local(
    hidden,
    attention_gain,
    query_weight,
    out_weight,
    root_cache,
    group_cache,
    group_length,
    suffix_cache,
    suffix_length,
    group_of,
    mixture_gain,
    routes,
    route_weight,
    expert_gate,
    expert_up,
    expert_down,
    shared_gate,
    shared_up,
    shared_down,
):
    owners = lax.axis_size("owner")
    tensor_index = lax.axis_index("tensor")
    requests = hidden.shape[0]
    rows_full = lax.all_gather(hidden, "tensor", axis=1, tiled=True)
    normed = rms_rows(rows_full, attention_gain).astype(jnp.bfloat16)
    projected = lax.dot_general(
        normed, query_weight, (((1,), (1,)), ((), ())), preferred_element_type=jnp.float32
    ).astype(jnp.bfloat16)
    projected = lax.all_gather(projected, "tensor", axis=1, tiled=True)
    queries = projected.reshape(requests, H, KVW)
    root_scores = (
        jnp.einsum("rhc,pc->rhp", queries, root_cache, preferred_element_type=jnp.float32)
        * score_scale
    )
    root_peak = jnp.max(root_scores, axis=-1, keepdims=True)
    root_weights = jnp.exp(root_scores - root_peak)
    root_numerator = jnp.einsum(
        "rhp,pl->rhl",
        root_weights.astype(jnp.bfloat16),
        root_cache[:, :LAT],
        preferred_element_type=jnp.float32,
    )
    root_mass = jnp.sum(root_weights, axis=-1)
    root_part = (root_numerator / root_mass[..., None], root_peak[..., 0] + jnp.log(root_mass))
    suffix_span = suffix_cache.shape[1]
    suffix_positions = tensor_index * suffix_span + jnp.arange(suffix_span)
    suffix_usable = suffix_positions[None, :] < suffix_length[:, None]
    suffix_scores = (
        jnp.einsum("rhc,rpc->rhp", queries, suffix_cache, preferred_element_type=jnp.float32)
        * score_scale
    )
    suffix_peak, suffix_weights, suffix_mass = block_weights(
        suffix_scores, suffix_usable[:, None, :]
    )
    suffix_numerator = jnp.einsum(
        "rhp,rpl->rhl",
        suffix_weights.astype(jnp.bfloat16),
        suffix_cache[:, :, :LAT],
        preferred_element_type=jnp.float32,
    )
    suffix_part = finish(suffix_peak, suffix_numerator, suffix_mass)
    group_span = group_cache.shape[1]
    group_positions = tensor_index * group_span + jnp.arange(group_span)
    capacity = 2 * requests // owners
    destination = group_of // GROUP_OWN
    local_group = group_of % GROUP_OWN
    matches = (destination[:, None] == jnp.arange(owners)[None, :]).astype(jnp.int32)
    slot_rank = jnp.sum((jnp.cumsum(matches, axis=0) - matches) * matches, axis=1)
    slot_index = destination * capacity + slot_rank
    send_rows = jnp.zeros((owners * capacity, H * KVW), jnp.bfloat16).at[slot_index].set(projected)
    send_groups = jnp.full((owners * capacity,), -1, jnp.int32).at[slot_index].set(local_group)
    arrived_rows = lax.all_to_all(
        send_rows.reshape(owners, capacity, H * KVW),
        "owner",
        split_axis=0,
        concat_axis=0,
        tiled=True,
    )
    group_ids = lax.all_to_all(
        send_groups.reshape(owners, capacity), "owner", split_axis=0, concat_axis=0, tiled=True
    )
    slot_count = arrived_rows.shape[1]
    present = group_ids >= 0
    chosen = jnp.where(present, group_ids, 0)
    cache_block = group_cache[chosen]
    lengths = group_length[chosen]
    usable = present[..., None] & (group_positions < lengths[..., None])
    block_out, log_mass = group_partial(
        arrived_rows.reshape(owners, slot_count, H, KVW), cache_block, usable
    )
    returned_out = lax.all_to_all(block_out, "owner", split_axis=0, concat_axis=0, tiled=True)
    returned_mass = lax.all_to_all(log_mass, "owner", split_axis=0, concat_axis=0, tiled=True)
    group_out = returned_out.reshape(owners * capacity, H, LAT)[slot_index]
    group_mass = returned_mass.reshape(owners * capacity, H)[slot_index]
    local_part = join_partials(
        join_partials(root_part, suffix_part), (group_out.astype(jnp.float32), group_mass)
    )
    merged_out, merged_mass = combined_all(local_part, "tensor", join_partials)
    attention = merged_out.astype(jnp.bfloat16).reshape(requests, H * LAT)
    mid = (
        hidden.astype(jnp.float32)
        + lax.dot_general(
            attention, out_weight, (((1,), (1,)), ((), ())), preferred_element_type=jnp.float32
        )
    ).astype(jnp.bfloat16)
    mid_full = lax.all_gather(mid, "tensor", axis=1, tiled=True)
    mixture_in = rms_rows(mid_full, mixture_gain).astype(jnp.bfloat16)
    fsplit = lax.axis_size("tensor") // EXP_OWN
    my_local = tensor_index // fsplit
    fanout = routes.shape[1]
    model_width = mixture_in.shape[1]
    capacity_expert = 2 * requests * fanout // (EXP_OWN * owners)
    gate_rows = expert_gate[0]
    up_rows = expert_up[0]
    down_rows = expert_down[0]
    owner_range = jnp.arange(owners)
    targets = owner_range * EXP_OWN + my_local
    route_hits = routes[:, :, None] == targets[None, None, :]
    share = jnp.sum(jnp.where(route_hits, route_weight[:, :, None], 0.0), axis=1)
    hit_any = jnp.any(route_hits, axis=1)
    hit_count = hit_any.astype(jnp.int32)
    slot_rank = jnp.cumsum(hit_count, axis=0) - hit_count
    placed = jnp.where(hit_any, slot_rank, capacity_expert)
    spread_rows = jnp.broadcast_to(mixture_in[:, None, :], (requests, owners, model_width))
    dispatch = (
        jnp.zeros((owners, capacity_expert, model_width), jnp.bfloat16)
        .at[owner_range[None, :], placed]
        .set(spread_rows, mode="drop")
    )
    arrived = lax.all_to_all(dispatch, "owner", split_axis=0, concat_axis=0, tiled=True)
    slot_count = arrived.shape[1]
    slot_rows = arrived.reshape(owners * slot_count, model_width)
    gate_part = lax.dot_general(
        slot_rows, gate_rows, (((1,), (1,)), ((), ())), preferred_element_type=jnp.float32
    )
    up_part = lax.dot_general(
        slot_rows, up_rows, (((1,), (1,)), ((), ())), preferred_element_type=jnp.float32
    )
    activation = (jax.nn.silu(gate_part) * up_part).astype(jnp.bfloat16)
    results = (
        jnp.dot(activation, down_rows, preferred_element_type=jnp.float32)
        .astype(jnp.bfloat16)
        .reshape(owners, slot_count, model_width)
    )
    returned = lax.all_to_all(results, "owner", split_axis=0, concat_axis=0, tiled=True)
    fetched = returned[owner_range[None, :], jnp.minimum(slot_rank, capacity_expert - 1)]
    routed = jnp.einsum("rod,ro->rd", fetched, share, preferred_element_type=jnp.float32)
    gate_part = lax.dot_general(
        mixture_in, shared_gate, (((1,), (1,)), ((), ())), preferred_element_type=jnp.float32
    )
    up_part = lax.dot_general(
        mixture_in, shared_up, (((1,), (1,)), ((), ())), preferred_element_type=jnp.float32
    )
    activation = (jax.nn.silu(gate_part) * up_part).astype(jnp.bfloat16)
    combined = lax.psum_scatter(
        routed + jnp.dot(activation, shared_down, preferred_element_type=jnp.float32),
        "tensor",
        scatter_dimension=1,
        tiled=True,
    )
    result = mid.astype(jnp.float32) + combined
    return result.astype(jnp.bfloat16)


def solution(mesh):
    return jax.shard_map(
        local,
        mesh=mesh,
        in_specs=(
            P("owner", "tensor"),
            P(),
            P("tensor", None),
            P("tensor", None),
            P("tensor", None),
            P("owner", "tensor", None),
            P("owner"),
            P("owner", "tensor", None),
            P("owner"),
            P("owner"),
            P(),
            P("owner", None),
            P("owner", None),
            P(("owner", "tensor"), None, None),
            P(("owner", "tensor"), None, None),
            P(("owner", "tensor"), None, None),
            P("tensor", None),
            P("tensor", None),
            P("tensor", None),
        ),
        out_specs=P("owner", "tensor"),
        check_vma=False,
    )
```

profile of v0, /device:TPU:0, one launch (start us, length us, event | category | flops | bytes accessed | tf_op | source)
XLA Modules:
  0.0 453.7 jit_solution(14077124363362763981)
XLA Ops:
  9.0 4.2 all-to-all-start
  13.2 31.6 %all_gather.19 = bf16[32,2048]{1,0:T(8,128)(2,1)S(1)} all-gather(bf16[32,256]{1,0:T(8,128)(2,1)} %param.21), channel_id=1, replica_groups=mesh['owner'=4,'tensor'=8] {'tensor'}, dimensions={1}, use_global_device_ids=true | all-gather | bytes 147456 | tf_op jit(solution)/shard_map/all_gather | solution.py:105
  45.7 3.9 convolution_convert_fusion
  49.5 31.4 %all_gather.20 = bf16[32,9216]{1,0:T(8,128)(2,1)S(1)} all-gather(bf16[32,1152]{1,0:T(8,128)(2,1)S(1)} %convolution_convert_fusion), channel_id=1, replica_groups=mesh['owner'=4,'tensor'=8] {'tensor'}, dimensions={1}, use_global_device_ids=true | all-gather | bytes 663552 | tf_op jit(solution)/shard_map/all_gather | solution.py:110
  81.5 2.6 scatter_custom_fusion.1
  84.1 8.3 %multiply_reduce_fusion = (f32[32,16]{1,0:T(8,128)S(1)}, f32[32,16,4096]{2,1,0:T(8,128)}) fusion(bf16[32,16,576]{2,1,0:T(8,128)(2,1)S(1)} %reshape.350, bf16[4096,576]{0,1:T(8,128)(2,1)} %param.25), kind=kOutput, calls=%fused_computation.20 | convolution fusion | flops 2420112896 | bytes 13699072 | tf_op jit(solution)/shard_map/rhc,pc->rhp/dot_general | solution.py:113
  93.9 4.9 %fusion.6 = f32[32,16]{1,0:T(8,128)S(1)} fusion(f32[32,16,4096]{2,1,0:T(8,128)} %get-tuple-element.193, f32[32,16]{1,0:T(8,128)S(1)} %get-tuple-element.192), kind=kLoop, calls=%fused_computation.22 | loop fusion | flops 6290944 | bytes 8392704 | tf_op jit(solution)/shard_map/reduce_sum | solution.py:124
  98.9 3.6 all-to-all-start.1
  102.7 5.9 %gather_fusion.1 = bf16[64,128,576]{1,2,0:T(8,128)(2,1)} fusion(bf16[12,128,576]{1,2,0:T(8,128)(2,1)S(1)} %copy-done, s32[1024]{0:T(1024)S(1)} %pad_clamp_fusion.1), kind=kCustom, calls=%fused_computation.1 | custom fusion | bytes 18874624 | tf_op jit(solution)/shard_map/gather | solution.py:166
  109.4 14.1 %copy.115 = bf16[64,128,576]{2,1,0:T(8,128)(2,1)} copy(bf16[64,128,576]{1,2,0:T(8,128)(2,1)} %gather_fusion.1) | data formatting | bytes 18874368 | tf_op jit(solution)/shard_map/gather | solution.py:166
  124.7 4.7 %fusion.123 = (f32[4,16,16]{2,1,0:T(8,128)S(1)}, f32[4,16,16,128]{3,2,1,0:T(8,128)S(1)}) fusion(bf16[4,16,16,576]{3,2,1,0:T(8,128)(2,1)S(1)} %reshape.352, bf16[4,16,128,576]{2,3,1,0:T(8,128)(2,1)} %bitcast.151, pred[4,16,128]{2,1,0:T(8,128)(4,1)S(1)} %compare_and_fusion), kind=kOutput, calls=%fused_computation.173 | convolution fusion | flops 151387136 | bytes 11153408 | tf_op jit(solution)/shard_map/...hc,...pc->...hp/dot_general | solution.py:65
  130.5 3.4 all-to-all-start.2
  133.9 5.6 %divide_convert_fusion = bf16[4,16,16,512]{3,2,1,0:T(8,128)(2,1)} fusion(f32[4,16,16]{2,1,0:T(8,128)S(1)} %get-tuple-element.184, bf16[4,16,128,576]{3,2,1,0:T(8,128)(2,1)} %bitcast.152, f32[4,16,16,128]{3,2,1,0:T(8,128)S(1)} %get-tuple-element.191, f32[4,16,16]{2,1,0:T(8,128)S(1)} %get-tuple-element.190, pred[4,16,128]{2,1,0:T(8,128)(4,1)S(1)} %compare_and_fusion), kind=kOutput, calls=%fused_computation.41 | convolution fusion | flops 135659520 | bytes 9977856 | tf_op jit(solution)/shard_map/...hp,...pl->...hl/dot_general | solution.py:71
  139.5 3.5 all-to-all-start.3
  143.1 7.0 %fusion.15 = f32[32,16,512]{2,1,0:T(8,128)S(1)} fusion(f32[32,16,4096]{2,1,0:T(8,128)} %get-tuple-element.193, bf16[4096,576]{0,1:T(8,128)(2,1)} %param.25, f32[32,16]{1,0:T(8,128)S(1)} %get-tuple-element.192), kind=kOutput, calls=%fused_computation.31 | convolution fusion | flops 2153775104 | bytes 13633536 | tf_op jit(solution)/shard_map/rhp,pl->rhl/dot_general | solution.py:118
  152.6 5.0 %all-to-all-done.3 = bf16[4,16,16,512]{3,2,1,0:T(8,128)(2,1)S(1)} async-done(((bf16[4,16,16,512]{3,2,1,0:T(8,128)(2,1)}), bf16[4,16,16,512]{3,2,1,0:T(8,128)(2,1)S(1)}, u32[]{:S(2)}, u32[]{:S(2)}) %all-to-all-start.3) | async-done | bytes 1048608 | tf_op jit(solution)/shard_map/all_to_all | solution.py:172
  158.2 3.4 add_divide_fusion
  162.3 31.0 %all_gather.23 = f32[8,32,16]{1,2,0:T(8,128)S(1)} all-gather(f32[1,32,16]{1,2,0:T(8,128)S(1)} %fusion.95), channel_id=1, replica_groups=mesh['owner'=4,'tensor'=8] {'tensor'}, dimensions={0}, use_global_device_ids=true | all-gather | bytes 18432 | tf_op jit(solution)/shard_map/all_gather | solution.py:19
  193.4 93.9 %all-gather.3.cloned.1.call-done = f32[256,16,512]{2,1,0:T(8,128)} async-done(((f32[32,16,512]{2,1,0:T(8,128)}), f32[256,16,512]{2,1,0:T(8,128)}) %all-gather.3.cloned.1.call-update) | async-done | bytes 8388624 | tf_op jit(solution)/shard_map/all_gather | solution.py:19
  288.6 11.9 %while.17 = (s32[]{:T(128)}, f32[32,16,512]{2,1,0:T(8,128)S(1)}, f32[32,16]{1,0:T(8,128)S(1)}, f32[8,32,16]{1,2,0:T(8,128)S(1)}, f32[8,32,16,512]{3,2,1,0:T(8,128)}, /*index=5*/s32[]{:T(128)}, s32[]{:T(128)}, s32[]{:T(128)}) while((s32[]{:T(128)}, f32[32,16,512]{2,1,0:T(8,128)S(1)}, f32[32,16]{1,0:T(8,128)S(1)}, ...), condition=%wide.region_12.13_spmd, body=%wide.region_11.12_spmd.sunk | while | flops 1051141 | bytes 3172487 | solution.py:25
  300.9 3.6 fusion.44
  304.5 30.5 %all_gather.24 = bf16[32,2048]{1,0:T(8,128)(2,1)S(1)} all-gather(bf16[32,256]{1,0:T(8,128)(2,1)S(1)} %fusion.44), channel_id=1, replica_groups=mesh['owner'=4,'tensor'=8] {'tensor'}, dimensions={1}, use_global_device_ids=true | all-gather | bytes 147456 | tf_op jit(solution)/shard_map/all_gather | solution.py:187
  335.7 11.7 %scatter_fusion = bf16[4,12,2048]{2,0,1:T(4,128)(2,1)S(1)} fusion(bf16[4,12,2048]{2,0,1:T(4,128)(2,1)S(1)} %broadcast_in_dim.161, s32[128]{0:T(128)S(1)} %reshape.412, bf16[128,2048]{1,0:T(8,128)(2,1)S(1)} %reshape.414), kind=kCustom, calls=%fused_computation.7 | custom fusion | bytes 1573888 | tf_op jit(solution)/shard_map/scatter | solution.py:209
  348.2 3.6 all-to-all-start.4
  352.2 5.4 %all-to-all-done.4 = bf16[4,12,2048]{2,1,0:T(8,128)(2,1)S(1)} async-done(((bf16[4,12,2048]{2,1,0:T(8,128)(2,1)}), bf16[4,12,2048]{2,1,0:T(8,128)(2,1)S(1)}, u32[]{:S(2)}, u32[]{:S(2)}) %all-to-all-start.4) | async-done | bytes 196640 | tf_op jit(solution)/shard_map/all_to_all | solution.py:211
  357.7 4.5 fusion.11
  362.2 7.4 %fusion.27 = bf16[48,2048]{1,0:T(8,128)(2,1)S(1)} fusion(bf16[1,1408,2048]{2,1,0:T(8,128)(2,1)} %param.36, bf16[48,2048]{1,0:T(8,128)(2,1)S(1)} %reshape.356, bf16[1,1408,2048]{2,1,0:T(8,128)(2,1)} %param.35, f32[48,1408]{1,0:T(8,128)S(1)} %fusion.11), kind=kOutput, calls=%fused_computation.38 | convolution fusion | flops 554151936 | bytes 12197888 | tf_op jit(solution)/shard_map/dot_general | solution.py:222
  370.3 3.4 all-to-all-start.5
  374.3 5.4 %all-to-all-done.5 = bf16[4,12,2048]{2,1,0:T(8,128)(2,1)S(1)} async-done(((bf16[4,12,2048]{2,1,0:T(8,128)(2,1)}), bf16[4,12,2048]{2,1,0:T(8,128)(2,1)S(1)}, u32[]{:S(2)}, u32[]{:S(2)}) %all-to-all-start.5) | async-done | bytes 196640 | tf_op jit(solution)/shard_map/all_to_all | solution.py:226
  379.9 2.4 gather_fusion.4
  382.9 3.6 convolution_add_fusion
  386.6 58.9 %reduce-scatter.2.cloned.1.call-done = f32[32,256]{1,0:T(8,128)} async-done(((f32[32,2048]{1,0:T(8,128)}), f32[32,256]{1,0:T(8,128)}) %reduce-scatter.2.cloned.1.call-update) | async-done | bytes 32784 | tf_op jit(solution)/shard_map/reduce_scatter | solution.py:236
  (136 shorter events, 31.2 us)
Async XLA Ops:
  6.5 96.1 %copy-start = (bf16[12,128,576]{1,2,0:T(8,128)(2,1)S(1)}, bf16[12,128,576]{1,2,0:T(8,128)(2,1)}, u32[]{:S(2)}) copy-start(bf16[12,128,576]{1,2,0:T(8,128)(2,1)} %param.26) | copy-start | bytes 5308420
  9.0 89.9 %all-to-all-start = ((s32[4,1,16]{2,1,0:T(1,128)}), s32[4,1,16]{2,1,0:T(1,128)S(1)}, u32[]{:S(2)}, u32[]{:S(2)}) async-start(s32[4,1,16]{2,1,0:T(1,128)} %bitcast.3), calls=%async_computation | async-start | bytes 4096 | tf_op jit(solution)/shard_map/all_to_all | solution.py:160
  84.1 8.3 %copy-start.9 = (s32[32]{0:T(128)S(1)}, s32[32]{0:T(128)}, u32[]{:S(2)}) copy-start(s32[32]{0:T(128)} %param.29) | copy-start | bytes 388
  84.1 8.4 %copy-start.3 = (bf16[32,64,576]{2,1,0:T(8,128)(2,1)S(1)}, bf16[32,64,576]{2,1,0:T(8,128)(2,1)}, u32[]{:S(2)}) copy-start(bf16[32,64,576]{2,1,0:T(8,128)(2,1)} %param.28) | copy-start | bytes 7077892
  98.9 24.6 %all-to-all-start.1 = ((bf16[4,16,9216]{2,1,0:T(8,128)(2,1)}), bf16[4,16,9216]{2,1,0:T(8,128)(2,1)S(1)}, u32[]{:S(2)}, u32[]{:S(2)}) async-start(bf16[4,16,9216]{2,1,0:T(8,128)(2,1)} %bitcast.5), calls=%async_computation.1 | async-start | bytes 2359296 | tf_op jit(solution)/shard_map/all_to_all | solution.py:153
  102.6 5.9 %copy-start.2 = (s32[12]{0:T(128)S(1)}, s32[12]{0:T(128)}, u32[]{:S(2)}) copy-start(s32[12]{0:T(128)} %param.27) | copy-start | bytes 148
  130.5 9.1 %all-to-all-start.2 = ((f32[4,1,256]{2,1,0:T(1,128)}), f32[4,1,256]{2,1,0:T(1,128)S(1)}, u32[]{:S(2)}, u32[]{:S(2)}) async-start(f32[4,1,256]{2,1,0:T(1,128)} %reshape.435), calls=%async_computation.2 | async-start | bytes 8192 | tf_op jit(solution)/shard_map/all_to_all | solution.py:173
  139.5 18.1 %all-to-all-start.3 = ((bf16[4,16,16,512]{3,2,1,0:T(8,128)(2,1)}), bf16[4,16,16,512]{3,2,1,0:T(8,128)(2,1)S(1)}, u32[]{:S(2)}, u32[]{:S(2)}) async-start(bf16[4,16,16,512]{3,2,1,0:T(8,128)(2,1)} %divide_convert_fusion), calls=%async_computation.3 | async-start | bytes 2097152 | tf_op jit(solution)/shard_map/all_to_all | solution.py:172
  143.1 144.2 %all-gather.3.cloned.1.call-start = ((), (), s32[]{:S(2)}) async-start(), calls=%async_computation.8 | async-start | bytes 9437184 | tf_op jit(solution)/shard_map/all_gather | solution.py:19
  158.2 3.5 copy-start.7
  158.2 3.5 copy-start.6
  288.6 12.3 %copy-start.5 = (bf16[32,256]{1,0:T(8,128)(2,1)S(1)}, bf16[32,256]{1,0:T(8,128)(2,1)}, u32[]{:S(2)}) copy-start(bf16[32,256]{1,0:T(8,128)(2,1)} %param.21) | copy-start | bytes 49156
  335.7 16.3 %copy-start.8 = (f32[32,6]{0,1:T(8,128)S(1)}, f32[32,6]{0,1:T(8,128)}, u32[]{:S(2)}) copy-start(f32[32,6]{0,1:T(8,128)} %param.33) | copy-start | bytes 2308
  348.2 9.4 %all-to-all-start.4 = ((bf16[4,12,2048]{2,1,0:T(8,128)(2,1)}), bf16[4,12,2048]{2,1,0:T(8,128)(2,1)S(1)}, u32[]{:S(2)}, u32[]{:S(2)}) async-start(bf16[4,12,2048]{2,1,0:T(8,128)(2,1)} %copy.135), calls=%async_computation.4 | async-start | bytes 524288 | tf_op jit(solution)/shard_map/all_to_all | solution.py:211
  362.1 11.6 %copy-start.4 = (bf16[352,2048]{1,0:T(8,128)(2,1)S(1)}, bf16[352,2048]{1,0:T(8,128)(2,1)}, u32[]{:S(2)}) copy-start(bf16[352,2048]{1,0:T(8,128)(2,1)} %param.37) | copy-start | bytes 4325380
  370.3 9.4 %all-to-all-start.5 = ((bf16[4,12,2048]{2,1,0:T(8,128)(2,1)}), bf16[4,12,2048]{2,1,0:T(8,128)(2,1)S(1)}, u32[]{:S(2)}, u32[]{:S(2)}) async-start(bf16[4,12,2048]{2,1,0:T(8,128)(2,1)} %reshape.357), calls=%async_computation.5 | async-start | bytes 524288 | tf_op jit(solution)/shard_map/all_to_all | solution.py:226
  373.7 71.8 %reduce-scatter.2.cloned.1.call-start = ((), (), s32[]{:S(2)}) async-start(), calls=%async_computation.7 | async-start | bytes 294912 | tf_op jit(solution)/shard_map/reduce_scatter | solution.py:236
  379.7 67.1 %copy-start.1 = (bf16[12,128,576]{1,2,0:T(8,128)(2,1)S(1)}, bf16[12,128,576]{1,2,0:T(8,128)(2,1)}, u32[]{:S(2)}) copy-start(bf16[12,128,576]{1,2,0:T(8,128)(2,1)} %param.26) | copy-start | bytes 5308420
Sparse Core Ops, SparseCore 0:
  161.8 125.4 all-gather.2
  386.7 58.7 reduce-scatter.1
where the time goes:
time: 455 us; the launch traced here: 454 us
  waiting for transfers between devices  169 us (37%)
  blocking collectives  125 us (27%)
  matrix products  53.9 us (12%)
  local copies, waits for them, and re-layouts  49.2 us (11%)
  starting transfers between devices  21.9 us (5%)
  other arithmetic  21.5 us (5%)
  between operations  13.8 us (3%)
    all_gather x1, waiting for transfers between devices, combined_all(): everything = jax.tree.map(lambda part: lax.all_gather(part, axis), x)  93.9 us
    reduce_scatter x1, waiting for transfers between devices, local(): lax.psum_scatter(routed + jnp.dot(activation, shared_down, preferred_elem...  58.9 us
    all_gather x1, blocking collectives, local(): rows_full = lax.all_gather(hidden, 'tensor', axis=1, tiled=True)  31.6 us
    all_gather x1, blocking collectives, local(): projected = lax.all_gather(projected, 'tensor', axis=1, tiled=True)  31.4 us
    all_gather x1, blocking collectives, combined_all(): everything = jax.tree.map(lambda part: lax.all_gather(part, axis), x)  31 us
    all_gather x1, blocking collectives, local(): mid_full = lax.all_gather(mid, 'tensor', axis=1, tiled=True)  30.5 us
    gather x2, local copies, waits for them, and re-layouts, local(): cache_block = group_cache[chosen]  19.9 us
    scatter x2, local copies, waits for them, and re-layouts, local(): dispatch = jnp.zeros((owners, capacity_expert, model_width), jnp.bfloat16...  12.5 us
  transfers between devices with their start and end apart: 8, of which 5 were waited for; matrix products, arithmetic and copies ran while one was open for 13% of the time, Pallas kernels for 0%

commit v1 on v0

v1 whole, which is shorter than its diff:
```python
import functools

import jax
import jax.numpy as jnp
from jax import lax
from jax.experimental import pallas as pl
from jax.experimental.pallas import tpu as pltpu
from jax.sharding import PartitionSpec as P

H = 16
LAT = 512
KVW = 576
EXP_OWN = 8
GROUP_OWN = 12
PIECES = 8
PAIR = 2 * KVW
LANES = 128
MIB = 1 << 20

score_scale = 192.0 ** (-0.5)
log2e = 1.4426950408889634
ln2 = 0.6931471805599453
lowest = -1e30
epsilon = 1e-06

NT = (((1,), (1,)), ((), ()))


def dot_nt(a, b):
    return lax.dot_general(a, b, NT, preferred_element_type=jnp.float32)


def dot_nn(a, b):
    return jnp.dot(a, b, preferred_element_type=jnp.float32)


def call(body, out_shape, vmem_mib, flops, nbytes, **options):
    return pl.pallas_call(
        body,
        out_shape=out_shape,
        compiler_params=pltpu.CompilerParams(vmem_limit_bytes=vmem_mib * MIB),
        cost_estimate=pl.CostEstimate(
            flops=int(flops), bytes_accessed=int(nbytes), transcendentals=0
        ),
        **options,
    )


def whole(shape):
    return pl.BlockSpec(shape, lambda *_: (0,) * len(shape))


def split_three(column):
    first = column.astype(jnp.bfloat16).astype(jnp.float32)
    second = (column - first).astype(jnp.bfloat16).astype(jnp.float32)
    third = (column - first - second).astype(jnp.bfloat16).astype(jnp.float32)
    return first, second, third


def normalised(read_piece, gain, width):
    rows = jnp.concatenate([read_piece(k) for k in range(PIECES)], axis=-1).astype(jnp.float32)
    square = jnp.sum(rows * rows, axis=-1, keepdims=True) * (1.0 / width)
    return (rows * lax.rsqrt(square + epsilon) * gain).astype(jnp.bfloat16)


def project_body(rows_ref, gain_ref, weight_ref, out_ref, normed_ref):
    @pl.when(pl.program_id(0) == 0)
    def _():
        normed_ref[...] = normalised(
            lambda k: rows_ref[k], gain_ref[...], normed_ref.shape[1]
        )

    out_ref[...] = dot_nt(normed_ref[...], weight_ref[...]).astype(jnp.bfloat16)


def project(rows, gain, weight):
    pieces, requests, part = rows.shape
    columns, width = weight.shape
    steps = 3 if columns % (3 * LANES) == 0 else 1
    return call(
        project_body,
        jax.ShapeDtypeStruct((requests, columns), jnp.bfloat16),
        24,
        2 * requests * columns * width,
        2 * columns * width,
        grid=(steps,),
        in_specs=[
            whole(rows.shape),
            whole(gain.shape),
            pl.BlockSpec((columns // steps, width), lambda i: (i, 0)),
        ],
        out_specs=pl.BlockSpec((requests, columns // steps), lambda i: (0, i)),
        scratch_shapes=[pltpu.VMEM((requests, width), jnp.bfloat16)],
    )(rows, gain, weight)


def pick_body(pick_ref, extra_ref, rows_ref, out_ref):
    owners, slots, _ = out_ref.shape
    for k in range(PIECES):
        picked = dot_nn(pick_ref[...], rows_ref[k]).astype(jnp.bfloat16)
        for o in range(owners):
            out_ref[o, :, k * PAIR : (k + 1) * PAIR] = picked[o * slots : (o + 1) * slots]
    for o in range(owners):
        out_ref[o, :, PIECES * PAIR :] = extra_ref[o]


def pick_queries(pick, extra, rows, owners, slots):
    return call(
        pick_body,
        jax.ShapeDtypeStruct((owners, slots, H * KVW + LANES), jnp.bfloat16),
        16,
        2 * owners * slots * rows.shape[1] * H * KVW,
        4 * owners * slots * H * KVW,
    )(pick, extra, rows)


def root_body(root_steps, rows_ref, root_ref, suffix_ref, holder_ref, out_ref, mass_ref, q_ref, m_ref, l_ref, acc_ref):
    step = pl.program_id(0)
    requests = rows_ref.shape[1]

    @pl.when(step == 0)
    def _():
        for k in range(PIECES):
            for j in range(2):
                at = (2 * k + j) * requests
                q_ref[at : at + requests, :] = rows_ref[k, :, j * KVW : (j + 1) * KVW]
        m_ref[...] = jnp.full(m_ref.shape, lowest, jnp.float32)
        l_ref[...] = jnp.zeros(l_ref.shape, jnp.float32)
        acc_ref[...] = jnp.zeros(acc_ref.shape, jnp.float32)

    def take(scores, block_ref):
        peak = jnp.maximum(m_ref[...], jnp.max(scores, axis=-1, keepdims=True))
        weights = jnp.exp2(scores - peak)
        shrink = jnp.exp2(m_ref[...] - peak)
        l_ref[...] = l_ref[...] * shrink + jnp.sum(weights, axis=-1, keepdims=True)
        acc_ref[...] = acc_ref[...] * shrink + dot_nn(
            weights.astype(jnp.bfloat16), block_ref[:, :LAT]
        )
        m_ref[...] = peak

    @pl.when(step < root_steps)
    def _():
        take(dot_nt(q_ref[...], root_ref[...]) * (score_scale * log2e), root_ref)

    @pl.when(step >= root_steps)
    def _():
        scores = dot_nt(q_ref[...], suffix_ref[...]) * (score_scale * log2e)
        request = lax.broadcasted_iota(jnp.int32, (q_ref.shape[0], 1), 0) % requests
        take(jnp.where(holder_ref[...] == request, scores, lowest), suffix_ref)

    @pl.when(step == pl.num_programs(0) - 1)
    def _():
        total = l_ref[...]
        out_ref[...] = acc_ref[...] / total
        mass_ref[...] = jnp.broadcast_to(m_ref[...] * ln2 + jnp.log(total), mass_ref.shape)


def root_attention(rows, root, suffix, holder):
    requests = rows.shape[1]
    count = H * requests
    block = 512
    root_steps, suffix_steps = root.shape[0] // block, suffix.shape[0] // block
    return call(
        functools.partial(root_body, root_steps),
        (
            jax.ShapeDtypeStruct((count, LAT), jnp.float32),
            jax.ShapeDtypeStruct((count, LANES), jnp.float32),
        ),
        32,
        2 * count * (root.shape[0] + suffix.shape[0]) * (KVW + LAT),
        2 * KVW * (root.shape[0] + suffix.shape[0]),
        grid=(root_steps + suffix_steps,),
        in_specs=[
            whole(rows.shape),
            pl.BlockSpec((block, KVW), lambda i: (jnp.minimum(i, root_steps - 1), 0)),
            pl.BlockSpec((block, KVW), lambda i: (jnp.maximum(i - root_steps, 0), 0)),
            pl.BlockSpec((1, block), lambda i: (0, jnp.maximum(i - root_steps, 0))),
        ],
        out_specs=(whole((count, LAT)), whole((count, LANES))),
        scratch_shapes=[
            pltpu.VMEM((count, KVW), jnp.bfloat16),
            pltpu.VMEM((count, 1), jnp.float32),
            pltpu.VMEM((count, 1), jnp.float32),
            pltpu.VMEM((count, LAT), jnp.float32),
        ],
    )(rows, root, suffix, holder)


def group_body(rows_ref, cache_ref, holder_ref, out_ref, q_ref):
    slots = rows_ref.shape[1]
    for h in range(H):
        q_ref[h * slots : (h + 1) * slots, :] = rows_ref[0, :, h * KVW : (h + 1) * KVW]
    asked = rows_ref[0, :, H * KVW :][:, :1].astype(jnp.float32)
    asked = jnp.concatenate([asked] * H, axis=0)
    usable = holder_ref[...] == asked
    scores = dot_nt(q_ref[...], cache_ref[...]) * (score_scale * log2e)
    scores = jnp.where(usable, scores, lowest)
    peak = jnp.max(scores, axis=-1, keepdims=True)
    weights = jnp.where(usable, jnp.exp2(scores - peak), 0.0)
    total = jnp.sum(weights, axis=-1, keepdims=True)
    present = total > 0.0
    safe = jnp.where(present, total, 1.0)
    block_out = dot_nn(weights.astype(jnp.bfloat16), cache_ref[:, :LAT]) / safe
    mass = jnp.where(present, peak * ln2 + jnp.log(safe), lowest)
    lane = lax.broadcasted_iota(jnp.int32, (slots, LANES), 1)
    extra = jnp.zeros((slots, LANES), jnp.float32)
    for h in range(H):
        at = slice(h * slots, (h + 1) * slots)
        out_ref[0, :, h * LAT : (h + 1) * LAT] = block_out[at].astype(jnp.bfloat16)
        for k, part in enumerate(split_three(mass[at])):
            extra = jnp.where(lane == k * H + h, part, extra)
    out_ref[0, :, H * LAT :] = extra.astype(jnp.bfloat16)


def group_attention(rows, cache, holder):
    owners, slots, width = rows.shape
    positions = cache.shape[0]
    return call(
        group_body,
        jax.ShapeDtypeStruct((owners, slots, H * LAT + LANES), jnp.bfloat16),
        32,
        2 * owners * slots * H * positions * (KVW + LAT),
        2 * KVW * positions,
        grid=(owners,),
        in_specs=[
            pl.BlockSpec((1, slots, width), lambda i: (i, 0, 0)),
            whole(cache.shape),
            whole(holder.shape),
        ],
        out_specs=pl.BlockSpec((1, slots, H * LAT + LANES), lambda i: (i, 0, 0)),
        scratch_shapes=[pltpu.VMEM((H * slots, KVW), jnp.bfloat16)],
    )(rows, cache, holder)


def local_body(unpick_ref, back_ref, first_ref, mass_ref, out_ref):
    requests = unpick_ref.shape[0]
    unpick = unpick_ref[...]
    extra = dot_nn(unpick, back_ref[:, H * LAT :])
    lane = lax.broadcasted_iota(jnp.int32, (requests, LANES), 1)
    for h in range(H):
        at = slice(h * requests, (h + 1) * requests)
        group_out = dot_nn(unpick, back_ref[:, h * LAT : (h + 1) * LAT])
        group_mass = (
            extra[:, h : h + 1] + extra[:, H + h : H + h + 1] + extra[:, 2 * H + h : 2 * H + h + 1]
        )
        first_mass = mass_ref[at, :1]
        peak = jnp.maximum(first_mass, group_mass)
        first_weight = jnp.exp(first_mass - peak)
        group_weight = jnp.exp(group_mass - peak)
        total = first_weight + group_weight
        out = (first_weight * first_ref[at, :] + group_weight * group_out) / total
        out_ref[at, :LAT] = out.astype(jnp.bfloat16)
        tail = jnp.zeros((requests, LANES), jnp.float32)
        for k, part in enumerate(split_three(peak + jnp.log(total))):
            tail = jnp.where(lane == k, part, tail)
        out_ref[at, LAT:] = tail.astype(jnp.bfloat16)


def local_join(unpick, back, first, mass):
    count = first.shape[0]
    return call(
        local_body,
        jax.ShapeDtypeStruct((count, LAT + LANES), jnp.bfloat16),
        24,
        2 * unpick.shape[0] * back.shape[0] * back.shape[1],
        4 * count * LAT,
    )(unpick, back, first, mass)


def join_body(parts_ref, out_ref):
    sources, copies = parts_ref.shape[0], out_ref.shape[0]
    tails = [parts_ref[s, :, LAT:].astype(jnp.float32) for s in range(sources)]
    masses = [t[:, 0:1] + t[:, 1:2] + t[:, 2:3] for t in tails]
    peak = functools.reduce(jnp.maximum, masses)
    scales = [jnp.exp(mass - peak) for mass in masses]
    total = functools.reduce(jnp.add, scales)
    out = functools.reduce(
        jnp.add,
        [scales[s] * parts_ref[s, :, :LAT].astype(jnp.float32) for s in range(sources)],
    )
    out = (out / total).astype(jnp.bfloat16)
    for c in range(copies):
        out_ref[c] = out


def join(parts):
    sources, rows, _ = parts.shape
    return call(
        join_body,
        jax.ShapeDtypeStruct((sources, rows, LAT), jnp.bfloat16),
        16,
        2 * sources * rows * LAT,
        4 * sources * rows * LAT,
    )(parts)


def output_body(rows_ref, weight_ref, hidden_ref, out_ref, acc_ref):
    step = pl.program_id(0)
    requests = hidden_ref.shape[0]
    heads = weight_ref.shape[1] // LAT

    @pl.when(step == 0)
    def _():
        acc_ref[...] = hidden_ref[...].astype(jnp.float32)

    acc = acc_ref[...]
    for h in range(heads):
        acc = acc + dot_nt(
            rows_ref[h * requests : (h + 1) * requests, :],
            weight_ref[:, h * LAT : (h + 1) * LAT],
        )
    acc_ref[...] = acc

    @pl.when(step == pl.num_programs(0) - 1)
    def _():
        out_ref[...] = acc.astype(jnp.bfloat16)


def output_projection(rows, weight, hidden):
    features, width = weight.shape
    requests = hidden.shape[0]
    steps = 4
    heads = H // steps
    return call(
        output_body,
        jax.ShapeDtypeStruct(hidden.shape, jnp.bfloat16),
        24,
        2 * requests * features * width,
        2 * features * width,
        grid=(steps,),
        in_specs=[
            pl.BlockSpec((heads * requests, LAT), lambda i: (i, 0)),
            pl.BlockSpec((features, heads * LAT), lambda i: (0, i)),
            whole(hidden.shape),
        ],
        out_specs=whole(hidden.shape),
        scratch_shapes=[pltpu.VMEM(hidden.shape, jnp.float32)],
    )(rows, weight, hidden)


def gated(rows, gate, up):
    gate_part = dot_nt(rows, gate)
    up_part = dot_nt(rows, up)
    return (gate_part / (1.0 + jnp.exp(-gate_part)) * up_part).astype(jnp.bfloat16)


def expert_body(pick_ref, rows_ref, gain_ref, gate_ref, up_ref, down_ref, out_ref, slot_ref, acc_ref):
    step = pl.program_id(0)
    owners, _, requests, part = rows_ref.shape
    width = gain_ref.shape[1]

    @pl.when(step == 0)
    def _():
        rows = jnp.concatenate(
            [
                normalised(lambda k, o=o: rows_ref[o, k], gain_ref[...], width)
                for o in range(owners)
            ],
            axis=0,
        )
        slot_ref[...] = dot_nn(pick_ref[...], rows).astype(jnp.bfloat16)
        acc_ref[...] = jnp.zeros(acc_ref.shape, jnp.float32)

    acc_ref[...] += dot_nn(gated(slot_ref[...], gate_ref[0], up_ref[0]), down_ref[0])

    @pl.when(step == pl.num_programs(0) - 1)
    def _():
        slots = out_ref.shape[2]
        for o in range(owners):
            for k in range(PIECES):
                out_ref[o, k] = acc_ref[
                    o * slots : (o + 1) * slots, k * part : (k + 1) * part
                ].astype(jnp.bfloat16)


def expert(pick, rows, gain, gate, up, down, slots):
    owners, _, requests, part = rows.shape
    _, units, width = gate.shape
    steps = 4 if units % 64 == 0 and units > 704 else 1
    weights = pl.BlockSpec((1, units // steps, width), lambda i: (0, i, 0))
    return call(
        expert_body,
        jax.ShapeDtypeStruct((owners, PIECES, slots, part), jnp.bfloat16),
        40,
        6 * pick.shape[0] * units * width,
        6 * units * width,
        grid=(steps,),
        in_specs=[whole(pick.shape), whole(rows.shape), whole(gain.shape), weights, weights, weights],
        out_specs=whole((owners, PIECES, slots, part)),
        scratch_shapes=[
            pltpu.VMEM((owners * slots, width), jnp.bfloat16),
            pltpu.VMEM((owners * slots, width), jnp.float32),
        ],
    )(pick, rows, gain, gate, up, down)


def shared_body(rows_ref, gain_ref, gate_ref, up_ref, down_ref, out_ref):
    part = rows_ref.shape[2]
    rows = normalised(lambda k: rows_ref[k], gain_ref[...], gain_ref.shape[1])
    out = dot_nn(gated(rows, gate_ref[...], up_ref[...]), down_ref[...])
    for k in range(PIECES):
        out_ref[k] = out[:, k * part : (k + 1) * part].astype(jnp.bfloat16)


def shared_expert(rows, gain, gate, up, down):
    return call(
        shared_body,
        jax.ShapeDtypeStruct(rows.shape, jnp.bfloat16),
        32,
        6 * rows.shape[1] * gate.shape[0] * gate.shape[1],
        6 * gate.shape[0] * gate.shape[1],
    )(rows, gain, gate, up, down)


def final_body(parts_ref, weight_ref, shared_ref, mid_ref, out_ref):
    weight = weight_ref[...]
    high = weight.astype(jnp.bfloat16)
    rest = weight - high.astype(jnp.float32)
    low = rest.astype(jnp.bfloat16)
    lower = (rest - low.astype(jnp.float32)).astype(jnp.bfloat16)
    parts = parts_ref[...]
    total = dot_nn(high, parts) + (dot_nn(low, parts) + dot_nn(lower, parts))
    for k in range(shared_ref.shape[0]):
        total = total + shared_ref[k].astype(jnp.float32)
    out_ref[...] = (mid_ref[...].astype(jnp.float32) + total).astype(jnp.bfloat16)


def final_sum(parts, weight, shared, mid):
    return call(
        final_body,
        jax.ShapeDtypeStruct(mid.shape, jnp.bfloat16),
        24,
        2 * weight.shape[0] * parts.shape[0] * parts.shape[1],
        2 * parts.shape[0] * parts.shape[1],
    )(parts, weight, shared, mid)


def spread(x, axis, count):
    return lax.all_to_all(jnp.broadcast_to(x[None], (count,) + x.shape), axis, 0, 0, tiled=True)


def gather_pieces(x):
    devices = x.shape[-3]
    each = devices // PIECES
    if each == 1:
        return x
    lead, (rows, columns) = x.shape[:-3], x.shape[-2:]
    x = x.reshape(lead + (PIECES, each, rows, columns))
    return jnp.swapaxes(x, -3, -2).reshape(lead + (PIECES, rows, each * columns))


def scatter_pieces(x, devices):
    each = devices // PIECES
    if each == 1:
        return x
    lead, (rows, columns) = x.shape[:-3], x.shape[-2:]
    x = x.reshape(lead + (PIECES, rows, each, columns // each))
    return jnp.swapaxes(x, -3, -2).reshape(lead + (devices, rows, columns // each))


def ranks(hits):
    count = hits.shape[0]
    ahead = jnp.arange(count)[:, None] > jnp.arange(count)[None, :]
    return jnp.sum(jnp.where(ahead[:, :, None], hits.astype(jnp.int32)[None], 0), axis=1)


def local(
    hidden,
    attention_gain,
    query_weight,
    out_weight,
    root_cache,
    group_cache,
    group_length,
    suffix_cache,
    suffix_length,
    group_of,
    mixture_gain,
    routes,
    route_weight,
    expert_gate,
    expert_up,
    expert_down,
    shared_gate,
    shared_up,
    shared_down,
):
    owners, tensors = lax.axis_size("owner"), lax.axis_size("tensor")
    owner_index, tensor_index = lax.axis_index("owner"), lax.axis_index("tensor")
    requests = hidden.shape[0]
    fanout = routes.shape[1]
    split = tensors // EXP_OWN
    slots = -(-2 * requests // (owners * 16)) * 16
    expert_slots = -(-2 * requests * fanout // (EXP_OWN * owners * 16)) * 16

    destination = group_of // GROUP_OWN
    owner_range = jnp.arange(owners)
    to_owner = destination[:, None] == owner_range[None, :]
    slot_rank = ranks(to_owner)
    placed = to_owner[:, :, None] & (slot_rank[:, :, None] == jnp.arange(slots))
    unpick = placed.reshape(requests, owners * slots).astype(jnp.bfloat16)
    pick = unpick.T
    asked = jnp.sum(
        jnp.where(placed, (group_of % GROUP_OWN + 1)[:, None, None], 0), axis=0
    ).astype(jnp.bfloat16)
    named = routes.astype(jnp.bfloat16).reshape(slots, requests * fanout // slots)
    extra = jnp.concatenate(
        [
            asked[:, :, None],
            jnp.broadcast_to(named[None], (owners,) + named.shape),
            jnp.zeros((owners, slots, LANES - 1 - named.shape[1]), jnp.bfloat16),
        ],
        axis=2,
    )
    suffix_span, group_span = suffix_cache.shape[1], group_cache.shape[1]
    suffix_usable = (
        tensor_index * suffix_span + jnp.arange(suffix_span)[None, :] < suffix_length[:, None]
    )
    suffix_holder = jnp.where(suffix_usable, jnp.arange(requests)[:, None], -1).reshape(1, -1)
    group_usable = (
        tensor_index * group_span + jnp.arange(group_span)[None, :] < group_length[:, None]
    )
    group_holder = (
        jnp.where(group_usable, jnp.arange(1, GROUP_OWN + 1)[:, None], -1)
        .reshape(1, -1)
        .astype(jnp.float32)
    )
    experts = jnp.arange(owners * EXP_OWN)
    hits = routes[:, :, None] == experts[None, None, :]
    share = jnp.sum(jnp.where(hits, route_weight[:, :, None], 0.0), axis=1)
    hit = jnp.any(hits, axis=1)
    taken = hit[:, :, None] & (ranks(hit)[:, :, None] == jnp.arange(expert_slots))
    back_weight = jnp.where(taken, share[:, :, None], 0.0)
    back_weight = jnp.repeat(back_weight, split, axis=1).reshape(requests, -1)

    rows = gather_pieces(spread(hidden, "tensor", tensors))
    projected = project(rows, attention_gain.astype(jnp.float32)[None], query_weight)
    queries = gather_pieces(spread(projected, "tensor", tensors))
    sent = pick_queries(pick, extra, queries, owners, slots)
    arrived = lax.all_to_all(sent, "owner", 0, 0, tiled=True)
    first, mass = root_attention(
        queries, root_cache, suffix_cache.reshape(-1, KVW), suffix_holder
    )
    answered = group_attention(arrived, group_cache.reshape(-1, KVW), group_holder)
    back = lax.all_to_all(answered, "owner", 0, 0, tiled=True)
    parts = local_join(unpick, back.reshape(owners * slots, -1), first, mass)
    parts = lax.all_to_all(
        parts.reshape(tensors, -1, LAT + LANES), "tensor", 0, 0, tiled=True
    )
    attention = lax.all_to_all(join(parts), "tensor", 0, 0, tiled=True)
    mid = output_projection(attention.reshape(-1, LAT), out_weight, hidden)

    everything = spread(mid, ("owner", "tensor"), owners * tensors)
    everything = gather_pieces(everything.reshape((owners, tensors) + mid.shape))
    gain = mixture_gain.astype(jnp.float32)[None]
    all_routes = (
        arrived[:, :, H * KVW + 1 : H * KVW + 1 + named.shape[1]]
        .reshape(owners, requests, fanout)
        .astype(jnp.int32)
    )
    mine = owner_index * EXP_OWN + tensor_index // split
    called = jnp.any(all_routes == mine, axis=2)
    call_rank = ranks(called.T).T
    expert_pick = called[:, None, :] & (
        call_rank[:, None, :] == jnp.arange(expert_slots)[None, :, None]
    )
    expert_pick = jnp.where(
        (owner_range[:, None] == owner_range[None, :])[:, None, :, None],
        expert_pick[:, :, None, :],
        False,
    )
    expert_pick = expert_pick.reshape(owners * expert_slots, owners * requests).astype(jnp.bfloat16)
    results = expert(
        expert_pick, everything, gain, expert_gate, expert_up, expert_down, expert_slots
    )
    results = scatter_pieces(results, tensors).reshape(
        (owners * tensors, expert_slots, mid.shape[1])
    )
    returned = lax.all_to_all(results, ("owner", "tensor"), 0, 0, tiled=True)
    own_rows = lax.dynamic_index_in_dim(everything, owner_index, 0, keepdims=False)
    shared = shared_expert(own_rows, gain, shared_gate, shared_up, shared_down)
    shared = lax.all_to_all(scatter_pieces(shared, tensors), "tensor", 0, 0, tiled=True)
    return final_sum(returned.reshape(-1, mid.shape[1]), back_weight, shared, mid)


def solution(mesh):
    return jax.shard_map(
        local,
        mesh=mesh,
        in_specs=(
            P("owner", "tensor"),
            P(),
            P("tensor", None),
            P("tensor", None),
            P("tensor", None),
            P("owner", "tensor", None),
            P("owner"),
            P("owner", "tensor", None),
            P("owner"),
            P("owner"),
            P(),
            P("owner", None),
            P("owner", None),
            P(("owner", "tensor"), None, None),
            P(("owner", "tensor"), None, None),
            P(("owner", "tensor"), None, None),
            P("tensor", None),
            P("tensor", None),
            P("tensor", None),
        ),
        out_specs=P("owner", "tensor"),
        check_vma=False,
    )
```

time: 455 us -> 206 us (0.45)
  waiting for transfers between devices: 169 us -> 55.9 us
  blocking collectives: 125 us -> 39.5 us
  matrix products: 53.9 us -> 0 us
  Pallas kernels: 0 us -> 43.5 us
  other arithmetic: 21.5 us -> 3.63 us
  local copies, waits for them, and re-layouts: 49.2 us -> 31.6 us
  between operations: 13.8 us -> 0.43 us
  starting transfers between devices: 21.9 us -> 29.8 us
    all_gather x4 -> x0, blocking collectives: 125 us -> none  [the longest x1 31.6 us: local(): rows_full = lax.all_gather(hidden, 'tensor', axis=1, tiled=True)]
    all_gather x1 -> x0, waiting for transfers between devices: 93.9 us -> none  [combined_all(): everything = jax.tree.map(lambda part: lax.all_gather(part, axis), x)]
    reduce_scatter x1 -> x0, waiting for transfers between devices: 58.9 us -> none  [local(): lax.psum_scatter(routed + jnp.dot(activation, shared_down, preferred_elem...]
    dot_general x13 -> x0, matrix products: 53.9 us -> none  [the longest x1 8.3 us: local(): jnp.einsum('rhc,pc->rhp', queries, root_cache, preferred_element_type=jnp...]
    pallas_call x0 -> x10, Pallas kernels: none -> 43.5 us  [the longest x1 18.7 us: root_attention(): call(functools.partial(root_body, root_steps), (jax.ShapeDtypeStruct((cou...]
    all_to_all x6 -> x7, waiting for transfers between devices: 15.8 us -> 55.9 us  [the longest x3 34.5 us: spread(): lax.all_to_all(jnp.broadcast_to(x[None], (count,) + x.shape), axis, 0, 0,...]
    all_to_all x0 -> x2, blocking collectives: none -> 39.5 us  [the longest x1 21.7 us: local(): lax.all_to_all(parts.reshape(tensors, -1, LAT + LANES), 'tensor', 0, 0, t...]
    unnamed x24 -> x37, local copies, waits for them, and re-layouts: 1.11 us -> 26.7 us
  transfers between devices with their start and end apart: 8 -> 7, of which waited for: 5 -> 5; matrix products, arithmetic and copies ran while one was open for 13% -> 8% of each run, Pallas kernels for 0% -> 13%
where the time goes in v1:
time: 206 us; the launch traced here: 204 us
  waiting for transfers between devices  55.9 us (27%)
  Pallas kernels  43.5 us (21%)
  blocking collectives  39.5 us (19%)
  local copies, waits for them, and re-layouts  31.6 us (15%)
  starting transfers between devices  29.8 us (14%)
  other arithmetic  3.63 us (2%)
    all_to_all x3, waiting for transfers between devices, spread(): lax.all_to_all(jnp.broadcast_to(x[None], (count,) + x.shape), axis, 0, 0,...  34.5 us
    unnamed x37, local copies, waits for them, and re-layouts  26.7 us
    all_to_all x1, blocking collectives, local(): lax.all_to_all(parts.reshape(tensors, -1, LAT + LANES), 'tensor', 0, 0, t...  21.7 us
    pallas_call x1, Pallas kernels, root_attention(): call(functools.partial(root_body, root_steps), (jax.ShapeDtypeStruct((cou...  18.7 us
    all_to_all x1, blocking collectives, local(): attention = lax.all_to_all(join(parts), 'tensor', 0, 0, tiled=True)  17.7 us
    all_to_all x3, starting transfers between devices, spread(): lax.all_to_all(jnp.broadcast_to(x[None], (count,) + x.shape), axis, 0, 0,...  14.2 us
    all_to_all x1, waiting for transfers between devices, local(): arrived = lax.all_to_all(sent, 'owner', 0, 0, tiled=True)  12 us
    all_to_all x1, waiting for transfers between devices, local(): returned = lax.all_to_all(results, ('owner', 'tensor'), 0, 0, tiled=True)  9.4 us
  transfers between devices with their start and end apart: 7, of which 5 were waited for; matrix products, arithmetic and copies ran while one was open for 8% of the time, Pallas kernels for 13%

profile of v1, /device:TPU:0, one launch (start us, length us, event | category | flops | bytes accessed | tf_op | source)
XLA Modules:
  0.0 204.3 jit_solution(6786496733258958830)
XLA Ops:
  0.0 1.4 broadcast_in_dim.219
  1.4 7.3 %all-to-all-start = ((bf16[8,32,256]{2,1,0:T(8,128)(2,1)}), bf16[8,32,256]{2,1,0:T(8,128)(2,1)S(1)}, u32[]{:S(2)}, u32[]{:S(2)}) async-start(bf16[8,32,256]{2,1,0:T(8,128)(2,1)} %broadcast_in_dim.219), calls=%async_computation | async-start | bytes 262144 | tf_op jit(solution)/shard_map/all_to_all | solution.py:439
  10.0 6.0 %all-to-all-done.rows_ref = bf16[8,32,256]{2,1,0:T(8,128)(2,1)S(1)} async-done(((bf16[8,32,256]{2,1,0:T(8,128)(2,1)}), bf16[8,32,256]{2,1,0:T(8,128)(2,1)S(1)}, u32[]{:S(2)}, u32[]{:S(2)}) %all-to-all-start) | async-done | bytes 131104 | tf_op jit(solution)/shard_map/all_to_all | solution.py:439
  16.0 2.3 %copy-done.3 = bf16[1152,2048]{1,0:T(8,128)(2,1)S(1)} copy-done((bf16[1152,2048]{1,0:T(8,128)(2,1)S(1)}, bf16[1152,2048]{1,0:T(8,128)(2,1)}, u32[]{:S(2)}) %copy-start.3) | copy-done | bytes 4718616
  18.3 1.9 shard_map.181
  21.1 3.5 %all-to-all-start.1 = ((bf16[8,32,1152]{2,1,0:T(8,128)(2,1)}), bf16[8,32,1152]{2,1,0:T(8,128)(2,1)S(1)}, u32[]{:S(2)}, u32[]{:S(2)}) async-start(bf16[8,32,1152]{2,1,0:T(8,128)(2,1)} %broadcast_in_dim.222), calls=%async_computation.1 | async-start | bytes 1179648 | tf_op jit(solution)/shard_map/all_to_all | solution.py:439
  25.9 13.4 %all-to-all-done.1.rows_ref = bf16[8,32,1152]{2,1,0:T(8,128)(2,1)S(1)} async-done(((bf16[8,32,1152]{2,1,0:T(8,128)(2,1)}), bf16[8,32,1152]{2,1,0:T(8,128)(2,1)S(1)}, u32[]{:S(2)}, u32[]{:S(2)}) %all-to-all-start.1) | async-done | bytes 589856 | tf_op jit(solution)/shard_map/all_to_all | solution.py:439
  39.3 1.5 shard_map.182
  40.8 3.5 %all-to-all-start.2 = ((bf16[4,16,9344]{2,1,0:T(8,128)(2,1)}), bf16[4,16,9344]{2,1,0:T(8,128)(2,1)S(1)}, u32[]{:S(2)}, u32[]{:S(2)}) async-start(bf16[4,16,9344]{2,1,0:T(8,128)(2,1)} %shard_map.182), calls=%async_computation.2 | async-start | bytes 2392064 | tf_op jit(solution)/shard_map/all_to_all | solution.py:540
  44.4 3.9 %copy.47 = bf16[12,128,576]{2,1,0:T(8,128)(2,1)} copy(bf16[12,128,576]{1,2,0:T(8,128)(2,1)} %param.24) | data formatting | bytes 3538944 | tf_op args[5]
  48.3 12.0 %all-to-all-done.2.rows_ref = bf16[4,16,9344]{2,1,0:T(8,128)(2,1)S(1)} async-done(((bf16[4,16,9344]{2,1,0:T(8,128)(2,1)}), bf16[4,16,9344]{2,1,0:T(8,128)(2,1)S(1)}, u32[]{:S(2)}, u32[]{:S(2)}) %all-to-all-start.2) | async-done | bytes 1196064 | tf_op jit(solution)/shard_map/all_to_all | solution.py:540
  60.3 2.0 copy-done.5
  62.3 7.2 %shard_map.183 = bf16[4,16,8320]{2,1,0:T(8,128)(2,1)} custom-call(bf16[4,16,9344]{2,1,0:T(8,128)(2,1)S(1)} %all-to-all-done.2.rows_ref, bf16[1536,576]{1,0:T(8,128)(2,1)S(1)} %bitcast.34, f32[1,1536]{1,0:T(1,128)S(1)} %bitcast.40), custom_call_target="tpu_custom_call" | custom-call | flops 3422552064 | bytes 1769472 | tf_op jit(solution)/shard_map/pallas_call | solution.py:218
  69.5 3.6 %all-to-all-start.3 = ((bf16[4,16,8320]{2,1,0:T(8,128)(2,1)}), bf16[4,16,8320]{2,1,0:T(8,128)(2,1)S(1)}, u32[]{:S(2)}, u32[]{:S(2)}) async-start(bf16[4,16,8320]{2,1,0:T(8,128)(2,1)} %shard_map.183), calls=%async_computation.3 | async-start | bytes 2129920 | tf_op jit(solution)/shard_map/all_to_all | solution.py:545
  73.3 7.6 %copy.48.root_ref = bf16[4096,576]{1,0:T(8,128)(2,1)} copy(bf16[4096,576]{0,1:T(8,128)(2,1)} %param.23) | data formatting | bytes 9437184 | tf_op args[4]
  80.9 2.5 %copy-done.2 = bf16[4096,576]{1,0:T(8,128)(2,1)S(1)} copy-done((bf16[4096,576]{1,0:T(8,128)(2,1)S(1)}, bf16[4096,576]{1,0:T(8,128)(2,1)}, u32[]{:S(2)}) %copy-start.2) | copy-done | bytes 4718616
  83.4 1.7 copy-done.11
  85.2 18.7 %shard_map.184 = (f32[512,512]{1,0:T(8,128)S(1)}, f32[512,128]{1,0:T(8,128)S(1)}) custom-call(bf16[8,32,1152]{2,1,0:T(8,128)(2,1)S(1)} %all-to-all-done.1.rows_ref, bf16[4096,576]{1,0:T(8,128)(2,1)S(1)} %copy-done.2, bf16[2048,576]{1,0:T(8,128)(2,1)S(1)} %bitcast.41, s32[1,2048]{1,0:T(1,128)S(1)} %select_n.83.holder_ref), custom_call_target="tpu_custom_call" | custom-call | flops 6845104128 | bytes 7077888 | tf_op jit(solution)/shard_map/pallas_call | solution.py:163
  103.9 1.3 shard_map.185
  105.2 21.7 %all_to_all.45.parts_ref = bf16[8,64,640]{2,1,0:T(8,128)(2,1)S(1)} all-to-all(bf16[8,64,640]{2,1,0:T(8,128)(2,1)S(1)} %bitcast.32), channel_id=1, replica_groups=mesh['owner'=4,'tensor'=8] {'tensor'}, dimensions={0} | all-to-all | bytes 1310720 | tf_op jit(solution)/shard_map/all_to_all | solution.py:547
  127.4 17.7 %all_to_all.46 = bf16[8,64,512]{2,1,0:T(8,128)(2,1)S(1)} all-to-all(bf16[8,64,512]{2,1,0:T(8,128)(2,1)S(1)} %shard_map.186), channel_id=1, replica_groups=mesh['owner'=4,'tensor'=8] {'tensor'}, dimensions={0} | all-to-all | bytes 1048576 | tf_op jit(solution)/shard_map/all_to_all | solution.py:550
  145.1 2.0 shard_map.187.mid_ref
  148.0 3.5 %all-to-all-start.6 = ((bf16[32,32,256]{2,1,0:T(8,128)(2,1)}), bf16[32,32,256]{2,1,0:T(8,128)(2,1)S(1)}, u32[]{:S(2)}, u32[]{:S(2)}) async-start(bf16[32,32,256]{2,1,0:T(8,128)(2,1)} %broadcast_in_dim.230), calls=%async_computation.6 | async-start | bytes 1048576 | tf_op jit(solution)/shard_map/all_to_all | solution.py:439
  152.7 15.1 %all-to-all-done.6 = bf16[32,32,256]{2,1,0:T(8,128)(2,1)S(1)} async-done(((bf16[32,32,256]{2,1,0:T(8,128)(2,1)}), bf16[32,32,256]{2,1,0:T(8,128)(2,1)S(1)}, u32[]{:S(2)}, u32[]{:S(2)}) %all-to-all-start.6) | async-done | bytes 524320 | tf_op jit(solution)/shard_map/all_to_all | solution.py:439
  167.8 1.4 copy-done.8
  169.2 1.9 shard_map.189
  171.1 3.4 %all-to-all-start.8 = ((bf16[8,32,256]{2,1,0:T(8,128)(2,1)}), bf16[8,32,256]{2,1,0:T(8,128)(2,1)S(1)}, u32[]{:S(2)}, u32[]{:S(2)}) async-start(bf16[8,32,256]{2,1,0:T(8,128)(2,1)} %shard_map.189), calls=%async_computation.8 | async-start | bytes 262144 | tf_op jit(solution)/shard_map/all_to_all | solution.py:582
  174.7 2.6 %copy-done = bf16[1,1408,2048]{2,1,0:T(8,128)(2,1)S(1)} copy-done((bf16[1,1408,2048]{2,1,0:T(8,128)(2,1)S(1)}, bf16[1,1408,2048]{2,1,0:T(8,128)(2,1)}, u32[]{:S(2)}) %copy-start) | copy-done | bytes 5767192
  177.3 2.6 %copy-done.1 = bf16[1,1408,2048]{2,1,0:T(8,128)(2,1)S(1)} copy-done((bf16[1,1408,2048]{2,1,0:T(8,128)(2,1)S(1)}, bf16[1,1408,2048]{2,1,0:T(8,128)(2,1)}, u32[]{:S(2)}) %copy-start.1) | copy-done | bytes 5767192
  180.0 7.8 %shard_map.188 = bf16[4,8,16,256]{3,2,1,0:T(8,128)(2,1)} custom-call(bf16[64,128]{1,0:T(8,128)(2,1)S(1)} %reshape.237.pick_ref, bf16[4,8,32,256]{3,2,1,0:T(8,128)(2,1)S(1)} %bitcast.31, f32[1,2048]{1,0:T(1,128)S(1)} %bitcast.37, bf16[1,1408,2048]{2,1,0:T(8,128)(2,1)S(1)} %copy-done, bf16[1,1408,2048]{2,1,0:T(8,128)(2,1)S(1)} %copy-done.1, ...), custom_call_target="tpu_custom_call" | custom-call | flops 1107296256 | bytes 17301504 | tf_op jit(solution)/shard_map/pallas_call | solution.py:381
  187.8 5.0 %all-to-all-start.7 = ((bf16[32,16,256]{2,1,0:T(8,128)(2,1)}), bf16[32,16,256]{2,1,0:T(8,128)(2,1)S(1)}, u32[]{:S(2)}, u32[]{:S(2)}) async-start(bf16[32,16,256]{2,1,0:T(8,128)(2,1)} %bitcast.14), calls=%async_computation.7 | async-start | bytes 524288 | tf_op jit(solution)/shard_map/all_to_all | solution.py:579
  194.0 9.4 %all-to-all-done.7 = bf16[32,16,256]{2,1,0:T(8,128)(2,1)S(1)} async-done(((bf16[32,16,256]{2,1,0:T(8,128)(2,1)}), bf16[32,16,256]{2,1,0:T(8,128)(2,1)S(1)}, u32[]{:S(2)}, u32[]{:S(2)}) %all-to-all-start.7) | async-done | bytes 262176 | tf_op jit(solution)/shard_map/all_to_all | solution.py:579
  (90 shorter events, 8.4 us)
Async XLA Ops:
  1.4 14.6 %all-to-all-start = ((bf16[8,32,256]{2,1,0:T(8,128)(2,1)}), bf16[8,32,256]{2,1,0:T(8,128)(2,1)S(1)}, u32[]{:S(2)}, u32[]{:S(2)}) async-start(bf16[8,32,256]{2,1,0:T(8,128)(2,1)} %broadcast_in_dim.219), calls=%async_computation | async-start | bytes 262144 | tf_op jit(solution)/shard_map/all_to_all | solution.py:439
  16.0 2.3 %copy-start.3 = (bf16[1152,2048]{1,0:T(8,128)(2,1)S(1)}, bf16[1152,2048]{1,0:T(8,128)(2,1)}, u32[]{:S(2)}) copy-start(bf16[1152,2048]{1,0:T(8,128)(2,1)} %weight_ref.2) | copy-start | bytes 14155780
  20.2 5.3 %copy-start.12 = (s32[32,6]{0,1:T(8,128)S(1)}, s32[32,6]{0,1:T(8,128)}, u32[]{:S(2)}) copy-start(s32[32,6]{0,1:T(8,128)} %param.30) | copy-start | bytes 2308
  21.1 18.2 %all-to-all-start.1 = ((bf16[8,32,1152]{2,1,0:T(8,128)(2,1)}), bf16[8,32,1152]{2,1,0:T(8,128)(2,1)S(1)}, u32[]{:S(2)}, u32[]{:S(2)}) async-start(bf16[8,32,1152]{2,1,0:T(8,128)(2,1)} %broadcast_in_dim.222), calls=%async_computation.1 | async-start | bytes 1179648 | tf_op jit(solution)/shard_map/all_to_all | solution.py:439
  25.9 18.5 %copy-start.15 = (s32[12]{0:T(128)S(1)}, s32[12]{0:T(128)}, u32[]{:S(2)}) copy-start(s32[12]{0:T(128)} %param.25) | copy-start | bytes 148
  40.8 19.5 %all-to-all-start.2 = ((bf16[4,16,9344]{2,1,0:T(8,128)(2,1)}), bf16[4,16,9344]{2,1,0:T(8,128)(2,1)S(1)}, u32[]{:S(2)}, u32[]{:S(2)}) async-start(bf16[4,16,9344]{2,1,0:T(8,128)(2,1)} %shard_map.182), calls=%async_computation.2 | async-start | bytes 2392064 | tf_op jit(solution)/shard_map/all_to_all | solution.py:540
  60.3 9.2 %copy-start.9 = (bf16[4,16,9344]{2,1,0:T(8,128)(2,1)}, bf16[4,16,9344]{2,1,0:T(8,128)(2,1)S(1)}, u32[]{:S(2)}) copy-start(bf16[4,16,9344]{2,1,0:T(8,128)(2,1)S(1)} %all-to-all-done.2.rows_ref) | copy-start | bytes 3588100
  60.3 2.0 copy-start.5
  69.5 3.7 %copy-start.16 = (s32[32]{0:T(128)S(1)}, s32[32]{0:T(128)}, u32[]{:S(2)}) copy-start(s32[32]{0:T(128)} %param.27) | copy-start | bytes 388
  69.5 34.4 %all-to-all-start.3 = ((bf16[4,16,8320]{2,1,0:T(8,128)(2,1)}), bf16[4,16,8320]{2,1,0:T(8,128)(2,1)S(1)}, u32[]{:S(2)}, u32[]{:S(2)}) async-start(bf16[4,16,8320]{2,1,0:T(8,128)(2,1)} %shard_map.183), calls=%async_computation.3 | async-start | bytes 2129920 | tf_op jit(solution)/shard_map/all_to_all | solution.py:545
  80.9 2.5 %copy-start.2 = (bf16[4096,576]{1,0:T(8,128)(2,1)S(1)}, bf16[4096,576]{1,0:T(8,128)(2,1)}, u32[]{:S(2)}) copy-start(bf16[4096,576]{1,0:T(8,128)(2,1)} %copy.48.root_ref) | copy-start | bytes 14155780
  83.4 1.7 copy-start.11
  103.9 41.2 %copy-start.4 = (bf16[256,8192]{1,0:T(8,128)(2,1)S(1)}, bf16[256,8192]{1,0:T(8,128)(2,1)}, u32[]{:S(2)}) copy-start(bf16[256,8192]{1,0:T(8,128)(2,1)} %weight_ref.3) | copy-start | bytes 12582916
  105.2 39.9 %copy-start.10 = (bf16[32,256]{1,0:T(8,128)(2,1)S(1)}, bf16[32,256]{1,0:T(8,128)(2,1)}, u32[]{:S(2)}) copy-start(bf16[32,256]{1,0:T(8,128)(2,1)} %hidden_ref.1) | copy-start | bytes 49156
  145.1 6.3 %copy-start.13 = (bf16[2048]{0:T(1024)(128)(2,1)S(1)}, bf16[2048]{0:T(1024)(128)(2,1)}, u32[]{:S(2)}) copy-start(bf16[2048]{0:T(1024)(128)(2,1)} %param.29) | copy-start | bytes 12292
  145.1 22.7 %copy-start.7 = (bf16[352,2048]{1,0:T(8,128)(2,1)S(1)}, bf16[352,2048]{1,0:T(8,128)(2,1)}, u32[]{:S(2)}) copy-start(bf16[352,2048]{1,0:T(8,128)(2,1)} %up_ref.3) | copy-start | bytes 4325380
  147.1 20.7 %copy-start.6 = (bf16[352,2048]{1,0:T(8,128)(2,1)S(1)}, bf16[352,2048]{1,0:T(8,128)(2,1)}, u32[]{:S(2)}) copy-start(bf16[352,2048]{1,0:T(8,128)(2,1)} %gate_ref.3) | copy-start | bytes 4325380
  148.0 19.8 %all-to-all-start.6 = ((bf16[32,32,256]{2,1,0:T(8,128)(2,1)}), bf16[32,32,256]{2,1,0:T(8,128)(2,1)S(1)}, u32[]{:S(2)}, u32[]{:S(2)}) async-start(bf16[32,32,256]{2,1,0:T(8,128)(2,1)} %broadcast_in_dim.230), calls=%async_computation.6 | async-start | bytes 1048576 | tf_op jit(solution)/shard_map/all_to_all | solution.py:439
  167.8 1.4 copy-start.8
  171.1 16.6 %all-to-all-start.8 = ((bf16[8,32,256]{2,1,0:T(8,128)(2,1)}), bf16[8,32,256]{2,1,0:T(8,128)(2,1)S(1)}, u32[]{:S(2)}, u32[]{:S(2)}) async-start(bf16[8,32,256]{2,1,0:T(8,128)(2,1)} %shard_map.189), calls=%async_computation.8 | async-start | bytes 262144 | tf_op jit(solution)/shard_map/all_to_all | solution.py:582
  174.7 2.6 %copy-start = (bf16[1,1408,2048]{2,1,0:T(8,128)(2,1)S(1)}, bf16[1,1408,2048]{2,1,0:T(8,128)(2,1)}, u32[]{:S(2)}) copy-start(bf16[1,1408,2048]{2,1,0:T(8,128)(2,1)} %gate_ref.2) | copy-start | bytes 17301508
  177.3 2.6 %copy-start.1 = (bf16[1,1408,2048]{2,1,0:T(8,128)(2,1)S(1)}, bf16[1,1408,2048]{2,1,0:T(8,128)(2,1)}, u32[]{:S(2)}) copy-start(bf16[1,1408,2048]{2,1,0:T(8,128)(2,1)} %up_ref.2) | copy-start | bytes 17301508
  180.0 13.6 %copy-start.14 = (f32[32,6]{0,1:T(8,128)S(1)}, f32[32,6]{0,1:T(8,128)}, u32[]{:S(2)}) copy-start(f32[32,6]{0,1:T(8,128)} %param.31) | copy-start | bytes 2308
  187.8 15.7 %all-to-all-start.7 = ((bf16[32,16,256]{2,1,0:T(8,128)(2,1)}), bf16[32,16,256]{2,1,0:T(8,128)(2,1)S(1)}, u32[]{:S(2)}, u32[]{:S(2)}) async-start(bf16[32,16,256]{2,1,0:T(8,128)(2,1)} %bitcast.14), calls=%async_computation.7 | async-start | bytes 524288 | tf_op jit(solution)/shard_map/all_to_all | solution.py:579

commit v2 on v1

v2 whole, which is shorter than its diff:
```python
import functools

import jax
import jax.numpy as jnp
from jax import lax
from jax.experimental import pallas as pl
from jax.experimental.pallas import tpu as pltpu
from jax.sharding import Mesh
from jax.sharding import PartitionSpec as P

H = 16
LAT = 512
KVW = 576
EXP_OWN = 8
GROUP_OWN = 12
PIECES = 8
PAIR = 2 * KVW
LANES = 128
OWNER = ("pair", "core")
MASS_ROWS = 8
MIB = 1 << 20

score_scale = 192.0 ** (-0.5)
log2e = 1.4426950408889634
ln2 = 0.6931471805599453
lowest = -1e30
epsilon = 1e-06

NT = (((1,), (1,)), ((), ()))


def dot_nt(a, b):
    return lax.dot_general(a, b, NT, preferred_element_type=jnp.float32)


def dot_nn(a, b):
    return jnp.dot(a, b, preferred_element_type=jnp.float32)


def call(body, out_shape, vmem_mib, flops, nbytes, **options):
    return pl.pallas_call(
        body,
        out_shape=out_shape,
        compiler_params=pltpu.CompilerParams(vmem_limit_bytes=vmem_mib * MIB),
        cost_estimate=pl.CostEstimate(
            flops=int(flops), bytes_accessed=int(nbytes), transcendentals=0
        ),
        **options,
    )


VMEM = pl.BlockSpec(memory_space=pltpu.VMEM)
HBM = pl.BlockSpec(memory_space=pltpu.HBM)


def in_hbm(x):
    return pltpu.with_memory_space_constraint(x, pltpu.HBM)


def whole(shape):
    return pl.BlockSpec(shape, lambda *_: (0,) * len(shape))


def split_three(column):
    first = column.astype(jnp.bfloat16).astype(jnp.float32)
    second = (column - first).astype(jnp.bfloat16).astype(jnp.float32)
    third = (column - first - second).astype(jnp.bfloat16).astype(jnp.float32)
    return first, second, third


def normalised(read_piece, gain, width):
    rows = jnp.concatenate([read_piece(k) for k in range(PIECES)], axis=-1).astype(jnp.float32)
    square = jnp.sum(rows * rows, axis=-1, keepdims=True) * (1.0 / width)
    return (rows * lax.rsqrt(square + epsilon) * gain.astype(jnp.float32)).astype(jnp.bfloat16)


def project_body(rows_ref, gain_ref, weight_hbm, out_ref, weight_ref, sems):
    steps, each, width = weight_ref.shape
    copies = [
        pltpu.make_async_copy(
            weight_hbm.at[pl.ds(c * each, each)], weight_ref.at[c], sems.at[c]
        )
        for c in range(steps)
    ]
    for copy in copies:
        copy.start()
    normed = normalised(lambda k: rows_ref[k], gain_ref[...], width)
    for step in range(steps):
        copies[step].wait()
        out = dot_nt(normed, weight_ref[step]).astype(jnp.bfloat16)
        for k in range(out_ref.shape[0]):
            out_ref[k, :, step * each : (step + 1) * each] = out


def project(rows, gain, weight, copies):
    pieces, requests, part = rows.shape
    columns, width = weight.shape
    steps = 3 if columns % (3 * LANES) == 0 else 1
    return call(
        project_body,
        jax.ShapeDtypeStruct((copies, requests, columns), jnp.bfloat16),
        16,
        2 * requests * columns * width,
        2 * columns * width,
        in_specs=[VMEM, VMEM, HBM],
        out_specs=VMEM,
        scratch_shapes=[
            pltpu.VMEM((steps, columns // steps, width), jnp.bfloat16),
            pltpu.SemaphoreType.DMA((steps,)),
        ],
    )(rows, gain, in_hbm(weight))


def pick_body(pick_ref, extra_ref, rows_ref, out_ref):
    owners, slots, _ = out_ref.shape
    for k in range(PIECES):
        picked = dot_nn(pick_ref[...], rows_ref[k]).astype(jnp.bfloat16)
        for o in range(owners):
            out_ref[o, :, k * PAIR : (k + 1) * PAIR] = picked[o * slots : (o + 1) * slots]
    for o in range(owners):
        out_ref[o, :, PIECES * PAIR :] = extra_ref[o]


def pick_queries(pick, extra, rows, owners, slots):
    return call(
        pick_body,
        jax.ShapeDtypeStruct((owners, slots, H * KVW + LANES), jnp.bfloat16),
        16,
        2 * owners * slots * rows.shape[1] * H * KVW,
        4 * owners * slots * H * KVW,
    )(pick, extra, rows)


def running_softmax(scores, value_dot, at, m_ref, l_ref, acc_ref):
    before = m_ref[at, :]
    peak = jnp.maximum(before, jnp.max(scores, axis=-1, keepdims=True))
    weights = jnp.exp2(scores - peak)
    shrink = jnp.exp2(before - peak)
    l_ref[at, :] = l_ref[at, :] * shrink + jnp.sum(weights, axis=-1, keepdims=True)
    acc_ref[at, :] = acc_ref[at, :] * shrink + value_dot(weights.astype(jnp.bfloat16))
    m_ref[at, :] = peak


def finish(out_ref, m_ref, l_ref, acc_ref):
    total = l_ref[...]
    out_ref[:, :LAT] = acc_ref[...] / total
    out_ref[:, LAT:] = jnp.broadcast_to(
        m_ref[...] * ln2 + jnp.log(total), (total.shape[0], LANES)
    )


def by_head(rows_ref, q_ref):
    requests = rows_ref.shape[1]
    for k in range(PIECES):
        for j in range(2):
            at = (2 * k + j) * requests
            q_ref[at : at + requests, :] = rows_ref[k, :, j * KVW : (j + 1) * KVW]


def halves_of(count):
    return [slice(0, count // 2), slice(count // 2, count)]


def attention_scratch(count):
    return [
        pltpu.VMEM((count, KVW), jnp.bfloat16),
        pltpu.VMEM((count, 1), jnp.float32),
        pltpu.VMEM((count, 1), jnp.float32),
        pltpu.VMEM((count, LAT), jnp.float32),
    ]


def root_body(rows_ref, cache_ref, out_ref, q_ref, m_ref, l_ref, acc_ref):
    step = pl.program_id(0)

    @pl.when(step == 0)
    def _():
        by_head(rows_ref, q_ref)
        m_ref[...] = jnp.full(m_ref.shape, lowest, jnp.float32)
        l_ref[...] = jnp.zeros(l_ref.shape, jnp.float32)
        acc_ref[...] = jnp.zeros(acc_ref.shape, jnp.float32)

    halves = halves_of(q_ref.shape[0])
    scores = [dot_nn(q_ref[at, :], cache_ref[...]) * (score_scale * log2e) for at in halves]
    for at, block in zip(halves, scores):
        running_softmax(
            block, lambda w: dot_nt(w, cache_ref[:LAT, :]), at, m_ref, l_ref, acc_ref
        )

    @pl.when(step == pl.num_programs(0) - 1)
    def _():
        finish(out_ref, m_ref, l_ref, acc_ref)


def root_attention(rows, cache):
    count = H * rows.shape[1]
    positions = cache.shape[1]
    block = min(1024, positions)
    return call(
        root_body,
        pltpu.HBM((count, LAT + LANES), jnp.float32),
        32,
        2 * count * positions * (KVW + LAT),
        2 * KVW * positions,
        grid=(positions // block,),
        in_specs=[whole(rows.shape), pl.BlockSpec((KVW, block), lambda i: (0, i))],
        out_specs=whole((count, LAT + LANES)),
        scratch_shapes=attention_scratch(count),
    )(rows, in_hbm(cache))


def suffix_body(rows_ref, cache_ref, holder_ref, first_ref, out_ref, q_ref):
    requests = rows_ref.shape[1]
    each = q_ref.shape[1] // H
    group = pl.program_id(0)
    for k in range(PIECES):
        for j in range(2):
            h = 2 * k + j
            q_ref[0, h * each : (h + 1) * each, :] = rows_ref[
                k, pl.ds(pl.multiple_of(group * each, each), each), j * KVW : (j + 1) * KVW
            ]
    scores = dot_nt(q_ref[0], cache_ref[...]) * (score_scale * log2e)
    request = lax.broadcasted_iota(jnp.int32, (H * each, 1), 0) % each + group * each
    usable = holder_ref[...] == request
    scores = jnp.where(usable, scores, lowest)
    first = jnp.concatenate(
        [
            first_ref[pl.ds(pl.multiple_of(h * requests + group * each, each), each), :]
            for h in range(H)
        ],
        axis=0,
    )
    mass = first[:, LAT : LAT + 1] * log2e
    peak = jnp.maximum(mass, jnp.max(scores, axis=-1, keepdims=True))
    weights = jnp.exp2(scores - peak)
    shrink = jnp.exp2(mass - peak)
    total = shrink + jnp.sum(weights, axis=-1, keepdims=True)
    out = first[:, :LAT] * shrink + dot_nn(weights.astype(jnp.bfloat16), cache_ref[:, :LAT])
    out = out / total
    mass = jnp.broadcast_to(peak * ln2 + jnp.log(total), (H * each, LANES))
    for h in range(H):
        at = pl.ds(pl.multiple_of(h * requests + group * each, each), each)
        out_ref[at, :LAT] = out[h * each : (h + 1) * each]
        out_ref[at, LAT:] = mass[h * each : (h + 1) * each]


def suffix_attention(rows, cache, holder, first):
    requests = rows.shape[1]
    count = H * requests
    positions = cache.shape[0]
    groups = 2
    block = positions // groups
    return call(
        suffix_body,
        pltpu.HBM((count, LAT + LANES), jnp.float32),
        32,
        2 * count * block * (KVW + LAT),
        2 * KVW * positions,
        grid=(groups,),
        in_specs=[
            whole(rows.shape),
            pl.BlockSpec((block, KVW), lambda i: (i, 0)),
            pl.BlockSpec((1, block), lambda i: (0, i)),
            whole((count, LAT + LANES)),
        ],
        out_specs=whole((count, LAT + LANES)),
        scratch_shapes=[pltpu.VMEM((1, count // groups, KVW), jnp.bfloat16)],
    )(rows, in_hbm(cache), holder, in_hbm(first))


def group_body(rows_ref, cache_hbm, holder_ref, out_hbm, q_ref, keys_ref, out_ref, sems, out_sems):
    owners, slots, _ = rows_ref.shape
    groups, _, span = cache_hbm.shape
    copies = [
        pltpu.make_async_copy(
            cache_hbm.at[g], keys_ref.at[:, pl.ds(g * span, span)], sems.at[g]
        )
        for g in range(groups)
    ]
    for copy in copies:
        copy.start()
    for o in range(owners):
        for h in range(H):
            q_ref[o, h * slots : (h + 1) * slots, :] = rows_ref[o, :, h * KVW : (h + 1) * KVW]
    for copy in copies:
        copy.wait()
    lane = lax.broadcasted_iota(jnp.int32, (slots, LANES), 1)
    scores = [dot_nn(q_ref[o], keys_ref[...]) for o in range(owners)]
    sent = []
    for o in range(owners):
        asked = rows_ref[o, :, H * KVW :][:, :1].astype(jnp.float32)
        asked = jnp.concatenate([asked] * H, axis=0)
        usable = holder_ref[...] == asked
        block = jnp.where(usable, scores[o] * (score_scale * log2e), lowest)
        peak = jnp.max(block, axis=-1, keepdims=True)
        weights = jnp.where(usable, jnp.exp2(block - peak), 0.0)
        total = jnp.sum(weights, axis=-1, keepdims=True)
        present = total > 0.0
        safe = jnp.where(present, total, 1.0)
        block_out = dot_nt(weights.astype(jnp.bfloat16), keys_ref[:LAT, :]) / safe
        mass = jnp.where(present, peak * ln2 + jnp.log(safe), lowest)
        extra = jnp.zeros((slots, LANES), jnp.float32)
        for h in range(H):
            at = slice(h * slots, (h + 1) * slots)
            out_ref[o, :, h * LAT : (h + 1) * LAT] = block_out[at].astype(jnp.bfloat16)
            for k, part in enumerate(split_three(mass[at])):
                extra = jnp.where(lane == k * H + h, part, extra)
        out_ref[o, :, H * LAT :] = extra.astype(jnp.bfloat16)
        copy = pltpu.make_async_copy(out_ref.at[o], out_hbm.at[o], out_sems.at[o])
        copy.start()
        sent.append(copy)
    for copy in sent:
        copy.wait()


def group_attention(rows, cache, holder):
    owners, slots, _ = rows.shape
    groups, _, span = cache.shape
    width = H * LAT + LANES
    return call(
        group_body,
        pltpu.HBM((owners, slots, width), jnp.bfloat16),
        40,
        2 * owners * slots * H * groups * span * (KVW + LAT),
        2 * KVW * groups * span,
        in_specs=[VMEM, HBM, VMEM],
        out_specs=HBM,
        scratch_shapes=[
            pltpu.VMEM((owners, H * slots, KVW), jnp.bfloat16),
            pltpu.VMEM((KVW, groups * span), jnp.bfloat16),
            pltpu.VMEM((owners, slots, width), jnp.bfloat16),
            pltpu.SemaphoreType.DMA((groups,)),
            pltpu.SemaphoreType.DMA((owners,)),
        ],
    )(rows, in_hbm(cache), holder)


def local_body(unpick_ref, back_ref, first_hbm, out_ref, first_ref, out_mass_ref, sem):
    copy = pltpu.make_async_copy(first_hbm, first_ref, sem)
    copy.start()
    requests = unpick_ref.shape[0]
    unpick = unpick_ref[...]
    extra = dot_nn(unpick, back_ref[:, H * LAT :])
    shares, length = out_ref.shape[0], out_ref.shape[1] - MASS_ROWS
    copy.wait()
    for h in range(H):
        at = slice(h * requests, (h + 1) * requests)
        group_out = dot_nn(unpick, back_ref[:, h * LAT : (h + 1) * LAT])
        group_mass = (
            extra[:, h : h + 1] + extra[:, H + h : H + h + 1] + extra[:, 2 * H + h : 2 * H + h + 1]
        )
        first_mass = first_ref[at, LAT : LAT + 1]
        peak = jnp.maximum(first_mass, group_mass)
        first_weight = jnp.exp(first_mass - peak)
        group_weight = jnp.exp(group_mass - peak)
        total = first_weight + group_weight
        out = (first_weight * first_ref[at, :LAT] + group_weight * group_out) / total
        out = out.astype(jnp.bfloat16)
        each = min(length, requests)
        for k in range(requests // each):
            share, row = divmod(h * requests + k * each, length)
            out_ref[share, row : row + each, :] = out[k * each : (k + 1) * each]
        out_mass_ref[at, :] = peak + jnp.log(total)
    diagonal = lax.broadcasted_iota(jnp.int32, (length, LAT), 0) == lax.broadcasted_iota(
        jnp.int32, (length, LAT), 1
    )
    row = lax.broadcasted_iota(jnp.int32, (MASS_ROWS, LAT), 0)
    for share in range(shares):
        masses = jnp.where(diagonal, out_mass_ref[share * length : (share + 1) * length, :], 0.0)
        masses = jnp.sum(masses, axis=0, keepdims=True)
        tail = jnp.zeros((MASS_ROWS, LAT), jnp.float32)
        for k, part in enumerate(split_three(masses)):
            tail = jnp.where(row == k, part, tail)
        out_ref[share, length:, :] = tail.astype(jnp.bfloat16)


def local_join(unpick, back, first, shares):
    count = first.shape[0]
    return call(
        local_body,
        jax.ShapeDtypeStruct((shares, count // shares + MASS_ROWS, LAT), jnp.bfloat16),
        10,
        2 * unpick.shape[0] * back.shape[0] * back.shape[1],
        4 * count * LAT,
        in_specs=[VMEM, VMEM, HBM],
        out_specs=VMEM,
        scratch_shapes=[
            pltpu.VMEM(first.shape, jnp.float32),
            pltpu.VMEM((count, 1), jnp.float32),
            pltpu.SemaphoreType.DMA,
        ],
    )(unpick, back, in_hbm(first))


def join_body(parts_ref, out_ref):
    sources, copies, length = parts_ref.shape[0], out_ref.shape[0], out_ref.shape[1]
    diagonal = lax.broadcasted_iota(jnp.int32, (length, LAT), 0) == lax.broadcasted_iota(
        jnp.int32, (length, LAT), 1
    )
    masses = []
    for s in range(sources):
        tail = parts_ref[s, length:, :].astype(jnp.float32)
        mass = tail[0:1] + tail[1:2] + tail[2:3]
        masses.append(jnp.sum(jnp.where(diagonal, mass, 0.0), axis=1, keepdims=True))
    peak = functools.reduce(jnp.maximum, masses)
    scales = [jnp.exp(mass - peak) for mass in masses]
    total = functools.reduce(jnp.add, scales)
    out = functools.reduce(
        jnp.add,
        [scales[s] * parts_ref[s, :length, :].astype(jnp.float32) for s in range(sources)],
    )
    out = (out / total).astype(jnp.bfloat16)
    for c in range(copies):
        out_ref[c] = out


def join(parts):
    sources, rows, _ = parts.shape
    rows -= MASS_ROWS
    return call(
        join_body,
        jax.ShapeDtypeStruct((sources, rows, LAT), jnp.bfloat16),
        6,
        3e10,
        4 * sources * rows * LAT,
    )(parts)


def output_body(rows_ref, weight_ref, hidden_ref, out_ref, copies_ref):
    requests = hidden_ref.shape[0]
    total = hidden_ref[...].astype(jnp.float32)
    for h in range(H):
        total = total + dot_nt(
            rows_ref[h * requests : (h + 1) * requests, :],
            weight_ref[:, h * LAT : (h + 1) * LAT],
        )
    out = total.astype(jnp.bfloat16)
    out_ref[...] = out
    for c in range(copies_ref.shape[0]):
        copies_ref[c] = out


def output_projection(rows, weight, hidden, copies):
    features, width = weight.shape
    requests = hidden.shape[0]
    return call(
        output_body,
        (
            jax.ShapeDtypeStruct(hidden.shape, jnp.bfloat16),
            jax.ShapeDtypeStruct((copies,) + hidden.shape, jnp.bfloat16),
        ),
        8,
        2 * requests * features * width,
        2 * features * width,
        in_specs=[VMEM] * 3,
        out_specs=(VMEM, VMEM),
    )(rows, weight, hidden)


def gated(rows, gate, up):
    gate_part = dot_nt(rows, gate)
    up_part = dot_nt(rows, up)
    return (gate_part / (1.0 + jnp.exp(-gate_part)) * up_part).astype(jnp.bfloat16)


def expert_body(pick_ref, rows_ref, gain_ref, shared_gate_ref, shared_up_ref, shared_down_ref, gate_ref, up_ref, down_ref, out_ref):
    owners, _, requests, part = rows_ref.shape
    width = gain_ref.shape[1]
    share = requests // owners
    slots = out_ref.shape[2] - share
    rows = jnp.concatenate(
        [
            normalised(lambda k, o=o: rows_ref[o, k], gain_ref[...], width)
            for o in range(owners)
        ],
        axis=0,
    )
    rows = dot_nn(pick_ref[...], rows).astype(jnp.bfloat16)
    named, rest = rows[: owners * slots], rows[owners * slots :]
    shared = dot_nn(gated(rest, shared_gate_ref[...], shared_up_ref[...]), shared_down_ref[...])
    units = gate_ref.shape[1]
    steps = 4 if units % 64 == 0 and units > 704 else 1
    each = units // steps
    total = jnp.zeros((owners * slots, width), jnp.float32)
    for c in range(steps):
        at = slice(c * each, (c + 1) * each)
        total = total + dot_nn(
            gated(named, gate_ref[0, at, :], up_ref[0, at, :]), down_ref[0, at, :]
        )
    for o in range(owners):
        both = jnp.concatenate(
            [total[o * slots : (o + 1) * slots], shared[o * share : (o + 1) * share]], axis=0
        ).astype(jnp.bfloat16)
        for k in range(PIECES):
            out_ref[o, k] = both[:, k * part : (k + 1) * part]


def expert(pick, rows, gain, slots, shared, weights):
    owners, _, requests, part = rows.shape
    _, units, width = weights[0].shape
    return call(
        expert_body,
        jax.ShapeDtypeStruct(
            (owners, PIECES, slots + requests // owners, part), jnp.bfloat16
        ),
        12,
        6 * pick.shape[0] * units * width,
        6 * units * width,
        in_specs=[VMEM] * 9,
        out_specs=VMEM,
    )(pick, rows, gain, *shared, *weights)


def final_body(parts_ref, weight_ref, mid_ref, out_ref):
    weight = weight_ref[...]
    high = weight.astype(jnp.bfloat16)
    rest = weight - high.astype(jnp.float32)
    low = rest.astype(jnp.bfloat16)
    lower = (rest - low.astype(jnp.float32)).astype(jnp.bfloat16)
    parts = parts_ref[...]
    total = dot_nn(high, parts) + (dot_nn(low, parts) + dot_nn(lower, parts))
    out_ref[...] = (mid_ref[...].astype(jnp.float32) + total).astype(jnp.bfloat16)


def final_sum(parts, weight, mid):
    return call(
        final_body,
        jax.ShapeDtypeStruct(mid.shape, jnp.bfloat16),
        16,
        2 * weight.shape[0] * parts.shape[0] * parts.shape[1],
        2 * parts.shape[0] * parts.shape[1],
    )(parts, weight, mid)


def exchange(x, axis):
    return lax.all_to_all(x, axis, 0, 0, tiled=True)


def gather_pieces(x):
    devices = x.shape[-3]
    each = devices // PIECES
    if each == 1:
        return x
    lead, (rows, columns) = x.shape[:-3], x.shape[-2:]
    x = x.reshape(lead + (PIECES, each, rows, columns))
    return jnp.swapaxes(x, -3, -2).reshape(lead + (PIECES, rows, each * columns))


def scatter_pieces(x, devices):
    each = devices // PIECES
    if each == 1:
        return x
    lead, (rows, columns) = x.shape[:-3], x.shape[-2:]
    x = x.reshape(lead + (PIECES, rows, each, columns // each))
    return jnp.swapaxes(x, -3, -2).reshape(lead + (devices, rows, columns // each))


def ranks(hits):
    count = hits.shape[0]
    ahead = jnp.arange(count)[:, None] > jnp.arange(count)[None, :]
    return jnp.sum(jnp.where(ahead[:, :, None], hits.astype(jnp.int32)[None], 0), axis=1)


def local(
    hidden,
    attention_gain,
    query_weight,
    out_weight,
    root_cache,
    group_cache,
    group_length,
    suffix_cache,
    suffix_length,
    group_of,
    mixture_gain,
    routes,
    route_weight,
    expert_gate,
    expert_up,
    expert_down,
    shared_gate,
    shared_up,
    shared_down,
):
    owners, tensors = lax.axis_size(OWNER), lax.axis_size("tensor")
    owner_index, tensor_index = lax.axis_index(OWNER), lax.axis_index("tensor")
    requests = hidden.shape[0]
    fanout = routes.shape[1]
    pairs = owners // 2
    split = tensors // EXP_OWN
    slots = -(-2 * requests // (owners * 16)) * 16
    expert_slots = -(-2 * requests * fanout // (EXP_OWN * owners * 16)) * 16

    if group_cache.shape[1] % LANES:
        group_columns = group_cache.reshape(-1, KVW).T[None]
    else:
        group_columns = jnp.swapaxes(group_cache, 1, 2)
    rows = exchange(jnp.broadcast_to(hidden[None], (tensors,) + hidden.shape), "tensor")

    projected = project(
        gather_pieces(rows), attention_gain[None], query_weight, tensors
    )
    projected, group_of, group_length, suffix_length, routes, route_weight = (
        lax.optimization_barrier(
            (projected, group_of, group_length, suffix_length, routes, route_weight)
        )
    )
    destination = group_of // GROUP_OWN
    owner_range = jnp.arange(owners)
    to_owner = destination[:, None] == owner_range[None, :]
    slot_rank = ranks(to_owner)
    placed = to_owner[:, :, None] & (slot_rank[:, :, None] == jnp.arange(slots))
    unpick = placed.reshape(requests, owners * slots).astype(jnp.bfloat16)
    pick = unpick.T
    asked = jnp.sum(
        jnp.where(placed, (group_of % GROUP_OWN + 1)[:, None, None], 0), axis=0
    ).astype(jnp.bfloat16)
    named = routes.astype(jnp.bfloat16).reshape(slots, requests * fanout // slots)
    extra = jnp.where(
        jnp.arange(LANES) == 0,
        asked[:, :, None],
        jnp.pad(named, ((0, 0), (1, LANES - 1 - named.shape[1])))[None],
    )
    suffix_span, group_span = suffix_cache.shape[1], group_cache.shape[1]
    suffix_usable = (
        tensor_index * suffix_span + jnp.arange(suffix_span)[None, :] < suffix_length[:, None]
    )
    suffix_holder = jnp.where(suffix_usable, jnp.arange(requests)[:, None], -1).reshape(1, -1)
    group_usable = (
        tensor_index * group_span + jnp.arange(group_span)[None, :] < group_length[:, None]
    )
    group_holder = (
        jnp.where(group_usable, jnp.arange(1, GROUP_OWN + 1)[:, None], -1)
        .reshape(1, -1)
        .astype(jnp.float32)
    )
    experts = jnp.arange(owners * EXP_OWN)
    hits = routes[:, :, None] == experts[None, None, :]
    share = jnp.sum(jnp.where(hits, route_weight[:, :, None], 0.0), axis=1)
    hit = jnp.any(hits, axis=1)
    taken = hit[:, :, None] & (ranks(hit)[:, :, None] == jnp.arange(expert_slots))
    back_weight = jnp.where(taken, share[:, :, None], 0.0)
    back_weight = jnp.repeat(back_weight, split, axis=1)
    token_share = requests // owners
    shared_token = owner_range[:, None] * token_share + jnp.arange(token_share)
    shared_weight = shared_token.reshape(-1)[None, :] == jnp.arange(requests)[:, None]
    shared_weight = jnp.broadcast_to(
        shared_weight.reshape(requests, owners, 1, token_share).astype(jnp.float32),
        (requests, owners, tensors, token_share),
    ).reshape(requests, owners * tensors, token_share)
    back_weight = jnp.concatenate([back_weight, shared_weight], axis=2).reshape(requests, -1)

    queries, back_weight, suffix_holder, group_holder = lax.optimization_barrier(
        (exchange(projected, "tensor"), back_weight, suffix_holder, group_holder)
    )
    queries = gather_pieces(queries)
    arrived = exchange(pick_queries(pick, extra, queries, owners, slots), OWNER)
    if group_span % LANES:
        group_columns = group_cache.reshape(-1, KVW).T[None]
    else:
        group_columns = jnp.swapaxes(group_cache, 1, 2)
    first = root_attention(queries, root_cache.T)
    arrived, first = lax.optimization_barrier((arrived, first))
    all_routes = (
        arrived[:, :, H * KVW + 1 : H * KVW + 1 + named.shape[1]]
        .reshape(owners, requests, fanout)
        .astype(jnp.int32)
    )
    mine = owner_index * EXP_OWN + tensor_index // split
    called = jnp.any(all_routes == mine, axis=2)
    call_rank = ranks(called.T).T
    expert_pick = called[:, None, :] & (
        call_rank[:, None, :] == jnp.arange(expert_slots)[None, :, None]
    )
    seen = owner_range.reshape(2, pairs)
    seen = 2 * (seen % pairs) + seen // pairs
    expert_pick = jnp.where(
        (owner_range[:, None] == seen.reshape(-1)[None, :])[:, None, :, None],
        expert_pick[:, :, None, :],
        False,
    )
    shared_pick = (
        owner_range[:, None, None] * requests
        + owner_index * token_share
        + jnp.arange(token_share)[None, :, None]
    ).reshape(-1, 1) == (seen.reshape(-1, 1) * requests + jnp.arange(requests)).reshape(1, -1)
    expert_pick = jnp.concatenate(
        [expert_pick.reshape(owners * expert_slots, owners * requests), shared_pick], axis=0
    ).astype(jnp.bfloat16)
    answered = group_attention(arrived, group_columns, group_holder)
    back = exchange(answered, OWNER)
    first = suffix_attention(queries, suffix_cache.reshape(-1, KVW), suffix_holder, first)
    back, expert_pick, gain = lax.optimization_barrier((back, expert_pick, mixture_gain[None]))
    parts = local_join(unpick, back.reshape(owners * slots, -1), first, tensors)
    attention = exchange(join(exchange(parts, "tensor")), "tensor")
    mid, copies = output_projection(
        attention.reshape(-1, LAT), out_weight, hidden, owners // 2 * tensors
    )

    half = exchange(copies, ("pair", "tensor"))
    both = lax.all_gather(half.reshape((pairs, tensors) + mid.shape), "core")
    everything = gather_pieces(both.reshape((owners, tensors) + mid.shape))
    results = expert(
        expert_pick,
        everything,
        gain,
        expert_slots,
        (shared_gate, shared_up, shared_down),
        (expert_gate, expert_up, expert_down),
    )
    results = scatter_pieces(results, tensors).reshape((owners * tensors, -1, mid.shape[1]))
    returned = exchange(results, ("pair", "core", "tensor"))
    return final_sum(returned.reshape(-1, mid.shape[1]), back_weight, mid)


def solution(mesh):
    owners, tensors = mesh.shape["owner"], mesh.shape["tensor"]
    devices = mesh.devices.reshape(owners // 2, 2, tensors)
    return jax.shard_map(
        local,
        mesh=Mesh(devices, OWNER + ("tensor",)),
        in_specs=(
            P(OWNER, "tensor"),
            P(),
            P("tensor", None),
            P("tensor", None),
            P("tensor", None),
            P(OWNER, "tensor", None),
            P(OWNER),
            P(OWNER, "tensor", None),
            P(OWNER),
            P(OWNER),
            P(),
            P(OWNER, None),
            P(OWNER, None),
            P(OWNER + ("tensor",), None, None),
            P(OWNER + ("tensor",), None, None),
            P(OWNER + ("tensor",), None, None),
            P("tensor", None),
            P("tensor", None),
            P("tensor", None),
        ),
        out_specs=P(OWNER, "tensor"),
        check_vma=False,
    )
```

time: 206 us -> 168 us (0.82)
  blocking collectives: 39.5 us -> 68.3 us
  local copies, waits for them, and re-layouts: 31.6 us -> 3.81 us
  waiting for transfers between devices: 55.9 us -> 34 us
  starting transfers between devices: 29.8 us -> 18.2 us
  Pallas kernels: 43.5 us -> 40.3 us
    all_to_all x2 -> x4, blocking collectives: 39.5 us -> 66.2 us  [exchange(): return lax.all_to_all(x, axis, 0, 0, tiled=True)]
    unnamed x37 -> x35, local copies, waits for them, and re-layouts: 26.7 us -> 0.1 us
    all_to_all x7 -> x4, waiting for transfers between devices: 55.9 us -> 34 us  [exchange(): return lax.all_to_all(x, axis, 0, 0, tiled=True)]
    all_to_all x7 -> x4, starting transfers between devices: 29.8 us -> 18.2 us  [exchange(): return lax.all_to_all(x, axis, 0, 0, tiled=True)]
    pallas_call x8, Pallas kernels: 41.6 us -> 38.6 us  [the longest x1 9.87 us: root_attention(): call(root_body, pltpu.HBM((count, LAT + LANES), jnp.float32), 32, 2 * cou...]
    all_gather x0 -> x1, blocking collectives: none -> 2.17 us  [local(): both = lax.all_gather(half.reshape((pairs, tensors) + mid.shape), 'core')]
  transfers between devices with their start and end apart: 7 -> 4, of which waited for: 5 -> 4; matrix products, arithmetic and copies ran while one was open for 8% -> 2% of each run, Pallas kernels for 13% -> 9%
where the time goes in v2:
time: 168 us
  blocking collectives  68.3 us (41%)
  Pallas kernels  40.3 us (24%)
  waiting for transfers between devices  34 us (20%)
  starting transfers between devices  18.2 us (11%)
  local copies, waits for them, and re-layouts  3.81 us (2%)
  other arithmetic  2.5 us (1%)
    all_to_all x4, blocking collectives, exchange(): return lax.all_to_all(x, axis, 0, 0, tiled=True)  66.2 us
    all_to_all x4, waiting for transfers between devices, exchange(): return lax.all_to_all(x, axis, 0, 0, tiled=True)  34 us
    all_to_all x4, starting transfers between devices, exchange(): return lax.all_to_all(x, axis, 0, 0, tiled=True)  18.2 us
    pallas_call x1, Pallas kernels, root_attention(): call(root_body, pltpu.HBM((count, LAT + LANES), jnp.float32), 32, 2 * cou...  9.87 us
    pallas_call x1, Pallas kernels, group_attention(): call(group_body, pltpu.HBM((owners, slots, width), jnp.bfloat16), 40, 2 *...  7.59 us
    pallas_call x1, Pallas kernels, expert(): call(expert_body, jax.ShapeDtypeStruct((owners, PIECES, slots + requests...  6.13 us
    pallas_call x1, Pallas kernels, suffix_attention(): call(suffix_body, pltpu.HBM((count, LAT + LANES), jnp.float32), 32, 2 * c...  5.35 us
    pallas_call x1, Pallas kernels, project(): call(project_body, jax.ShapeDtypeStruct((copies, requests, columns), jnp....  4.24 us
  transfers between devices with their start and end apart: 4, of which 4 were waited for; matrix products, arithmetic and copies ran while one was open for 2% of the time, Pallas kernels for 9%

profile of v2, /device:TPU:0, one launch (start us, length us, event | category | flops | bytes accessed | tf_op | source)
XLA Modules:
  0.0 167.6 jit_solution(725862261038907708)
XLA Ops:
  0.0 1.4 broadcast_in_dim.213
  1.4 7.3 %all-to-all-start = ((bf16[8,32,256]{2,1,0:T(8,128)(2,1)}), bf16[8,32,256]{2,1,0:T(8,128)(2,1)S(1)}, u32[]{:S(2)}, u32[]{:S(2)}) async-start(bf16[8,32,256]{2,1,0:T(8,128)(2,1)} %broadcast_in_dim.213), calls=%async_computation | async-start | bytes 262144 | tf_op jit(solution)/shard_map/all_to_all | solution.py:536
  9.0 0.7 broadcast_in_dim.214.gain_ref
  9.8 6.1 %all-to-all-done.rows_ref = bf16[8,32,256]{2,1,0:T(8,128)(2,1)S(1)} async-done(((bf16[8,32,256]{2,1,0:T(8,128)(2,1)}), bf16[8,32,256]{2,1,0:T(8,128)(2,1)S(1)}, u32[]{:S(2)}, u32[]{:S(2)}) %all-to-all-start) | async-done | bytes 131104 | tf_op jit(solution)/shard_map/all_to_all | solution.py:536
  16.0 4.2 %shard_map.181 = bf16[8,32,1152]{2,1,0:T(8,128)(2,1)} custom-call(bf16[8,32,256]{2,1,0:T(8,128)(2,1)S(1)} %all-to-all-done.rows_ref, bf16[1,2048]{1,0:T(2,128)(2,1)S(1)} %broadcast_in_dim.214.gain_ref, bf16[1152,2048]{1,0:T(8,128)(2,1)} %weight_hbm.1), custom_call_target="tpu_custom_call" | custom-call | flops 150994944 | bytes 4718592 | tf_op jit(solution)/shard_map/pallas_call | solution.py:99
  20.5 0.2 select_reduce_fusion
  20.7 0.5 fusion.1
  21.2 0.2 pad_maximum_fusion
  21.4 0.3 reshape.407.weight_ref
  22.0 3.5 %all-to-all-start.1 = ((bf16[8,32,1152]{2,1,0:T(8,128)(2,1)}), bf16[8,32,1152]{2,1,0:T(8,128)(2,1)S(1)}, u32[]{:S(2)}, u32[]{:S(2)}) async-start(bf16[8,32,1152]{2,1,0:T(8,128)(2,1)} %shard_map.181), calls=%async_computation.1 | async-start | bytes 1179648 | tf_op jit(solution)/shard_map/all_to_all | solution.py:536
  25.7 0.2 select_reduce_fusion.4
  26.5 13.7 %all-to-all-done.1.rows_ref = bf16[8,32,1152]{2,1,0:T(8,128)(2,1)S(1)} async-done(((bf16[8,32,1152]{2,1,0:T(8,128)(2,1)}), bf16[8,32,1152]{2,1,0:T(8,128)(2,1)S(1)}, u32[]{:S(2)}, u32[]{:S(2)}) %all-to-all-start.1) | async-done | bytes 589856 | tf_op jit(solution)/shard_map/all_to_all | solution.py:536
  40.2 1.5 shard_map.182
  41.7 3.7 %all-to-all-start.2 = ((bf16[4,16,9344]{2,1,0:T(8,128)(2,1)}), bf16[4,16,9344]{2,1,0:T(8,128)(2,1)S(1)}, u32[]{:S(2)}, u32[]{:S(2)}) async-start(bf16[4,16,9344]{2,1,0:T(8,128)(2,1)} %shard_map.182), calls=%async_computation.2 | async-start | bytes 2392064 | tf_op jit(solution)/shard_map/all_to_all | solution.py:536
  45.8 9.9 %shard_map.183.first_ref = f32[512,640]{1,0:T(8,128)} custom-call(bf16[8,32,1152]{2,1,0:T(8,128)(2,1)S(1)} %all-to-all-done.1.rows_ref, bf16[576,4096]{1,0:T(8,128)(2,1)} %bitcast.43), custom_call_target="tpu_custom_call" | custom-call | flops 4563402752 | bytes 4718592 | tf_op jit(solution)/shard_map/pallas_call | solution.py:199
  55.7 5.7 %all-to-all-done.2.rows_ref = bf16[4,16,9344]{2,1,0:T(8,128)(2,1)S(1)} async-done(((bf16[4,16,9344]{2,1,0:T(8,128)(2,1)}), bf16[4,16,9344]{2,1,0:T(8,128)(2,1)S(1)}, u32[]{:S(2)}, u32[]{:S(2)}) %all-to-all-start.2) | async-done | bytes 1196064 | tf_op jit(solution)/shard_map/all_to_all | solution.py:536
  61.5 7.6 %shard_map.184 = bf16[4,16,8320]{2,1,0:T(8,128)(2,1)} custom-call(bf16[4,16,9344]{2,1,0:T(8,128)(2,1)S(1)} %all-to-all-done.2.rows_ref, bf16[12,576,128]{2,1,0:T(8,128)(2,1)} %bitcast.44, f32[1,1536]{1,0:T(1,128)S(1)} %bitcast.37), custom_call_target="tpu_custom_call" | custom-call | flops 3422552064 | bytes 1769472 | tf_op jit(solution)/shard_map/pallas_call | solution.py:320
  69.1 3.7 %all-to-all-start.3 = ((bf16[4,16,8320]{2,1,0:T(8,128)(2,1)}), bf16[4,16,8320]{2,1,0:T(8,128)(2,1)S(1)}, u32[]{:S(2)}, u32[]{:S(2)}) async-start(bf16[4,16,8320]{2,1,0:T(8,128)(2,1)} %shard_map.184), calls=%async_computation.3 | async-start | bytes 2129920 | tf_op jit(solution)/shard_map/all_to_all | solution.py:536
  72.8 0.1 reduce_or.19
  73.0 0.1 select_reduce_fusion.2
  73.4 5.3 %shard_map.185.first_hbm = f32[512,640]{1,0:T(8,128)} custom-call(bf16[8,32,1152]{2,1,0:T(8,128)(2,1)S(1)} %all-to-all-done.1.rows_ref, bf16[2048,576]{1,0:T(8,128)(2,1)} %bitcast.38, s32[1,2048]{1,0:T(1,128)S(1)} %select_n.118.holder_ref, f32[512,640]{1,0:T(8,128)} %shard_map.183.first_ref), custom_call_target="tpu_custom_call" | custom-call | flops 1140850688 | bytes 2359296 | tf_op jit(solution)/shard_map/pallas_call | solution.py:253
  78.8 8.5 %all-to-all-done.3 = bf16[4,16,8320]{2,1,0:T(8,128)(2,1)S(1)} async-done(((bf16[4,16,8320]{2,1,0:T(8,128)(2,1)}), bf16[4,16,8320]{2,1,0:T(8,128)(2,1)S(1)}, u32[]{:S(2)}, u32[]{:S(2)}) %all-to-all-start.3) | async-done | bytes 1064992 | tf_op jit(solution)/shard_map/all_to_all | solution.py:536
  87.3 3.1 %shard_map.186 = bf16[8,72,512]{2,1,0:T(8,128)(2,1)S(1)} custom-call(bf16[32,64]{1,0:T(8,128)(2,1)S(1)} %and_convert_fusion.unpick_ref, bf16[64,8320]{1,0:T(8,128)(2,1)S(1)} %bitcast.31, f32[512,640]{1,0:T(8,128)} %shard_map.185.first_hbm), custom_call_target="tpu_custom_call" | custom-call | flops 34078720 | bytes 1048576 | tf_op jit(solution)/shard_map/pallas_call | solution.py:379
  90.4 20.1 %all_to_all.40.parts_ref = bf16[8,72,512]{2,1,0:T(8,128)(2,1)S(1)} all-to-all(bf16[8,72,512]{2,1,0:T(8,128)(2,1)S(1)} %shard_map.186), channel_id=1, replica_groups=mesh['pair'=2,'core'=2,'tensor'=8] {'tensor'}, dimensions={0} | all-to-all | bytes 1179648 | tf_op jit(solution)/shard_map/all_to_all | solution.py:536
  110.5 0.3 shard_map.187
  110.8 17.2 %all_to_all.41 = bf16[8,64,512]{2,1,0:T(8,128)(2,1)S(1)} all-to-all(bf16[8,64,512]{2,1,0:T(8,128)(2,1)S(1)} %shard_map.187), channel_id=1, replica_groups=mesh['pair'=2,'core'=2,'tensor'=8] {'tensor'}, dimensions={0} | all-to-all | bytes 1048576 | tf_op jit(solution)/shard_map/all_to_all | solution.py:536
  128.0 1.3 shard_map.188
  129.4 13.2 %all_to_all.42 = bf16[16,32,256]{2,1,0:T(8,128)(2,1)S(1)} all-to-all(bf16[16,32,256]{2,1,0:T(8,128)(2,1)S(1)} %get-tuple-element.35), channel_id=1, replica_groups=mesh['pair'=2,'core'=2,'tensor'=8] {'pair','tensor'}, dimensions={0} | all-to-all | bytes 524288 | tf_op jit(solution)/shard_map/all_to_all | solution.py:536
  142.6 2.2 %all_gather.3 = bf16[2,2,8,32,256]{4,3,2,1,0:T(8,128)(2,1)S(1)} all-gather(bf16[1,2,8,32,256]{4,3,2,1,0:T(8,128)(2,1)S(1)} %bitcast.39), channel_id=1, replica_groups=mesh['pair'=2,'core'=2,'tensor'=8] {'core'}, dimensions={0}, use_global_device_ids=true | all-gather | bytes 786432 | tf_op jit(solution)/shard_map/all_gather | solution.py:701
  144.8 6.1 %shard_map.189 = bf16[4,8,24,256]{3,2,1,0:T(8,128)(2,1)S(1)} custom-call(bf16[96,128]{1,0:T(8,128)(2,1)S(1)} %add_convert_fusion.pick_ref, bf16[4,8,32,256]{3,2,1,0:T(8,128)(2,1)S(1)} %bitcast.33, bf16[1,2048]{1,0:T(2,128)(2,1)S(1)} %broadcast_in_dim.239.gain_ref, bf16[352,2048]{1,0:T(8,128)(2,1)S(1)} %copy-done.1, bf16[352,2048]{1,0:T(8,128)(2,1)S(1)} %copy-done.2, ...), custom_call_target="tpu_custom_call" | custom-call | flops 1660944384 | bytes 17301504 | tf_op jit(solution)/shard_map/pallas_call | solution.py:501
  151.0 15.7 %all_to_all.43 = bf16[32,24,256]{2,1,0:T(8,128)(2,1)S(1)} all-to-all(bf16[32,24,256]{2,1,0:T(8,128)(2,1)S(1)} %bitcast.35), channel_id=1, replica_groups=mesh['pair'=2,'core'=2,'tensor'=8] {'pair','core','tensor'}, dimensions={0} | all-to-all | bytes 786432 | tf_op jit(solution)/shard_map/all_to_all | solution.py:536
  166.7 0.9 shard_map.190
  (91 shorter events, 2.6 us)
Async XLA Ops:
  1.4 14.6 %all-to-all-start = ((bf16[8,32,256]{2,1,0:T(8,128)(2,1)}), bf16[8,32,256]{2,1,0:T(8,128)(2,1)S(1)}, u32[]{:S(2)}, u32[]{:S(2)}) async-start(bf16[8,32,256]{2,1,0:T(8,128)(2,1)} %broadcast_in_dim.213), calls=%async_computation | async-start | bytes 262144 | tf_op jit(solution)/shard_map/all_to_all | solution.py:536
  9.8 10.4 %copy-start.5 = (s32[32,6]{0,1:T(8,128)S(1)}, s32[32,6]{0,1:T(8,128)}, u32[]{:S(2)}) copy-start(s32[32,6]{0,1:T(8,128)} %param.30) | copy-start | bytes 2308
  9.8 10.5 %copy-start.7 = (f32[32,6]{0,1:T(8,128)S(1)}, f32[32,6]{0,1:T(8,128)}, u32[]{:S(2)}) copy-start(f32[32,6]{0,1:T(8,128)} %param.31) | copy-start | bytes 2308
  20.2 1.5 copy-start.8
  20.3 1.5 copy-start.9
  21.2 4.3 %copy-start.10 = (s32[32]{0:T(128)S(1)}, s32[32]{0:T(128)}, u32[]{:S(2)}) copy-start(s32[32]{0:T(128)} %param.28) | copy-start | bytes 388
  22.0 18.2 %all-to-all-start.1 = ((bf16[8,32,1152]{2,1,0:T(8,128)(2,1)}), bf16[8,32,1152]{2,1,0:T(8,128)(2,1)S(1)}, u32[]{:S(2)}, u32[]{:S(2)}) async-start(bf16[8,32,1152]{2,1,0:T(8,128)(2,1)} %shard_map.181), calls=%async_computation.1 | async-start | bytes 1179648 | tf_op jit(solution)/shard_map/all_to_all | solution.py:536
  41.7 4.0 %copy-start.6 = (bf16[2048]{0:T(1024)(128)(2,1)S(1)}, bf16[2048]{0:T(1024)(128)(2,1)}, u32[]{:S(2)}) copy-start(bf16[2048]{0:T(1024)(128)(2,1)} %param.29) | copy-start | bytes 12292
  41.7 19.7 %all-to-all-start.2 = ((bf16[4,16,9344]{2,1,0:T(8,128)(2,1)}), bf16[4,16,9344]{2,1,0:T(8,128)(2,1)S(1)}, u32[]{:S(2)}, u32[]{:S(2)}) async-start(bf16[4,16,9344]{2,1,0:T(8,128)(2,1)} %shard_map.182), calls=%async_computation.2 | async-start | bytes 2392064 | tf_op jit(solution)/shard_map/all_to_all | solution.py:536
  69.1 18.1 %all-to-all-start.3 = ((bf16[4,16,8320]{2,1,0:T(8,128)(2,1)}), bf16[4,16,8320]{2,1,0:T(8,128)(2,1)S(1)}, u32[]{:S(2)}, u32[]{:S(2)}) async-start(bf16[4,16,8320]{2,1,0:T(8,128)(2,1)} %shard_map.184), calls=%async_computation.3 | async-start | bytes 2129920 | tf_op jit(solution)/shard_map/all_to_all | solution.py:536
  90.4 54.4 %slice-start = ((s8[5767168]{0:T(1024)(128)(4,1)}), s8[4194304]{0:T(1024)(128)(4,1)S(1)}, s32[]{:S(2)}) async-start(s8[5767168]{0:T(1024)(128)(4,1)} %bitcast.25), calls=%async_computation.8 | async-start | bytes 8388608
  90.4 54.3 %slice-start.2 = ((s8[5767168]{0:T(1024)(128)(4,1)}), s8[4194304]{0:T(1024)(128)(4,1)S(1)}, s32[]{:S(2)}) async-start(s8[5767168]{0:T(1024)(128)(4,1)} %bitcast.27), calls=%async_computation.10 | async-start | bytes 8388608
  90.4 54.3 %slice-start.4 = ((s8[5767168]{0:T(1024)(128)(4,1)}), s8[4194304]{0:T(1024)(128)(4,1)S(1)}, s32[]{:S(2)}) async-start(s8[5767168]{0:T(1024)(128)(4,1)} %bitcast.29), calls=%async_computation.12 | async-start | bytes 8388608
  110.5 17.5 %copy-start = (bf16[256,8192]{1,0:T(8,128)(2,1)S(1)}, bf16[256,8192]{1,0:T(8,128)(2,1)}, u32[]{:S(2)}) copy-start(bf16[256,8192]{1,0:T(8,128)(2,1)} %weight_ref.1) | copy-start | bytes 12582916
  110.5 17.5 %copy-start.4 = (bf16[32,256]{1,0:T(8,128)(2,1)S(1)}, bf16[32,256]{1,0:T(8,128)(2,1)}, u32[]{:S(2)}) copy-start(bf16[32,256]{1,0:T(8,128)(2,1)} %hidden_ref.1) | copy-start | bytes 49156
  110.5 34.2 %slice-start.1 = ((s8[5767168]{0:T(1024)(128)(4,1)}), s8[1572864]{0:T(1024)(128)(4,1)S(1)}, s32[]{:S(2)}) async-start(s8[5767168]{0:T(1024)(128)(4,1)} %bitcast.25), calls=%async_computation.9 | async-start | bytes 3145728
  110.5 34.2 %slice-start.3 = ((s8[5767168]{0:T(1024)(128)(4,1)}), s8[1572864]{0:T(1024)(128)(4,1)S(1)}, s32[]{:S(2)}) async-start(s8[5767168]{0:T(1024)(128)(4,1)} %bitcast.27), calls=%async_computation.11 | async-start | bytes 3145728
  110.5 34.2 %slice-start.5 = ((s8[5767168]{0:T(1024)(128)(4,1)}), s8[1572864]{0:T(1024)(128)(4,1)S(1)}, s32[]{:S(2)}) async-start(s8[5767168]{0:T(1024)(128)(4,1)} %bitcast.29), calls=%async_computation.13 | async-start | bytes 3145728
  128.0 16.8 %copy-start.1 = (bf16[352,2048]{1,0:T(8,128)(2,1)S(1)}, bf16[352,2048]{1,0:T(8,128)(2,1)}, u32[]{:S(2)}) copy-start(bf16[352,2048]{1,0:T(8,128)(2,1)} %shared_gate_ref.1) | copy-start | bytes 4325380
  128.0 16.8 %copy-start.2 = (bf16[352,2048]{1,0:T(8,128)(2,1)S(1)}, bf16[352,2048]{1,0:T(8,128)(2,1)}, u32[]{:S(2)}) copy-start(bf16[352,2048]{1,0:T(8,128)(2,1)} %shared_up_ref.1) | copy-start | bytes 4325380
  128.0 16.8 %copy-start.3 = (bf16[352,2048]{1,0:T(8,128)(2,1)S(1)}, bf16[352,2048]{1,0:T(8,128)(2,1)}, u32[]{:S(2)}) copy-start(bf16[352,2048]{1,0:T(8,128)(2,1)} %shared_down_ref.1) | copy-start | bytes 4325380

commit v3 on v2

--- a/solution.py
+++ b/solution.py
@@ -2,6 +2,7 @@
 
 import jax
 import jax.numpy as jnp
+import numpy as np
 from jax import lax
 from jax.experimental import pallas as pl
 from jax.experimental.pallas import tpu as pltpu
@@ -17,6 +18,8 @@
 PAIR = 2 * KVW
 LANES = 128
 OWNER = ("pair", "core")
+SHARES = 2
+HEADS = H // SHARES
 MASS_ROWS = 8
 MIB = 1 << 20
 
@@ -111,165 +114,126 @@
     )(rows, gain, in_hbm(weight))
 
 
-def pick_body(pick_ref, extra_ref, rows_ref, out_ref):
-    owners, slots, _ = out_ref.shape
-    for k in range(PIECES):
-        picked = dot_nn(pick_ref[...], rows_ref[k]).astype(jnp.bfloat16)
-        for o in range(owners):
-            out_ref[o, :, k * PAIR : (k + 1) * PAIR] = picked[o * slots : (o + 1) * slots]
-    for o in range(owners):
-        out_ref[o, :, PIECES * PAIR :] = extra_ref[o]
-
-
-def pick_queries(pick, extra, rows, owners, slots):
-    return call(
-        pick_body,
-        jax.ShapeDtypeStruct((owners, slots, H * KVW + LANES), jnp.bfloat16),
+def pick_body(share, pick_ref, extra_ref, rows_ref, *out_refs):
+    slots = extra_ref.shape[1]
+    each = PIECES // SHARES
+    for k in range(each):
+        picked = dot_nn(pick_ref[...], rows_ref[share * each + k]).astype(jnp.bfloat16)
+        for o, out_ref in enumerate(out_refs):
+            out_ref[:, k * PAIR : (k + 1) * PAIR] = picked[o * slots : (o + 1) * slots]
+    for o, out_ref in enumerate(out_refs):
+        out_ref[:, each * PAIR :] = extra_ref[o]
+
+
+def pick_queries(share, pick, extra, rows):
+    owners, slots, _ = extra.shape
+    return call(
+        functools.partial(pick_body, share),
+        (jax.ShapeDtypeStruct((slots, HEADS * KVW + LANES), jnp.bfloat16),) * owners,
         16,
-        2 * owners * slots * rows.shape[1] * H * KVW,
-        4 * owners * slots * H * KVW,
+        2 * owners * slots * rows.shape[1] * HEADS * KVW,
+        4 * owners * slots * HEADS * KVW,
     )(pick, extra, rows)
 
 
-def running_softmax(scores, value_dot, at, m_ref, l_ref, acc_ref):
-    before = m_ref[at, :]
-    peak = jnp.maximum(before, jnp.max(scores, axis=-1, keepdims=True))
-    weights = jnp.exp2(scores - peak)
-    shrink = jnp.exp2(before - peak)
-    l_ref[at, :] = l_ref[at, :] * shrink + jnp.sum(weights, axis=-1, keepdims=True)
-    acc_ref[at, :] = acc_ref[at, :] * shrink + value_dot(weights.astype(jnp.bfloat16))
-    m_ref[at, :] = peak
-
-
-def finish(out_ref, m_ref, l_ref, acc_ref):
-    total = l_ref[...]
-    out_ref[:, :LAT] = acc_ref[...] / total
-    out_ref[:, LAT:] = jnp.broadcast_to(
-        m_ref[...] * ln2 + jnp.log(total), (total.shape[0], LANES)
-    )
-
-
-def by_head(rows_ref, q_ref):
+def sums(scores, usable=None):
+    if usable is not None:
+        scores = [jnp.where(u, x, lowest) for u, x in zip(usable, scores)]
+    peak = functools.reduce(
+        jnp.maximum, [jnp.max(x, axis=-1, keepdims=True) for x in scores]
+    )
+    weights = [jnp.exp2(x - peak) for x in scores]
+    if usable is not None:
+        weights = [jnp.where(u, w, 0.0) for u, w in zip(usable, weights)]
+    total = functools.reduce(jnp.add, [jnp.sum(w, axis=-1, keepdims=True) for w in weights])
+    return peak, [w.astype(jnp.bfloat16) for w in weights], total
+
+
+def own_body(share, rows_ref, holder_ref, root_hbm, suffix_hbm, out_hbm, out_ref, q_ref, root_ref, suffix_ref, s_ref, root_sems, suffix_sems, out_sem):
     requests = rows_ref.shape[1]
-    for k in range(PIECES):
-        for j in range(2):
-            at = (2 * k + j) * requests
-            q_ref[at : at + requests, :] = rows_ref[k, :, j * KVW : (j + 1) * KVW]
-
-
-def halves_of(count):
-    return [slice(0, count // 2), slice(count // 2, count)]
-
-
-def attention_scratch(count):
-    return [
-        pltpu.VMEM((count, KVW), jnp.bfloat16),
-        pltpu.VMEM((count, 1), jnp.float32),
-        pltpu.VMEM((count, 1), jnp.float32),
-        pltpu.VMEM((count, LAT), jnp.float32),
+    blocks, _, block = root_ref.shape
+    groups, span, _ = suffix_ref.shape
+    each = requests // groups
+    root_copies = [
+        pltpu.make_async_copy(
+            root_hbm.at[:, pl.ds(b * block, block)], root_ref.at[b], root_sems.at[b]
+        )
+        for b in range(blocks)
     ]
-
-
-def root_body(rows_ref, cache_ref, out_ref, q_ref, m_ref, l_ref, acc_ref):
-    step = pl.program_id(0)
-
-    @pl.when(step == 0)
-    def _():
-        by_head(rows_ref, q_ref)
-        m_ref[...] = jnp.full(m_ref.shape, lowest, jnp.float32)
-        l_ref[...] = jnp.zeros(l_ref.shape, jnp.float32)
-        acc_ref[...] = jnp.zeros(acc_ref.shape, jnp.float32)
-
-    halves = halves_of(q_ref.shape[0])
-    scores = [dot_nn(q_ref[at, :], cache_ref[...]) * (score_scale * log2e) for at in halves]
-    for at, block in zip(halves, scores):
-        running_softmax(
-            block, lambda w: dot_nt(w, cache_ref[:LAT, :]), at, m_ref, l_ref, acc_ref
-        )
-
-    @pl.when(step == pl.num_programs(0) - 1)
-    def _():
-        finish(out_ref, m_ref, l_ref, acc_ref)
-
-
-def root_attention(rows, cache):
-    count = H * rows.shape[1]
-    positions = cache.shape[1]
+    suffix_copies = [
+        pltpu.make_async_copy(
+            suffix_hbm.at[pl.ds(g * span, span)], suffix_ref.at[g], suffix_sems.at[g]
+        )
+        for g in range(groups)
+    ]
+    for copy in root_copies + suffix_copies:
+        copy.start()
+    for h in range(HEADS):
+        k, j = divmod(share * HEADS + h, 2)
+        q_ref[h * requests : (h + 1) * requests, :] = rows_ref[k, :, j * KVW : (j + 1) * KVW]
+    scale = score_scale * log2e
+    peaks = []
+    for b in range(blocks):
+        root_copies[b].wait()
+        s_ref[b] = dot_nn(q_ref[...], root_ref[b]) * scale
+    root_peak, weights, root_total = sums([s_ref[b] for b in range(blocks)])
+    root_out = functools.reduce(
+        jnp.add, [dot_nt(weights[b], root_ref[b, :LAT, :]) for b in range(blocks)]
+    )
+    for g in range(groups):
+        suffix_copies[g].wait()
+        mine = [slice(h * requests + g * each, h * requests + (g + 1) * each) for h in range(HEADS)]
+        scores = dot_nt(
+            jnp.concatenate([q_ref[at, :] for at in mine], axis=0), suffix_ref[g]
+        )
+        request = lax.broadcasted_iota(jnp.int32, (HEADS * each, 1), 0) % each + g * each
+        usable = holder_ref[:, g * span : (g + 1) * span] == request
+        peak, weights, total = sums([scores * scale], [usable])
+        out = dot_nn(weights[0], suffix_ref[g, :, :LAT])
+        for h, at in enumerate(mine):
+            own = slice(h * each, (h + 1) * each)
+            top = jnp.maximum(root_peak[at], peak[own])
+            root_scale = jnp.exp2(root_peak[at] - top)
+            scaled = jnp.exp2(peak[own] - top)
+            both = root_total[at] * root_scale + total[own] * scaled
+            out_ref[at, :LAT] = (root_out[at] * root_scale + out[own] * scaled) / both
+            out_ref[at, LAT:] = jnp.broadcast_to(top * ln2 + jnp.log(both), (each, LANES))
+    copy = pltpu.make_async_copy(out_ref, out_hbm, out_sem)
+    copy.start()
+    copy.wait()
+
+
+def own_attention(share, rows, holder, root, suffix):
+    count = HEADS * rows.shape[1]
+    positions = root.shape[1]
     block = min(1024, positions)
-    return call(
-        root_body,
+    blocks, groups = positions // block, 2
+    span = suffix.shape[0] // groups
+    return call(
+        functools.partial(own_body, share),
         pltpu.HBM((count, LAT + LANES), jnp.float32),
-        32,
-        2 * count * positions * (KVW + LAT),
-        2 * KVW * positions,
-        grid=(positions // block,),
-        in_specs=[whole(rows.shape), pl.BlockSpec((KVW, block), lambda i: (0, i))],
-        out_specs=whole((count, LAT + LANES)),
-        scratch_shapes=attention_scratch(count),
-    )(rows, in_hbm(cache))
-
-
-def suffix_body(rows_ref, cache_ref, holder_ref, first_ref, out_ref, q_ref):
-    requests = rows_ref.shape[1]
-    each = q_ref.shape[1] // H
-    group = pl.program_id(0)
-    for k in range(PIECES):
-        for j in range(2):
-            h = 2 * k + j
-            q_ref[0, h * each : (h + 1) * each, :] = rows_ref[
-                k, pl.ds(pl.multiple_of(group * each, each), each), j * KVW : (j + 1) * KVW
-            ]
-    scores = dot_nt(q_ref[0], cache_ref[...]) * (score_scale * log2e)
-    request = lax.broadcasted_iota(jnp.int32, (H * each, 1), 0) % each + group * each
-    usable = holder_ref[...] == request
-    scores = jnp.where(usable, scores, lowest)
-    first = jnp.concatenate(
-        [
-            first_ref[pl.ds(pl.multiple_of(h * requests + group * each, each), each), :]
-            for h in range(H)
+        44,
+        2 * count * (positions + span) * (KVW + LAT),
+        2 * KVW * (positions + suffix.shape[0]),
+        in_specs=[VMEM, VMEM, HBM, HBM],
+        out_specs=HBM,
+        scratch_shapes=[
+            pltpu.VMEM((count, LAT + LANES), jnp.float32),
+            pltpu.VMEM((count, KVW), jnp.bfloat16),
+            pltpu.VMEM((blocks, KVW, block), jnp.bfloat16),
+            pltpu.VMEM((groups, span, KVW), jnp.bfloat16),
+            pltpu.VMEM((blocks, count, block), jnp.float32),
+            pltpu.SemaphoreType.DMA((blocks,)),
+            pltpu.SemaphoreType.DMA((groups,)),
+            pltpu.SemaphoreType.DMA,
         ],
-        axis=0,
-    )
-    mass = first[:, LAT : LAT + 1] * log2e
-    peak = jnp.maximum(mass, jnp.max(scores, axis=-1, keepdims=True))
-    weights = jnp.exp2(scores - peak)
-    shrink = jnp.exp2(mass - peak)
-    total = shrink + jnp.sum(weights, axis=-1, keepdims=True)
-    out = first[:, :LAT] * shrink + dot_nn(weights.astype(jnp.bfloat16), cache_ref[:, :LAT])
-    out = out / total
-    mass = jnp.broadcast_to(peak * ln2 + jnp.log(total), (H * each, LANES))
-    for h in range(H):
-        at = pl.ds(pl.multiple_of(h * requests + group * each, each), each)
-        out_ref[at, :LAT] = out[h * each : (h + 1) * each]
-        out_ref[at, LAT:] = mass[h * each : (h + 1) * each]
-
-
-def suffix_attention(rows, cache, holder, first):
-    requests = rows.shape[1]
-    count = H * requests
-    positions = cache.shape[0]
-    groups = 2
-    block = positions // groups
-    return call(
-        suffix_body,
-        pltpu.HBM((count, LAT + LANES), jnp.float32),
-        32,
-        2 * count * block * (KVW + LAT),
-        2 * KVW * positions,
-        grid=(groups,),
-        in_specs=[
-            whole(rows.shape),
-            pl.BlockSpec((block, KVW), lambda i: (i, 0)),
-            pl.BlockSpec((1, block), lambda i: (0, i)),
-            whole((count, LAT + LANES)),
-        ],
-        out_specs=whole((count, LAT + LANES)),
-        scratch_shapes=[pltpu.VMEM((1, count // groups, KVW), jnp.bfloat16)],
-    )(rows, in_hbm(cache), holder, in_hbm(first))
-
-
-def group_body(rows_ref, cache_hbm, holder_ref, out_hbm, q_ref, keys_ref, out_ref, sems, out_sems):
-    owners, slots, _ = rows_ref.shape
+    )(rows, holder, in_hbm(root), in_hbm(suffix))
+
+
+def group_body(owners, cache_hbm, holder_ref, *refs):
+    rows_refs, out_refs = refs[:owners], refs[owners : 2 * owners]
+    q_ref, keys_ref, sems = refs[2 * owners :]
+    slots = rows_refs[0].shape[0]
     groups, _, span = cache_hbm.shape
     copies = [
         pltpu.make_async_copy(
@@ -279,19 +243,32 @@
     ]
     for copy in copies:
         copy.start()
+    each = HEADS * slots
     for o in range(owners):
-        for h in range(H):
-            q_ref[o, h * slots : (h + 1) * slots, :] = rows_ref[o, :, h * KVW : (h + 1) * KVW]
-    for copy in copies:
-        copy.wait()
+        for h in range(HEADS):
+            at = o * each + h * slots
+            q_ref[at : at + slots, :] = rows_refs[o][:, h * KVW : (h + 1) * KVW]
     lane = lax.broadcasted_iota(jnp.int32, (slots, LANES), 1)
-    scores = [dot_nn(q_ref[o], keys_ref[...]) for o in range(owners)]
-    sent = []
-    for o in range(owners):
-        asked = rows_ref[o, :, H * KVW :][:, :1].astype(jnp.float32)
-        asked = jnp.concatenate([asked] * H, axis=0)
+    both = 2 * each
+    blocks = 3 if groups % 3 == 0 else 1
+    scores = [[] for _ in range(owners // 2)]
+    for b in range(blocks):
+        for copy in copies[b * groups // blocks : (b + 1) * groups // blocks]:
+            copy.wait()
+        at = slice(b * groups * span // blocks, (b + 1) * groups * span // blocks)
+        for pair in range(owners // 2):
+            scores[pair].append(
+                dot_nn(q_ref[pair * both : (pair + 1) * both, :], keys_ref[:, at])
+            )
+    for pair in range(owners // 2):
+        asked = [
+            rows_refs[o][:, HEADS * KVW :][:, :1].astype(jnp.float32)
+            for o in (2 * pair, 2 * pair + 1)
+        ]
+        asked = jnp.concatenate([asked[0]] * HEADS + [asked[1]] * HEADS, axis=0)
         usable = holder_ref[...] == asked
-        block = jnp.where(usable, scores[o] * (score_scale * log2e), lowest)
+        block = jnp.concatenate(scores[pair], axis=1) * (score_scale * log2e)
+        block = jnp.where(usable, block, lowest)
         peak = jnp.max(block, axis=-1, keepdims=True)
         weights = jnp.where(usable, jnp.exp2(block - peak), 0.0)
         total = jnp.sum(weights, axis=-1, keepdims=True)
@@ -299,68 +276,78 @@
         safe = jnp.where(present, total, 1.0)
         block_out = dot_nt(weights.astype(jnp.bfloat16), keys_ref[:LAT, :]) / safe
         mass = jnp.where(present, peak * ln2 + jnp.log(safe), lowest)
-        extra = jnp.zeros((slots, LANES), jnp.float32)
-        for h in range(H):
-            at = slice(h * slots, (h + 1) * slots)
-            out_ref[o, :, h * LAT : (h + 1) * LAT] = block_out[at].astype(jnp.bfloat16)
-            for k, part in enumerate(split_three(mass[at])):
-                extra = jnp.where(lane == k * H + h, part, extra)
-        out_ref[o, :, H * LAT :] = extra.astype(jnp.bfloat16)
-        copy = pltpu.make_async_copy(out_ref.at[o], out_hbm.at[o], out_sems.at[o])
+        for o in (2 * pair, 2 * pair + 1):
+            out_ref = out_refs[o]
+            extra = jnp.zeros((slots, LANES), jnp.float32)
+            for h in range(HEADS):
+                at = (o - 2 * pair) * each + h * slots
+                at = slice(at, at + slots)
+                out_ref[:, h * LAT : (h + 1) * LAT] = block_out[at].astype(jnp.bfloat16)
+                for k, part in enumerate(split_three(mass[at])):
+                    extra = jnp.where(lane == k * HEADS + h, part, extra)
+            out_ref[:, HEADS * LAT :] = extra.astype(jnp.bfloat16)
+
+
+def group_attention(rows, cache, holder):
+    owners, slots = len(rows), rows[0].shape[0]
+    groups, _, span = cache.shape
+    out = jax.ShapeDtypeStruct((slots, HEADS * LAT + LANES), jnp.bfloat16)
+    return call(
+        functools.partial(group_body, owners),
+        (out,) * owners,
+        40,
+        2 * owners * slots * HEADS * groups * span * (KVW + LAT),
+        2 * KVW * groups * span,
+        in_specs=[HBM, VMEM] + [VMEM] * owners,
+        out_specs=(VMEM,) * owners,
+        scratch_shapes=[
+            pltpu.VMEM((owners * HEADS * slots, KVW), jnp.bfloat16),
+            pltpu.VMEM((KVW, groups * span), jnp.bfloat16),
+            pltpu.SemaphoreType.DMA((groups,)),
+        ],
+    )(in_hbm(cache), holder, *rows)
+
+
+def local_body(unpick_ref, *refs):
+    first_hbm, back_refs = refs[:SHARES], refs[SHARES:-4]
+    out_ref, first_ref, out_mass_ref, sems = refs[-4:]
+    copies = [
+        pltpu.make_async_copy(first_hbm[k], first_ref.at[k], sems.at[k]) for k in range(SHARES)
+    ]
+    for copy in copies:
         copy.start()
-        sent.append(copy)
-    for copy in sent:
-        copy.wait()
-
-
-def group_attention(rows, cache, holder):
-    owners, slots, _ = rows.shape
-    groups, _, span = cache.shape
-    width = H * LAT + LANES
-    return call(
-        group_body,
-        pltpu.HBM((owners, slots, width), jnp.bfloat16),
-        40,
-        2 * owners * slots * H * groups * span * (KVW + LAT),
-        2 * KVW * groups * span,
-        in_specs=[VMEM, HBM, VMEM],
-        out_specs=HBM,
-        scratch_shapes=[
-            pltpu.VMEM((owners, H * slots, KVW), jnp.bfloat16),
-            pltpu.VMEM((KVW, groups * span), jnp.bfloat16),
-            pltpu.VMEM((owners, slots, width), jnp.bfloat16),
-            pltpu.SemaphoreType.DMA((groups,)),
-            pltpu.SemaphoreType.DMA((owners,)),
-        ],
-    )(rows, in_hbm(cache), holder)
-
-
-def local_body(unpick_ref, back_ref, first_hbm, out_ref, first_ref, out_mass_ref, sem):
-    copy = pltpu.make_async_copy(first_hbm, first_ref, sem)
-    copy.start()
+    owners = len(back_refs) // SHARES
     requests = unpick_ref.shape[0]
     unpick = unpick_ref[...]
-    extra = dot_nn(unpick, back_ref[:, H * LAT :])
+
+    def returned(share, at):
+        rows = [ref[:, at] for ref in back_refs[share * owners : (share + 1) * owners]]
+        return dot_nn(unpick, jnp.concatenate(rows, axis=0))
+
+    extras = [returned(share, slice(HEADS * LAT, None)) for share in range(SHARES)]
     shares, length = out_ref.shape[0], out_ref.shape[1] - MASS_ROWS
-    copy.wait()
     for h in range(H):
-        at = slice(h * requests, (h + 1) * requests)
-        group_out = dot_nn(unpick, back_ref[:, h * LAT : (h + 1) * LAT])
-        group_mass = (
-            extra[:, h : h + 1] + extra[:, H + h : H + h + 1] + extra[:, 2 * H + h : 2 * H + h + 1]
-        )
-        first_mass = first_ref[at, LAT : LAT + 1]
+        share, head = divmod(h, HEADS)
+        if head == 0:
+            copies[share].wait()
+        at = slice(head * requests, (head + 1) * requests)
+        group_out = returned(share, slice(head * LAT, (head + 1) * LAT))
+        group_mass = functools.reduce(
+            jnp.add,
+            [extras[share][:, k * HEADS + head : k * HEADS + head + 1] for k in range(3)],
+        )
+        first_mass = first_ref[share, at, LAT : LAT + 1]
         peak = jnp.maximum(first_mass, group_mass)
         first_weight = jnp.exp(first_mass - peak)
         group_weight = jnp.exp(group_mass - peak)
         total = first_weight + group_weight
-        out = (first_weight * first_ref[at, :LAT] + group_weight * group_out) / total
+        out = (first_weight * first_ref[share, at, :LAT] + group_weight * group_out) / total
         out = out.astype(jnp.bfloat16)
         each = min(length, requests)
         for k in range(requests // each):
-            share, row = divmod(h * requests + k * each, length)
-            out_ref[share, row : row + each, :] = out[k * each : (k + 1) * each]
-        out_mass_ref[at, :] = peak + jnp.log(total)
+            target, row = divmod(h * requests + k * each, length)
+            out_ref[target, row : row + each, :] = out[k * each : (k + 1) * each]
+        out_mass_ref[h * requests : (h + 1) * requests, :] = peak + jnp.log(total)
     diagonal = lax.broadcasted_iota(jnp.int32, (length, LAT), 0) == lax.broadcasted_iota(
         jnp.int32, (length, LAT), 1
     )
@@ -374,22 +361,22 @@
         out_ref[share, length:, :] = tail.astype(jnp.bfloat16)
 
 
-def local_join(unpick, back, first, shares):
-    count = first.shape[0]
+def local_join(unpick, first, back, shares):
+    count = SHARES * first[0].shape[0]
     return call(
         local_body,
         jax.ShapeDtypeStruct((shares, count // shares + MASS_ROWS, LAT), jnp.bfloat16),
         10,
-        2 * unpick.shape[0] * back.shape[0] * back.shape[1],
+        2 * unpick.shape[0] * unpick.shape[1] * H * LAT,
         4 * count * LAT,
-        in_specs=[VMEM, VMEM, HBM],
+        in_specs=[VMEM] + [HBM] * SHARES + [VMEM] * len(back),
         out_specs=VMEM,
         scratch_shapes=[
-            pltpu.VMEM(first.shape, jnp.float32),
+            pltpu.VMEM((SHARES,) + first[0].shape, jnp.float32),
             pltpu.VMEM((count, 1), jnp.float32),
-            pltpu.SemaphoreType.DMA,
+            pltpu.SemaphoreType.DMA((SHARES,)),
         ],
-    )(unpick, back, in_hbm(first))
+    )(unpick, *[in_hbm(x) for x in first], *back)
 
 
 def join_body(parts_ref, out_ref):
@@ -534,6 +521,14 @@
 
 def exchange(x, axis):
     return lax.all_to_all(x, axis, 0, 0, tiled=True)
+
+
+def swap_owners(arrays):
+    count = len(arrays)
+    out = {0: arrays[0]}
+    for k in reversed(range(1, count)):
+        out[k] = lax.ppermute(arrays[k], OWNER, [(i, i ^ k) for i in range(count)])
+    return [out[k] for k in range(count)]
 
 
 def gather_pieces(x):
@@ -586,6 +581,7 @@
     owner_index, tensor_index = lax.axis_index(OWNER), lax.axis_index("tensor")
     requests = hidden.shape[0]
     fanout = routes.shape[1]
+    token_share = requests // owners
     pairs = owners // 2
     split = tensors // EXP_OWN
     slots = -(-2 * requests // (owners * 16)) * 16
@@ -607,7 +603,7 @@
     )
     destination = group_of // GROUP_OWN
     owner_range = jnp.arange(owners)
-    to_owner = destination[:, None] == owner_range[None, :]
+    to_owner = (destination ^ owner_index)[:, None] == owner_range[None, :]
     slot_rank = ranks(to_owner)
     placed = to_owner[:, :, None] & (slot_rank[:, :, None] == jnp.arange(slots))
     unpick = placed.reshape(requests, owners * slots).astype(jnp.bfloat16)
@@ -634,37 +630,18 @@
         .reshape(1, -1)
         .astype(jnp.float32)
     )
-    experts = jnp.arange(owners * EXP_OWN)
-    hits = routes[:, :, None] == experts[None, None, :]
-    share = jnp.sum(jnp.where(hits, route_weight[:, :, None], 0.0), axis=1)
-    hit = jnp.any(hits, axis=1)
-    taken = hit[:, :, None] & (ranks(hit)[:, :, None] == jnp.arange(expert_slots))
-    back_weight = jnp.where(taken, share[:, :, None], 0.0)
-    back_weight = jnp.repeat(back_weight, split, axis=1)
-    token_share = requests // owners
-    shared_token = owner_range[:, None] * token_share + jnp.arange(token_share)
-    shared_weight = shared_token.reshape(-1)[None, :] == jnp.arange(requests)[:, None]
-    shared_weight = jnp.broadcast_to(
-        shared_weight.reshape(requests, owners, 1, token_share).astype(jnp.float32),
-        (requests, owners, tensors, token_share),
-    ).reshape(requests, owners * tensors, token_share)
-    back_weight = jnp.concatenate([back_weight, shared_weight], axis=2).reshape(requests, -1)
-
-    queries, back_weight, suffix_holder, group_holder = lax.optimization_barrier(
-        (exchange(projected, "tensor"), back_weight, suffix_holder, group_holder)
-    )
-    queries = gather_pieces(queries)
-    arrived = exchange(pick_queries(pick, extra, queries, owners, slots), OWNER)
-    if group_span % LANES:
-        group_columns = group_cache.reshape(-1, KVW).T[None]
-    else:
-        group_columns = jnp.swapaxes(group_cache, 1, 2)
-    first = root_attention(queries, root_cache.T)
-    arrived, first = lax.optimization_barrier((arrived, first))
-    all_routes = (
-        arrived[:, :, H * KVW + 1 : H * KVW + 1 + named.shape[1]]
-        .reshape(owners, requests, fanout)
-        .astype(jnp.int32)
+    queries = gather_pieces(exchange(projected, "tensor"))
+    arrived, asking = [], queries
+    for share in range(SHARES):
+        sent = pick_queries(share, pick, extra, asking)
+        asking, sent = lax.optimization_barrier((queries, sent))
+        arrived.append(swap_owners(sent))
+    all_routes = jnp.stack(
+        [x[:, HEADS * KVW + 1 : HEADS * KVW + 1 + named.shape[1]] for x in arrived[0]]
+    ).reshape(1, owners, requests, fanout)
+    turned = owner_range[:, None] ^ owner_index == owner_range[None, :]
+    all_routes = jnp.sum(
+        jnp.where(turned[:, :, None, None], all_routes.astype(jnp.int32), 0), axis=1
     )
     mine = owner_index * EXP_OWN + tensor_index // split
     called = jnp.any(all_routes == mine, axis=2)
@@ -687,11 +664,20 @@
     expert_pick = jnp.concatenate(
         [expert_pick.reshape(owners * expert_slots, owners * requests), shared_pick], axis=0
     ).astype(jnp.bfloat16)
-    answered = group_attention(arrived, group_columns, group_holder)
-    back = exchange(answered, OWNER)
-    first = suffix_attention(queries, suffix_cache.reshape(-1, KVW), suffix_holder, first)
-    back, expert_pick, gain = lax.optimization_barrier((back, expert_pick, mixture_gain[None]))
-    parts = local_join(unpick, back.reshape(owners * slots, -1), first, tensors)
+    root_columns, suffix_rows = root_cache.T, suffix_cache.reshape(-1, KVW)
+    first, back, own = [], [], queries
+    for share in range(SHARES):
+        first.append(own_attention(share, own, suffix_holder, root_columns, suffix_rows))
+        if share == 0:
+            before = first[0]
+            for k in range(SHARES):
+                waited, before = lax.optimization_barrier((arrived[k], before))
+                answered = group_attention(waited, group_columns, group_holder)
+                before = answered[0]
+                back.append(swap_owners(answered))
+            own, before, expert_pick = lax.optimization_barrier((own, before, expert_pick))
+    back, gain = lax.optimization_barrier((back, mixture_gain[None]))
+    parts = local_join(unpick, first, sum(back, []), tensors)
     attention = exchange(join(exchange(parts, "tensor")), "tensor")
     mid, copies = output_projection(
         attention.reshape(-1, LAT), out_weight, hidden, owners // 2 * tensors
@@ -708,8 +694,21 @@
         (shared_gate, shared_up, shared_down),
         (expert_gate, expert_up, expert_down),
     )
+    results, routes, route_weight = lax.optimization_barrier((results, routes, route_weight))
     results = scatter_pieces(results, tensors).reshape((owners * tensors, -1, mid.shape[1]))
     returned = exchange(results, ("pair", "core", "tensor"))
+    experts = jnp.arange(owners * EXP_OWN)
+    hits = routes[:, :, None] == experts[None, None, :]
+    share = jnp.sum(jnp.where(hits, route_weight[:, :, None], 0.0), axis=1)
+    hit = jnp.any(hits, axis=1)
+    taken = hit[:, :, None] & (ranks(hit)[:, :, None] == jnp.arange(expert_slots))
+    back_weight = jnp.where(taken, share[:, :, None], 0.0)
+    back_weight = jnp.repeat(back_weight, split, axis=1)
+    shared_weight = np.eye(requests, dtype=np.float32).reshape(requests, owners, 1, token_share)
+    shared_weight = np.repeat(shared_weight, tensors, axis=2).reshape(
+        requests, owners * tensors, token_share
+    )
+    back_weight = jnp.concatenate([back_weight, shared_weight], axis=2).reshape(requests, -1)
     return final_sum(returned.reshape(-1, mid.shape[1]), back_weight, mid)
 
 

time: 168 us -> 160 us (0.952)
  blocking collectives: 68.3 us -> 54.5 us
  starting transfers between devices: 18.2 us -> 21.2 us
  Pallas kernels: 40.3 us -> 42.1 us
    all_to_all x4 -> x3, blocking collectives: 66.2 us -> 52.4 us  [exchange(): return lax.all_to_all(x, axis, 0, 0, tiled=True)]
    ppermute x0 -> x12, starting transfers between devices: none -> 7.85 us  [swap_owners(): out[k] = lax.ppermute(arrays[k], OWNER, [(i, i ^ k) for i in range(count)])]
    all_to_all x4 -> x3, starting transfers between devices: 18.2 us -> 13.4 us  [exchange(): return lax.all_to_all(x, axis, 0, 0, tiled=True)]
    all_to_all x4 -> x3, waiting for transfers between devices: 34 us -> 30.7 us  [exchange(): return lax.all_to_all(x, axis, 0, 0, tiled=True)]
    ppermute x0 -> x12, waiting for transfers between devices: none -> 2.15 us  [swap_owners(): out[k] = lax.ppermute(arrays[k], OWNER, [(i, i ^ k) for i in range(count)])]
    pallas_call x4 -> x6, Pallas kernels: 24.3 us -> 26.4 us  [the longest x2 16.7 us: own_attention(): call(functools.partial(own_body, share), pltpu.HBM((count, LAT + LANES),...]
  transfers between devices with their start and end apart: 4 -> 15, of which waited for: 4 -> 6; matrix products, arithmetic and copies ran while one was open for 2% -> 4% of each run, Pallas kernels for 9% -> 14%
where the time goes in v3:
time: 160 us; the launch traced here: 159 us
  blocking collectives  54.5 us (34%)
  Pallas kernels  42.1 us (26%)
  waiting for transfers between devices  32.8 us (20%)
  starting transfers between devices  21.2 us (13%)
  local copies, waits for them, and re-layouts  5.43 us (3%)
  other arithmetic  2.41 us (2%)
    all_to_all x3, blocking collectives, exchange(): return lax.all_to_all(x, axis, 0, 0, tiled=True)  52.4 us
    all_to_all x3, waiting for transfers between devices, exchange(): return lax.all_to_all(x, axis, 0, 0, tiled=True)  30.7 us
    pallas_call x2, Pallas kernels, own_attention(): call(functools.partial(own_body, share), pltpu.HBM((count, LAT + LANES),...  16.7 us
    all_to_all x3, starting transfers between devices, exchange(): return lax.all_to_all(x, axis, 0, 0, tiled=True)  13.4 us
    pallas_call x2, Pallas kernels, group_attention(): call(functools.partial(group_body, owners), (out,) * owners, 40, 2 * owne...  9.1 us
    ppermute x12, starting transfers between devices, swap_owners(): out[k] = lax.ppermute(arrays[k], OWNER, [(i, i ^ k) for i in range(count)])  7.85 us
    pallas_call x1, Pallas kernels, expert(): call(expert_body, jax.ShapeDtypeStruct((owners, PIECES, slots + requests...  6.85 us
    pallas_call x1, Pallas kernels, project(): call(project_body, jax.ShapeDtypeStruct((copies, requests, columns), jnp....  4.25 us
  transfers between devices with their start and end apart: 15, of which 6 were waited for; matrix products, arithmetic and copies ran while one was open for 4% of the time, Pallas kernels for 14%

profile of v3, /device:TPU:0, one launch (start us, length us, event | category | flops | bytes accessed | tf_op | source)
XLA Modules:
  0.0 159.1 jit_solution(18263313473923963779)
XLA Ops:
  0.0 1.4 broadcast_in_dim.228
  1.4 7.2 %all-to-all-start = ((bf16[8,32,256]{2,1,0:T(8,128)(2,1)}), bf16[8,32,256]{2,1,0:T(8,128)(2,1)S(1)}, u32[]{:S(2)}, u32[]{:S(2)}) async-start(bf16[8,32,256]{2,1,0:T(8,128)(2,1)} %broadcast_in_dim.228), calls=%async_computation | async-start | bytes 262144 | tf_op jit(solution)/shard_map/all_to_all | solution.py:523
  9.4 0.7 broadcast_in_dim.229.gain_ref
  10.1 0.7 broadcast_in_dim.249.gain_ref
  10.9 5.1 %all-to-all-done.rows_ref = bf16[8,32,256]{2,1,0:T(8,128)(2,1)S(1)} async-done(((bf16[8,32,256]{2,1,0:T(8,128)(2,1)}), bf16[8,32,256]{2,1,0:T(8,128)(2,1)S(1)}, u32[]{:S(2)}, u32[]{:S(2)}) %all-to-all-start) | async-done | bytes 131104 | tf_op jit(solution)/shard_map/all_to_all | solution.py:523
  16.0 4.3 %shard_map.190 = bf16[8,32,1152]{2,1,0:T(8,128)(2,1)} custom-call(bf16[8,32,256]{2,1,0:T(8,128)(2,1)S(1)} %all-to-all-done.rows_ref, bf16[1,2048]{1,0:T(2,128)(2,1)S(1)} %broadcast_in_dim.229.gain_ref, bf16[1152,2048]{1,0:T(8,128)(2,1)} %weight_hbm.1), custom_call_target="tpu_custom_call" | custom-call | flops 150994944 | bytes 4718592 | tf_op jit(solution)/shard_map/pallas_call | solution.py:102
  20.3 3.5 %all-to-all-start.1 = ((bf16[8,32,1152]{2,1,0:T(8,128)(2,1)}), bf16[8,32,1152]{2,1,0:T(8,128)(2,1)S(1)}, u32[]{:S(2)}, u32[]{:S(2)}) async-start(bf16[8,32,1152]{2,1,0:T(8,128)(2,1)} %shard_map.190), calls=%async_computation.1 | async-start | bytes 1179648 | tf_op jit(solution)/shard_map/all_to_all | solution.py:523
  25.1 13.5 %all-to-all-done.1.rows_ref = bf16[8,32,1152]{2,1,0:T(8,128)(2,1)S(1)} async-done(((bf16[8,32,1152]{2,1,0:T(8,128)(2,1)}), bf16[8,32,1152]{2,1,0:T(8,128)(2,1)S(1)}, u32[]{:S(2)}, u32[]{:S(2)}) %all-to-all-start.1) | async-done | bytes 589856 | tf_op jit(solution)/shard_map/all_to_all | solution.py:523
  39.1 1.6 collective-permute-start.4
  40.7 0.3 collective-permute-start.5
  41.3 0.4 collective-permute-start
  41.7 1.5 collective-permute-start.1
  43.2 8.2 %shard_map.193.refs_0_ = f32[256,640]{1,0:T(8,128)} custom-call(bf16[8,32,1152]{2,1,0:T(8,128)(2,1)S(1)} %all-to-all-done.1.rows_ref, s32[1,2048]{1,0:T(1,128)S(1)} %select_n.120.holder_ref, bf16[576,4096]{1,0:T(8,128)(2,1)} %bitcast.38, bf16[2048,576]{1,0:T(8,128)(2,1)} %bitcast.40), custom_call_target="tpu_custom_call" | custom-call | flops 2852126720 | bytes 7077888 | tf_op jit(solution)/shard_map/pallas_call | solution.py:212
  52.7 4.6 %shard_map.194 = (bf16[16,4224]{1,0:T(8,128)(2,1)S(1)}, bf16[16,4224]{1,0:T(8,128)(2,1)S(1)}, bf16[16,4224]{1,0:T(8,128)(2,1)S(1)}, bf16[16,4224]{1,0:T(8,128)(2,1)S(1)}) custom-call(bf16[12,576,128]{2,1,0:T(8,128)(2,1)} %bitcast.42, f32[1,1536]{1,0:T(1,128)S(1)} %bitcast.32, bf16[16,4736]{1,0:T(8,128)(2,1)S(1)} %get-tuple-element.82.refs_0_, ...), custom_call_target="tpu_custom_call" | custom-call | flops 1711276032 | bytes 1769472 | tf_op jit(solution)/shard_map/pallas_call | solution.py:295
  57.2 0.4 collective-permute-done.2.refs_3_
  57.7 4.5 %shard_map.195 = (bf16[16,4224]{1,0:T(8,128)(2,1)S(1)}, bf16[16,4224]{1,0:T(8,128)(2,1)S(1)}, bf16[16,4224]{1,0:T(8,128)(2,1)S(1)}, bf16[16,4224]{1,0:T(8,128)(2,1)S(1)}) custom-call(bf16[12,576,128]{2,1,0:T(8,128)(2,1)} %bitcast.43, f32[1,1536]{1,0:T(1,128)S(1)} %bitcast.33, bf16[16,4736]{1,0:T(8,128)(2,1)S(1)} %get-tuple-element.87.refs_0_, ...), custom_call_target="tpu_custom_call" | custom-call | flops 1711276032 | bytes 1769472 | tf_op jit(solution)/shard_map/pallas_call | solution.py:295
  62.7 1.6 collective-permute-start.10
  64.4 0.5 collective-permute-start.6
  64.9 1.5 collective-permute-start.7
  66.5 8.4 %shard_map.196.refs_1_ = f32[256,640]{1,0:T(8,128)} custom-call(bf16[8,32,1152]{2,1,0:T(8,128)(2,1)S(1)} %all-to-all-done.1.rows_ref, s32[1,2048]{1,0:T(1,128)S(1)} %select_n.120.holder_ref, bf16[576,4096]{1,0:T(8,128)(2,1)} %bitcast.39, bf16[2048,576]{1,0:T(8,128)(2,1)} %bitcast.41), custom_call_target="tpu_custom_call" | custom-call | flops 2852126720 | bytes 7077888 | tf_op jit(solution)/shard_map/pallas_call | solution.py:212
  75.0 1.7 %collective-permute-done.8.refs_5_ = bf16[16,4224]{1,0:T(8,128)(2,1)S(1)} collective-permute-done((bf16[16,4224]{1,0:T(8,128)(2,1)S(1)}, bf16[16,4224]{1,0:T(8,128)(2,1)S(1)}, u32[]{:S(2)}, u32[]{:S(2)}) %collective-permute-start.8) | collective-permute-done | bytes 135200 | tf_op jit(solution)/shard_map/ppermute | solution.py:530
  76.7 2.1 %shard_map.197 = bf16[8,72,512]{2,1,0:T(8,128)(2,1)S(1)} custom-call(bf16[32,64]{1,0:T(8,128)(2,1)S(1)} %and_convert_fusion.unpick_ref, f32[256,640]{1,0:T(8,128)} %shard_map.193.refs_0_, f32[256,640]{1,0:T(8,128)} %shard_map.196.refs_1_, bf16[16,4224]{1,0:T(8,128)(2,1)S(1)} %get-tuple-element.100.refs_2_, ...), custom_call_target="tpu_custom_call" | custom-call | flops 33554432 | bytes 1048576 | tf_op jit(solution)/shard_map/pallas_call | solution.py:366
  78.8 20.9 %all_to_all.30.parts_ref = bf16[8,72,512]{2,1,0:T(8,128)(2,1)S(1)} all-to-all(bf16[8,72,512]{2,1,0:T(8,128)(2,1)S(1)} %shard_map.197), channel_id=1, replica_groups=mesh['pair'=2,'core'=2,'tensor'=8] {'tensor'}, dimensions={0} | all-to-all | bytes 1179648 | tf_op jit(solution)/shard_map/all_to_all | solution.py:523
  100.0 17.5 %all_to_all.31 = bf16[8,64,512]{2,1,0:T(8,128)(2,1)S(1)} all-to-all(bf16[8,64,512]{2,1,0:T(8,128)(2,1)S(1)} %shard_map.198), channel_id=1, replica_groups=mesh['pair'=2,'core'=2,'tensor'=8] {'tensor'}, dimensions={0} | all-to-all | bytes 1048576 | tf_op jit(solution)/shard_map/all_to_all | solution.py:523
  117.5 1.3 shard_map.199
  118.9 14.0 %all_to_all.32 = bf16[16,32,256]{2,1,0:T(8,128)(2,1)S(1)} all-to-all(bf16[16,32,256]{2,1,0:T(8,128)(2,1)S(1)} %get-tuple-element.108), channel_id=1, replica_groups=mesh['pair'=2,'core'=2,'tensor'=8] {'pair','tensor'}, dimensions={0} | all-to-all | bytes 524288 | tf_op jit(solution)/shard_map/all_to_all | solution.py:523
  132.9 2.2 %all_gather.3 = bf16[2,2,8,32,256]{4,3,2,1,0:T(8,128)(2,1)S(1)} all-gather(bf16[1,2,8,32,256]{4,3,2,1,0:T(8,128)(2,1)S(1)} %bitcast.34), channel_id=1, replica_groups=mesh['pair'=2,'core'=2,'tensor'=8] {'core'}, dimensions={0}, use_global_device_ids=true | all-gather | bytes 786432 | tf_op jit(solution)/shard_map/all_gather | solution.py:687
  135.2 6.8 %shard_map.200 = bf16[4,8,24,256]{3,2,1,0:T(8,128)(2,1)} custom-call(bf16[96,128]{1,0:T(8,128)(2,1)S(1)} %add_convert_fusion.pick_ref, bf16[4,8,32,256]{3,2,1,0:T(8,128)(2,1)S(1)} %bitcast.29, bf16[1,2048]{1,0:T(2,128)(2,1)S(1)} %broadcast_in_dim.249.gain_ref, bf16[352,2048]{1,0:T(8,128)(2,1)S(1)} %copy-done.1, bf16[352,2048]{1,0:T(8,128)(2,1)S(1)} %copy-done.2, ...), custom_call_target="tpu_custom_call" | custom-call | flops 1660944384 | bytes 17301504 | tf_op jit(solution)/shard_map/pallas_call | solution.py:488
  142.0 2.6 %all-to-all-start.5 = ((bf16[32,24,256]{2,1,0:T(8,128)(2,1)}), bf16[32,24,256]{2,1,0:T(8,128)(2,1)S(1)}, u32[]{:S(2)}, u32[]{:S(2)}) async-start(bf16[32,24,256]{2,1,0:T(8,128)(2,1)} %bitcast.11), calls=%async_computation.5 | async-start | bytes 786432 | tf_op jit(solution)/shard_map/all_to_all | solution.py:523
  145.1 0.5 fusion.1
  146.1 12.1 %all-to-all-done.5 = bf16[32,24,256]{2,1,0:T(8,128)(2,1)S(1)} async-done(((bf16[32,24,256]{2,1,0:T(8,128)(2,1)}), bf16[32,24,256]{2,1,0:T(8,128)(2,1)S(1)}, u32[]{:S(2)}, u32[]{:S(2)}) %all-to-all-start.5) | async-done | bytes 393248 | tf_op jit(solution)/shard_map/all_to_all | solution.py:523
  158.2 0.9 shard_map.201
  (124 shorter events, 6.0 us)
Async XLA Ops:
  0.0 24.0 %copy-start.6 = (s32[32,6]{0,1:T(8,128)S(1)}, s32[32,6]{0,1:T(8,128)}, u32[]{:S(2)}) copy-start(s32[32,6]{0,1:T(8,128)} %param.31) | copy-start | bytes 2308
  0.0 20.3 %copy-start.10 = (s32[32]{0:T(128)S(1)}, s32[32]{0:T(128)}, u32[]{:S(2)}) copy-start(s32[32]{0:T(128)} %param.29) | copy-start | bytes 388
  0.0 24.6 %copy-start.9 = (s32[32]{0:T(128)S(1)}, s32[32]{0:T(128)}, u32[]{:S(2)}) copy-start(s32[32]{0:T(128)} %param.28) | copy-start | bytes 388
  0.0 24.4 %copy-start.8 = (s32[12]{0:T(128)S(1)}, s32[12]{0:T(128)}, u32[]{:S(2)}) copy-start(s32[12]{0:T(128)} %param.26) | copy-start | bytes 148
  1.4 14.6 %all-to-all-start = ((bf16[8,32,256]{2,1,0:T(8,128)(2,1)}), bf16[8,32,256]{2,1,0:T(8,128)(2,1)S(1)}, u32[]{:S(2)}, u32[]{:S(2)}) async-start(bf16[8,32,256]{2,1,0:T(8,128)(2,1)} %broadcast_in_dim.228), calls=%async_computation | async-start | bytes 262144 | tf_op jit(solution)/shard_map/all_to_all | solution.py:523
  20.3 18.2 %all-to-all-start.1 = ((bf16[8,32,1152]{2,1,0:T(8,128)(2,1)}), bf16[8,32,1152]{2,1,0:T(8,128)(2,1)S(1)}, u32[]{:S(2)}, u32[]{:S(2)}) async-start(bf16[8,32,1152]{2,1,0:T(8,128)(2,1)} %shard_map.190), calls=%async_computation.1 | async-start | bytes 1179648 | tf_op jit(solution)/shard_map/all_to_all | solution.py:523
  39.1 12.3 %collective-permute-start.3 = (bf16[16,4736]{1,0:T(8,128)(2,1)S(1)}, bf16[16,4736]{1,0:T(8,128)(2,1)S(1)}, u32[]{:S(2)}, u32[]{:S(2)}) collective-permute-start(bf16[16,4736]{1,0:T(8,128)(2,1)S(1)} %get-tuple-element.78), channel_id=1, source_target_pairs={{0,8},{8,0},{16,24},{24,16},{1,9},{9,1},{17,25},{25,17},{2,10},{10... | collective-permute-start | bytes 454664 | tf_op jit(solution)/shard_map/ppermute | solution.py:530
  39.1 12.7 %collective-permute-start.4 = (bf16[16,4736]{1,0:T(8,128)(2,1)S(1)}, bf16[16,4736]{1,0:T(8,128)(2,1)S(1)}, u32[]{:S(2)}, u32[]{:S(2)}) collective-permute-start(bf16[16,4736]{1,0:T(8,128)(2,1)S(1)} %get-tuple-element.79), channel_id=1, source_target_pairs={{0,16},{8,24},{16,0},{24,8},{1,17},{9,25},{17,1},{25,9},{2,18},{10... | collective-permute-start | bytes 454664 | tf_op jit(solution)/shard_map/ppermute | solution.py:530
  40.7 11.4 %collective-permute-start.5 = (bf16[16,4736]{1,0:T(8,128)(2,1)S(1)}, bf16[16,4736]{1,0:T(8,128)(2,1)S(1)}, u32[]{:S(2)}, u32[]{:S(2)}) collective-permute-start(bf16[16,4736]{1,0:T(8,128)(2,1)S(1)} %get-tuple-element.80), channel_id=1, source_target_pairs={{0,24},{8,16},{16,8},{24,0},{1,25},{9,17},{17,9},{25,1},{2,26},{10... | collective-permute-start | bytes 454664 | tf_op jit(solution)/shard_map/ppermute | solution.py:530
  41.3 16.0 %collective-permute-start = (bf16[16,4736]{1,0:T(8,128)(2,1)S(1)}, bf16[16,4736]{1,0:T(8,128)(2,1)S(1)}, u32[]{:S(2)}, u32[]{:S(2)}) collective-permute-start(bf16[16,4736]{1,0:T(8,128)(2,1)S(1)} %get-tuple-element.74), channel_id=1, source_target_pairs={{0,8},{8,0},{16,24},{24,16},{1,9},{9,1},{17,25},{25,17},{2,10},{10... | collective-permute-start | bytes 454664 | tf_op jit(solution)/shard_map/ppermute | solution.py:530
  41.7 15.6 %collective-permute-start.1 = (bf16[16,4736]{1,0:T(8,128)(2,1)S(1)}, bf16[16,4736]{1,0:T(8,128)(2,1)S(1)}, u32[]{:S(2)}, u32[]{:S(2)}) collective-permute-start(bf16[16,4736]{1,0:T(8,128)(2,1)S(1)} %get-tuple-element.75), channel_id=1, source_target_pairs={{0,16},{8,24},{16,0},{24,8},{1,17},{9,25},{17,1},{25,9},{2,18},{10... | collective-permute-start | bytes 454664 | tf_op jit(solution)/shard_map/ppermute | solution.py:530
  51.4 6.2 %collective-permute-start.2 = (bf16[16,4736]{1,0:T(8,128)(2,1)S(1)}, bf16[16,4736]{1,0:T(8,128)(2,1)S(1)}, u32[]{:S(2)}, u32[]{:S(2)}) collective-permute-start(bf16[16,4736]{1,0:T(8,128)(2,1)S(1)} %get-tuple-element.76), channel_id=1, source_target_pairs={{0,24},{8,16},{16,8},{24,0},{1,25},{9,17},{17,9},{25,1},{2,26},{10... | collective-permute-start | bytes 454664 | tf_op jit(solution)/shard_map/ppermute | solution.py:530
  62.2 4.2 %collective-permute-start.9 = (bf16[16,4224]{1,0:T(8,128)(2,1)S(1)}, bf16[16,4224]{1,0:T(8,128)(2,1)S(1)}, u32[]{:S(2)}, u32[]{:S(2)}) collective-permute-start(bf16[16,4224]{1,0:T(8,128)(2,1)S(1)} %get-tuple-element.97), channel_id=1, source_target_pairs={{0,8},{8,0},{16,24},{24,16},{1,9},{9,1},{17,25},{25,17},{2,10},{10... | collective-permute-start | bytes 405512 | tf_op jit(solution)/shard_map/ppermute | solution.py:530
  62.7 12.2 %collective-permute-start.10 = (bf16[16,4224]{1,0:T(8,128)(2,1)S(1)}, bf16[16,4224]{1,0:T(8,128)(2,1)S(1)}, u32[]{:S(2)}, u32[]{:S(2)}) collective-permute-start(bf16[16,4224]{1,0:T(8,128)(2,1)S(1)} %get-tuple-element.98), channel_id=1, source_target_pairs={{0,16},{8,24},{16,0},{24,8},{1,17},{9,25},{17,1},{25,9},{2,18},{10... | collective-permute-start | bytes 405512 | tf_op jit(solution)/shard_map/ppermute | solution.py:530
  64.3 10.6 %collective-permute-start.11 = (bf16[16,4224]{1,0:T(8,128)(2,1)S(1)}, bf16[16,4224]{1,0:T(8,128)(2,1)S(1)}, u32[]{:S(2)}, u32[]{:S(2)}) collective-permute-start(bf16[16,4224]{1,0:T(8,128)(2,1)S(1)} %get-tuple-element.99), channel_id=1, source_target_pairs={{0,24},{8,16},{16,8},{24,0},{1,25},{9,17},{17,9},{25,1},{2,26},{10... | collective-permute-start | bytes 405512 | tf_op jit(solution)/shard_map/ppermute | solution.py:530
  64.4 10.5 %collective-permute-start.6 = (bf16[16,4224]{1,0:T(8,128)(2,1)S(1)}, bf16[16,4224]{1,0:T(8,128)(2,1)S(1)}, u32[]{:S(2)}, u32[]{:S(2)}) collective-permute-start(bf16[16,4224]{1,0:T(8,128)(2,1)S(1)} %get-tuple-element.94), channel_id=1, source_target_pairs={{0,8},{8,0},{16,24},{24,16},{1,9},{9,1},{17,25},{25,17},{2,10},{10... | collective-permute-start | bytes 405512 | tf_op jit(solution)/shard_map/ppermute | solution.py:530
  64.9 10.1 %collective-permute-start.7 = (bf16[16,4224]{1,0:T(8,128)(2,1)S(1)}, bf16[16,4224]{1,0:T(8,128)(2,1)S(1)}, u32[]{:S(2)}, u32[]{:S(2)}) collective-permute-start(bf16[16,4224]{1,0:T(8,128)(2,1)S(1)} %get-tuple-element.95), channel_id=1, source_target_pairs={{0,16},{8,24},{16,0},{24,8},{1,17},{9,25},{17,1},{25,9},{2,18},{10... | collective-permute-start | bytes 405512 | tf_op jit(solution)/shard_map/ppermute | solution.py:530
  66.5 10.2 %collective-permute-start.8 = (bf16[16,4224]{1,0:T(8,128)(2,1)S(1)}, bf16[16,4224]{1,0:T(8,128)(2,1)S(1)}, u32[]{:S(2)}, u32[]{:S(2)}) collective-permute-start(bf16[16,4224]{1,0:T(8,128)(2,1)S(1)} %get-tuple-element.96), channel_id=1, source_target_pairs={{0,24},{8,16},{16,8},{24,0},{1,25},{9,17},{17,9},{25,1},{2,26},{10... | collective-permute-start | bytes 405512 | tf_op jit(solution)/shard_map/ppermute | solution.py:530
  78.8 56.3 %slice-start = ((s8[5767168]{0:T(1024)(128)(4,1)}), s8[4194304]{0:T(1024)(128)(4,1)S(1)}, s32[]{:S(2)}) async-start(s8[5767168]{0:T(1024)(128)(4,1)} %bitcast.22), calls=%async_computation.6 | async-start | bytes 8388608
  78.8 56.3 %slice-start.2 = ((s8[5767168]{0:T(1024)(128)(4,1)}), s8[4194304]{0:T(1024)(128)(4,1)S(1)}, s32[]{:S(2)}) async-start(s8[5767168]{0:T(1024)(128)(4,1)} %bitcast.24), calls=%async_computation.8 | async-start | bytes 8388608
  78.8 56.3 %slice-start.4 = ((s8[5767168]{0:T(1024)(128)(4,1)}), s8[4194304]{0:T(1024)(128)(4,1)S(1)}, s32[]{:S(2)}) async-start(s8[5767168]{0:T(1024)(128)(4,1)} %bitcast.26), calls=%async_computation.10 | async-start | bytes 8388608
  99.7 17.9 %copy-start = (bf16[256,8192]{1,0:T(8,128)(2,1)S(1)}, bf16[256,8192]{1,0:T(8,128)(2,1)}, u32[]{:S(2)}) copy-start(bf16[256,8192]{1,0:T(8,128)(2,1)} %weight_ref.1) | copy-start | bytes 12582916
  99.7 17.9 %copy-start.4 = (bf16[32,256]{1,0:T(8,128)(2,1)S(1)}, bf16[32,256]{1,0:T(8,128)(2,1)}, u32[]{:S(2)}) copy-start(bf16[32,256]{1,0:T(8,128)(2,1)} %hidden_ref.1) | copy-start | bytes 49156
  99.7 35.4 %slice-start.1 = ((s8[5767168]{0:T(1024)(128)(4,1)}), s8[1572864]{0:T(1024)(128)(4,1)S(1)}, s32[]{:S(2)}) async-start(s8[5767168]{0:T(1024)(128)(4,1)} %bitcast.22), calls=%async_computation.7 | async-start | bytes 3145728
  99.7 35.4 %slice-start.3 = ((s8[5767168]{0:T(1024)(128)(4,1)}), s8[1572864]{0:T(1024)(128)(4,1)S(1)}, s32[]{:S(2)}) async-start(s8[5767168]{0:T(1024)(128)(4,1)} %bitcast.24), calls=%async_computation.9 | async-start | bytes 3145728
  99.7 35.4 %slice-start.5 = ((s8[5767168]{0:T(1024)(128)(4,1)}), s8[1572864]{0:T(1024)(128)(4,1)S(1)}, s32[]{:S(2)}) async-start(s8[5767168]{0:T(1024)(128)(4,1)} %bitcast.26), calls=%async_computation.11 | async-start | bytes 3145728
  100.0 35.1 %copy-start.1 = (bf16[352,2048]{1,0:T(8,128)(2,1)S(1)}, bf16[352,2048]{1,0:T(8,128)(2,1)}, u32[]{:S(2)}) copy-start(bf16[352,2048]{1,0:T(8,128)(2,1)} %shared_gate_ref.1) | copy-start | bytes 4325380
  100.0 35.1 %copy-start.2 = (bf16[352,2048]{1,0:T(8,128)(2,1)S(1)}, bf16[352,2048]{1,0:T(8,128)(2,1)}, u32[]{:S(2)}) copy-start(bf16[352,2048]{1,0:T(8,128)(2,1)} %shared_up_ref.1) | copy-start | bytes 4325380
  100.0 35.1 %copy-start.3 = (bf16[352,2048]{1,0:T(8,128)(2,1)S(1)}, bf16[352,2048]{1,0:T(8,128)(2,1)}, u32[]{:S(2)}) copy-start(bf16[352,2048]{1,0:T(8,128)(2,1)} %shared_down_ref.1) | copy-start | bytes 4325380
  135.2 9.6 %copy-start.7 = (f32[32,6]{0,1:T(8,128)S(1)}, f32[32,6]{0,1:T(8,128)}, u32[]{:S(2)}) copy-start(f32[32,6]{0,1:T(8,128)} %param.32) | copy-start | bytes 2308
  135.2 10.4 %copy-start.5 = (f32[32,32,8]{2,1,0:T(8,128)S(1)}, f32[32,32,8]{2,1,0:T(8,128)}, u32[]{:S(2)}) copy-start(f32[32,32,8]{2,1,0:T(8,128)} %constant.93.clone) | copy-start | bytes 98308
  142.0 16.1 %all-to-all-start.5 = ((bf16[32,24,256]{2,1,0:T(8,128)(2,1)}), bf16[32,24,256]{2,1,0:T(8,128)(2,1)S(1)}, u32[]{:S(2)}, u32[]{:S(2)}) async-start(bf16[32,24,256]{2,1,0:T(8,128)(2,1)} %bitcast.11), calls=%async_computation.5 | async-start | bytes 786432 | tf_op jit(solution)/shard_map/all_to_all | solution.py:523

commit v4 on v3

--- a/solution.py
+++ b/solution.py
@@ -91,17 +91,16 @@
     for step in range(steps):
         copies[step].wait()
         out = dot_nt(normed, weight_ref[step]).astype(jnp.bfloat16)
-        for k in range(out_ref.shape[0]):
-            out_ref[k, :, step * each : (step + 1) * each] = out
-
-
-def project(rows, gain, weight, copies):
+        out_ref[:, step * each : (step + 1) * each] = out
+
+
+def project(rows, gain, weight):
     pieces, requests, part = rows.shape
     columns, width = weight.shape
     steps = 3 if columns % (3 * LANES) == 0 else 1
     return call(
         project_body,
-        jax.ShapeDtypeStruct((copies, requests, columns), jnp.bfloat16),
+        jax.ShapeDtypeStruct((requests, columns), jnp.bfloat16),
         16,
         2 * requests * columns * width,
         2 * columns * width,
@@ -114,26 +113,27 @@
     )(rows, gain, in_hbm(weight))
 
 
-def pick_body(share, pick_ref, extra_ref, rows_ref, *out_refs):
+def pick_body(pick_ref, extra_ref, *refs):
     slots = extra_ref.shape[1]
     each = PIECES // SHARES
+    rows_refs, out_refs = refs[:each], refs[each:]
     for k in range(each):
-        picked = dot_nn(pick_ref[...], rows_ref[share * each + k]).astype(jnp.bfloat16)
+        picked = dot_nn(pick_ref[...], rows_refs[k][...]).astype(jnp.bfloat16)
         for o, out_ref in enumerate(out_refs):
             out_ref[:, k * PAIR : (k + 1) * PAIR] = picked[o * slots : (o + 1) * slots]
     for o, out_ref in enumerate(out_refs):
         out_ref[:, each * PAIR :] = extra_ref[o]
 
 
-def pick_queries(share, pick, extra, rows):
+def pick_queries(pick, extra, rows):
     owners, slots, _ = extra.shape
     return call(
-        functools.partial(pick_body, share),
+        pick_body,
         (jax.ShapeDtypeStruct((slots, HEADS * KVW + LANES), jnp.bfloat16),) * owners,
         16,
-        2 * owners * slots * rows.shape[1] * HEADS * KVW,
+        2 * owners * slots * pick.shape[1] * HEADS * KVW,
         4 * owners * slots * HEADS * KVW,
-    )(pick, extra, rows)
+    )(pick, extra, *rows)
 
 
 def sums(scores, usable=None):
@@ -149,8 +149,12 @@
     return peak, [w.astype(jnp.bfloat16) for w in weights], total
 
 
-def own_body(share, rows_ref, holder_ref, root_hbm, suffix_hbm, out_hbm, out_ref, q_ref, root_ref, suffix_ref, s_ref, root_sems, suffix_sems, out_sem):
-    requests = rows_ref.shape[1]
+def own_body(holder_ref, root_hbm, suffix_hbm, *refs):
+    rows_refs, out_hbm = refs[: HEADS // 2], refs[HEADS // 2]
+    out_ref, q_ref, root_ref, suffix_ref, s_ref, root_sems, suffix_sems, out_sem = refs[
+        HEADS // 2 + 1 :
+    ]
+    requests = rows_refs[0].shape[0]
     blocks, _, block = root_ref.shape
     groups, span, _ = suffix_ref.shape
     each = requests // groups
@@ -169,10 +173,9 @@
     for copy in root_copies + suffix_copies:
         copy.start()
     for h in range(HEADS):
-        k, j = divmod(share * HEADS + h, 2)
-        q_ref[h * requests : (h + 1) * requests, :] = rows_ref[k, :, j * KVW : (j + 1) * KVW]
+        k, j = divmod(h, 2)
+        q_ref[h * requests : (h + 1) * requests, :] = rows_refs[k][:, j * KVW : (j + 1) * KVW]
     scale = score_scale * log2e
-    peaks = []
     for b in range(blocks):
         root_copies[b].wait()
         s_ref[b] = dot_nn(q_ref[...], root_ref[b]) * scale
@@ -203,19 +206,19 @@
     copy.wait()
 
 
-def own_attention(share, rows, holder, root, suffix):
-    count = HEADS * rows.shape[1]
+def own_attention(rows, holder, root, suffix):
+    count = HEADS * rows[0].shape[0]
     positions = root.shape[1]
     block = min(1024, positions)
     blocks, groups = positions // block, 2
     span = suffix.shape[0] // groups
     return call(
-        functools.partial(own_body, share),
+        own_body,
         pltpu.HBM((count, LAT + LANES), jnp.float32),
         44,
         2 * count * (positions + span) * (KVW + LAT),
         2 * KVW * (positions + suffix.shape[0]),
-        in_specs=[VMEM, VMEM, HBM, HBM],
+        in_specs=[VMEM, HBM, HBM] + [VMEM] * len(rows),
         out_specs=HBM,
         scratch_shapes=[
             pltpu.VMEM((count, LAT + LANES), jnp.float32),
@@ -227,7 +230,7 @@
             pltpu.SemaphoreType.DMA((groups,)),
             pltpu.SemaphoreType.DMA,
         ],
-    )(rows, holder, in_hbm(root), in_hbm(suffix))
+    )(holder, in_hbm(root), in_hbm(suffix), *rows)
 
 
 def group_body(owners, cache_hbm, holder_ref, *refs):
@@ -308,7 +311,7 @@
     )(in_hbm(cache), holder, *rows)
 
 
-def local_body(unpick_ref, *refs):
+def local_body(base_ref, unpick_ref, *refs):
     first_hbm, back_refs = refs[:SHARES], refs[SHARES:-4]
     out_ref, first_ref, out_mass_ref, sems = refs[-4:]
     copies = [
@@ -326,6 +329,7 @@
 
     extras = [returned(share, slice(HEADS * LAT, None)) for share in range(SHARES)]
     shares, length = out_ref.shape[0], out_ref.shape[1] - MASS_ROWS
+    per_piece = shares // PIECES
     for h in range(H):
         share, head = divmod(h, HEADS)
         if head == 0:
@@ -345,7 +349,8 @@
         out = out.astype(jnp.bfloat16)
         each = min(length, requests)
         for k in range(requests // each):
-            target, row = divmod(h * requests + k * each, length)
+            sub, row = divmod(h % 2 * requests + k * each, length)
+            target = (h // 2 ^ base_ref[0]) * per_piece + sub
             out_ref[target, row : row + each, :] = out[k * each : (k + 1) * each]
         out_mass_ref[h * requests : (h + 1) * requests, :] = peak + jnp.log(total)
     diagonal = lax.broadcasted_iota(jnp.int32, (length, LAT), 0) == lax.broadcasted_iota(
@@ -358,10 +363,12 @@
         tail = jnp.zeros((MASS_ROWS, LAT), jnp.float32)
         for k, part in enumerate(split_three(masses)):
             tail = jnp.where(row == k, part, tail)
-        out_ref[share, length:, :] = tail.astype(jnp.bfloat16)
-
-
-def local_join(unpick, first, back, shares):
+        piece, sub = divmod(share, per_piece)
+        target = (piece ^ base_ref[0]) * per_piece + sub
+        out_ref[target, length:, :] = tail.astype(jnp.bfloat16)
+
+
+def local_join(base, unpick, first, back, shares):
     count = SHARES * first[0].shape[0]
     return call(
         local_body,
@@ -369,14 +376,16 @@
         10,
         2 * unpick.shape[0] * unpick.shape[1] * H * LAT,
         4 * count * LAT,
-        in_specs=[VMEM] + [HBM] * SHARES + [VMEM] * len(back),
+        in_specs=[pl.BlockSpec(memory_space=pltpu.SMEM), VMEM]
+        + [HBM] * SHARES
+        + [VMEM] * len(back),
         out_specs=VMEM,
         scratch_shapes=[
             pltpu.VMEM((SHARES,) + first[0].shape, jnp.float32),
             pltpu.VMEM((count, 1), jnp.float32),
             pltpu.SemaphoreType.DMA((SHARES,)),
         ],
-    )(unpick, *[in_hbm(x) for x in first], *back)
+    )(base, unpick, *[in_hbm(x) for x in first], *back)
 
 
 def join_body(parts_ref, out_ref):
@@ -521,6 +530,11 @@
 
 def exchange(x, axis):
     return lax.all_to_all(x, axis, 0, 0, tiled=True)
+
+
+def turn(x, k):
+    count = lax.axis_size("tensor")
+    return lax.ppermute(x, "tensor", [(i, i ^ k) for i in range(count)])
 
 
 def swap_owners(arrays):
@@ -593,9 +607,7 @@
         group_columns = jnp.swapaxes(group_cache, 1, 2)
     rows = exchange(jnp.broadcast_to(hidden[None], (tensors,) + hidden.shape), "tensor")
 
-    projected = project(
-        gather_pieces(rows), attention_gain[None], query_weight, tensors
-    )
+    projected = project(gather_pieces(rows), attention_gain[None], query_weight)
     projected, group_of, group_length, suffix_length, routes, route_weight = (
         lax.optimization_barrier(
             (projected, group_of, group_length, suffix_length, routes, route_weight)
@@ -630,12 +642,18 @@
         .reshape(1, -1)
         .astype(jnp.float32)
     )
-    queries = gather_pieces(exchange(projected, "tensor"))
-    arrived, asking = [], queries
-    for share in range(SHARES):
-        sent = pick_queries(share, pick, extra, asking)
-        asking, sent = lax.optimization_barrier((queries, sent))
-        arrived.append(swap_owners(sent))
+    if tensors == PIECES:
+        base = tensor_index
+        pieces = [projected] + [turn(projected, k) for k in (1, 2, 3)]
+        pieces.append(turn(projected, 4))
+        pieces += [turn(pieces[4], k) for k in (1, 2, 3)]
+    else:
+        base = jnp.zeros((), jnp.int32)
+        copies = jnp.broadcast_to(projected[None], (tensors,) + projected.shape)
+        queries = gather_pieces(exchange(copies, "tensor"))
+        pieces = [queries[k] for k in range(PIECES)]
+    near, far = pieces[: PIECES // 2], pieces[PIECES // 2 :]
+    arrived = [swap_owners(pick_queries(pick, extra, near))]
     all_routes = jnp.stack(
         [x[:, HEADS * KVW + 1 : HEADS * KVW + 1 + named.shape[1]] for x in arrived[0]]
     ).reshape(1, owners, requests, fanout)
@@ -665,19 +683,24 @@
         [expert_pick.reshape(owners * expert_slots, owners * requests), shared_pick], axis=0
     ).astype(jnp.bfloat16)
     root_columns, suffix_rows = root_cache.T, suffix_cache.reshape(-1, KVW)
-    first, back, own = [], [], queries
-    for share in range(SHARES):
-        first.append(own_attention(share, own, suffix_holder, root_columns, suffix_rows))
-        if share == 0:
-            before = first[0]
-            for k in range(SHARES):
-                waited, before = lax.optimization_barrier((arrived[k], before))
-                answered = group_attention(waited, group_columns, group_holder)
-                before = answered[0]
-                back.append(swap_owners(answered))
-            own, before, expert_pick = lax.optimization_barrier((own, before, expert_pick))
+    near, far[0] = lax.optimization_barrier((near, far[0]))
+    first = [own_attention(near, suffix_holder, root_columns, suffix_rows)]
+    far, first = lax.optimization_barrier((far, first))
+    sent = pick_queries(pick, extra, far)
+    arrived[0], sent = lax.optimization_barrier((arrived[0], sent))
+    arrived.append(swap_owners(sent))
+    back = []
+    for share in arrived:
+        if back:
+            share, answered = lax.optimization_barrier((share, answered))
+            back[0] = swap_owners(answered)
+        answered = group_attention(share, group_columns, group_holder)
+        back.append(swap_owners(answered))
+    far, answered, expert_pick = lax.optimization_barrier((far, answered, expert_pick))
+    back[1] = swap_owners(answered)
+    first.append(own_attention(far, suffix_holder, root_columns, suffix_rows))
     back, gain = lax.optimization_barrier((back, mixture_gain[None]))
-    parts = local_join(unpick, first, sum(back, []), tensors)
+    parts = local_join(base[None], unpick, first, sum(back, []), tensors)
     attention = exchange(join(exchange(parts, "tensor")), "tensor")
     mid, copies = output_projection(
         attention.reshape(-1, LAT), out_weight, hidden, owners // 2 * tensors

time: 160 us -> 154 us (0.963)
  waiting for transfers between devices: 32.8 us -> 22.8 us
  starting transfers between devices: 21.2 us -> 24.9 us
    all_to_all x3 -> x2, waiting for transfers between devices: 30.7 us -> 17.9 us  [exchange(): return lax.all_to_all(x, axis, 0, 0, tiled=True)]
    ppermute x0 -> x7, starting transfers between devices: none -> 7.14 us  [turn(): return lax.ppermute(x, 'tensor', [(i, i ^ k) for i in range(count)])]
    all_to_all x3 -> x2, starting transfers between devices: 13.4 us -> 9.85 us  [exchange(): return lax.all_to_all(x, axis, 0, 0, tiled=True)]
  transfers between devices with their start and end apart: 15 -> 21, of which waited for: 6 -> 7; matrix products, arithmetic and copies ran while one was open for 4% -> 3% of each run, Pallas kernels for 14% -> 15%
where the time goes in v4:
time: 154 us
  blocking collectives  55.6 us (36%)
  Pallas kernels  42.8 us (28%)
  starting transfers between devices  24.9 us (16%)
  waiting for transfers between devices  22.8 us (15%)
  local copies, waits for them, and re-layouts  4.75 us (3%)
  other arithmetic  2.42 us (2%)
    all_to_all x3, blocking collectives, exchange(): return lax.all_to_all(x, axis, 0, 0, tiled=True)  53.4 us
    pallas_call x2, Pallas kernels, own_attention(): call(own_body, pltpu.HBM((count, LAT + LANES), jnp.float32), 44, 2 * coun...  18.1 us
    all_to_all x2, waiting for transfers between devices, exchange(): return lax.all_to_all(x, axis, 0, 0, tiled=True)  17.9 us
    all_to_all x2, starting transfers between devices, exchange(): return lax.all_to_all(x, axis, 0, 0, tiled=True)  9.85 us
    pallas_call x2, Pallas kernels, group_attention(): call(functools.partial(group_body, owners), (out,) * owners, 40, 2 * owne...  9.28 us
    ppermute x12, starting transfers between devices, swap_owners(): out[k] = lax.ppermute(arrays[k], OWNER, [(i, i ^ k) for i in range(count)])  7.93 us
    ppermute x7, starting transfers between devices, turn(): return lax.ppermute(x, 'tensor', [(i, i ^ k) for i in range(count)])  7.14 us
    pallas_call x1, Pallas kernels, expert(): call(expert_body, jax.ShapeDtypeStruct((owners, PIECES, slots + requests...  6.87 us
  transfers between devices with their start and end apart: 21, of which 7 were waited for; matrix products, arithmetic and copies ran while one was open for 3% of the time, Pallas kernels for 15%

profile of v4, /device:TPU:0, one launch (start us, length us, event | category | flops | bytes accessed | tf_op | source)
XLA Modules:
  0.0 153.8 jit_solution(2003513284939637607)
XLA Ops:
  0.0 1.4 broadcast_in_dim.231
  1.4 7.3 %all-to-all-start = ((bf16[8,32,256]{2,1,0:T(8,128)(2,1)}), bf16[8,32,256]{2,1,0:T(8,128)(2,1)S(1)}, u32[]{:S(2)}, u32[]{:S(2)}) async-start(bf16[8,32,256]{2,1,0:T(8,128)(2,1)} %broadcast_in_dim.231), calls=%async_computation | async-start | bytes 262144 | tf_op jit(solution)/shard_map/all_to_all | solution.py:532
  9.5 0.7 broadcast_in_dim.232.gain_ref
  10.2 5.8 %all-to-all-done.rows_ref = bf16[8,32,256]{2,1,0:T(8,128)(2,1)S(1)} async-done(((bf16[8,32,256]{2,1,0:T(8,128)(2,1)}), bf16[8,32,256]{2,1,0:T(8,128)(2,1)S(1)}, u32[]{:S(2)}, u32[]{:S(2)}) %all-to-all-start) | async-done | bytes 131104 | tf_op jit(solution)/shard_map/all_to_all | solution.py:532
  16.0 3.4 %shard_map.190.refs_0_ = bf16[32,1152]{1,0:T(8,128)(2,1)S(1)} custom-call(bf16[8,32,256]{2,1,0:T(8,128)(2,1)S(1)} %all-to-all-done.rows_ref, bf16[1,2048]{1,0:T(2,128)(2,1)S(1)} %broadcast_in_dim.232.gain_ref, bf16[1152,2048]{1,0:T(8,128)(2,1)} %weight_hbm.1), custom_call_target="tpu_custom_call" | custom-call | flops 150994944 | bytes 4718592 | tf_op jit(solution)/shard_map/pallas_call | solution.py:101
  19.9 1.3 collective-permute-start.2
  21.6 1.8 %collective-permute-start = (bf16[32,1152]{1,0:T(8,128)(2,1)S(1)}, bf16[32,1152]{1,0:T(8,128)(2,1)S(1)}, u32[]{:S(2)}, u32[]{:S(2)}) collective-permute-start(bf16[32,1152]{1,0:T(8,128)(2,1)S(1)} %shard_map.190.refs_0_), channel_id=1, source_target_pairs={{0,1},{1,0},{2,3},{3,2},{4,5},{5,4},{6,7},{7,6},{8,9},{9,8},{10,11... | collective-permute-start | bytes 221192 | tf_op jit(solution)/shard_map/ppermute | solution.py:537
  24.4 0.9 collective-permute-done.3.refs_0_
  25.3 1.0 collective-permute-start.6
  26.9 1.6 %collective-permute-start.8 = (bf16[16,4736]{1,0:T(8,128)(2,1)S(1)}, bf16[16,4736]{1,0:T(8,128)(2,1)S(1)}, u32[]{:S(2)}, u32[]{:S(2)}) collective-permute-start(bf16[16,4736]{1,0:T(8,128)(2,1)S(1)} %get-tuple-element.92), channel_id=1, source_target_pairs={{0,16},{8,24},{16,0},{24,8},{1,17},{9,25},{17,1},{25,9},{2,18},{10... | collective-permute-start | bytes 454664 | tf_op jit(solution)/shard_map/ppermute | solution.py:544
  28.7 1.4 collective-permute-start.5
  30.5 0.8 collective-permute-start.4
  31.3 9.0 %shard_map.191.refs_0_ = f32[256,640]{1,0:T(8,128)} custom-call(s32[1,2048]{1,0:T(1,128)S(1)} %select_n.114.holder_ref, bf16[576,4096]{1,0:T(8,128)(2,1)} %bitcast.39, bf16[2048,576]{1,0:T(8,128)(2,1)} %bitcast.41, bf16[32,1152]{1,0:T(8,128)(2,1)S(1)} %shard_map.190.refs_0_, bf16[32,1152]{1,0:T(8,128)(2,1)S(1)} %collective-permute-done.refs_1_, ...), custom_call_target="tpu_custom_call" | custom-call | flops 2852126720 | bytes 7077888 | tf_op jit(solution)/shard_map/pallas_call | solution.py:215
  42.3 1.6 %collective-permute-start.11 = (bf16[16,4736]{1,0:T(8,128)(2,1)S(1)}, bf16[16,4736]{1,0:T(8,128)(2,1)S(1)}, u32[]{:S(2)}, u32[]{:S(2)}) collective-permute-start(bf16[16,4736]{1,0:T(8,128)(2,1)S(1)} %get-tuple-element.100), channel_id=1, source_target_pairs={{0,16},{8,24},{16,0},{24,8},{1,17},{9,25},{17,1},{25,9},{2,18},{10... | collective-permute-start | bytes 454664 | tf_op jit(solution)/shard_map/ppermute | solution.py:544
  44.2 4.6 %shard_map.194 = (bf16[16,4224]{1,0:T(8,128)(2,1)S(1)}, bf16[16,4224]{1,0:T(8,128)(2,1)S(1)}, bf16[16,4224]{1,0:T(8,128)(2,1)S(1)}, bf16[16,4224]{1,0:T(8,128)(2,1)S(1)}) custom-call(bf16[12,576,128]{2,1,0:T(8,128)(2,1)} %bitcast.43, f32[1,1536]{1,0:T(1,128)S(1)} %bitcast.33, bf16[16,4736]{1,0:T(8,128)(2,1)S(1)} %get-tuple-element.102.refs_0_, ...), custom_call_target="tpu_custom_call" | custom-call | flops 1711276032 | bytes 1769472 | tf_op jit(solution)/shard_map/pallas_call | solution.py:298
  49.1 2.3 %collective-permute-done.12.refs_3_ = bf16[16,4736]{1,0:T(8,128)(2,1)S(1)} collective-permute-done((bf16[16,4736]{1,0:T(8,128)(2,1)S(1)}, bf16[16,4736]{1,0:T(8,128)(2,1)S(1)}, u32[]{:S(2)}, u32[]{:S(2)}) %collective-permute-start.12) | collective-permute-done | bytes 151584 | tf_op jit(solution)/shard_map/ppermute | solution.py:544
  51.5 4.7 %shard_map.195 = (bf16[16,4224]{1,0:T(8,128)(2,1)S(1)}, bf16[16,4224]{1,0:T(8,128)(2,1)S(1)}, bf16[16,4224]{1,0:T(8,128)(2,1)S(1)}, bf16[16,4224]{1,0:T(8,128)(2,1)S(1)}) custom-call(bf16[12,576,128]{2,1,0:T(8,128)(2,1)} %bitcast.44, f32[1,1536]{1,0:T(1,128)S(1)} %bitcast.34, bf16[16,4736]{1,0:T(8,128)(2,1)S(1)} %get-tuple-element.110.refs_0_, ...), custom_call_target="tpu_custom_call" | custom-call | flops 1711276032 | bytes 1769472 | tf_op jit(solution)/shard_map/pallas_call | solution.py:298
  56.6 1.6 %collective-permute-start.17 = (bf16[16,4224]{1,0:T(8,128)(2,1)S(1)}, bf16[16,4224]{1,0:T(8,128)(2,1)S(1)}, u32[]{:S(2)}, u32[]{:S(2)}) collective-permute-start(bf16[16,4224]{1,0:T(8,128)(2,1)S(1)} %get-tuple-element.130), channel_id=1, source_target_pairs={{0,16},{8,24},{16,0},{24,8},{1,17},{9,25},{17,1},{25,9},{2,18},{10... | collective-permute-start | bytes 405512 | tf_op jit(solution)/shard_map/ppermute | solution.py:544
  58.2 0.6 collective-permute-start.13
  58.8 1.5 collective-permute-start.14
  60.3 9.1 %shard_map.196.refs_1_ = f32[256,640]{1,0:T(8,128)} custom-call(s32[1,2048]{1,0:T(1,128)S(1)} %select_n.114.holder_ref, bf16[576,4096]{1,0:T(8,128)(2,1)} %bitcast.40, bf16[2048,576]{1,0:T(8,128)(2,1)} %bitcast.42, bf16[32,1152]{1,0:T(8,128)(2,1)S(1)} %collective-permute-done.3.refs_0_, bf16[32,1152]{1,0:T(8,128)(2,1)S(1)} %collective-permute-done.4.refs_1_, ...), custom_call_target="tpu_custom_call" | custom-call | flops 2852126720 | bytes 7077888 | tf_op jit(solution)/shard_map/pallas_call | solution.py:215
  69.4 0.9 collective-permute-done.15.refs_5_
  70.3 2.1 %shard_map.197 = bf16[8,72,512]{2,1,0:T(8,128)(2,1)S(1)} custom-call(s32[1]{0:T(128)} %bitcast.8.base_ref, bf16[32,64]{1,0:T(8,128)(2,1)S(1)} %and_convert_fusion.unpick_ref, f32[256,640]{1,0:T(8,128)} %shard_map.191.refs_0_, f32[256,640]{1,0:T(8,128)} %shard_map.196.refs_1_, bf16[16,4224]{1,0:T(8,128)(2,1)S(1)} %get-tuple-element.132.refs_2_, ...), custom_call_target="tpu_custom_call" | custom-call | flops 33554432 | bytes 1048576 | tf_op jit(solution)/shard_map/pallas_call | solution.py:373
  72.5 21.6 %all_to_all.25.parts_ref = bf16[8,72,512]{2,1,0:T(8,128)(2,1)S(1)} all-to-all(bf16[8,72,512]{2,1,0:T(8,128)(2,1)S(1)} %shard_map.197), channel_id=1, replica_groups=mesh['pair'=2,'core'=2,'tensor'=8] {'tensor'}, dimensions={0} | all-to-all | bytes 1179648 | tf_op jit(solution)/shard_map/all_to_all | solution.py:532
  94.5 17.8 %all_to_all.26 = bf16[8,64,512]{2,1,0:T(8,128)(2,1)S(1)} all-to-all(bf16[8,64,512]{2,1,0:T(8,128)(2,1)S(1)} %shard_map.198), channel_id=1, replica_groups=mesh['pair'=2,'core'=2,'tensor'=8] {'tensor'}, dimensions={0} | all-to-all | bytes 1048576 | tf_op jit(solution)/shard_map/all_to_all | solution.py:532
  112.2 1.3 shard_map.199
  113.6 14.0 %all_to_all.27 = bf16[16,32,256]{2,1,0:T(8,128)(2,1)S(1)} all-to-all(bf16[16,32,256]{2,1,0:T(8,128)(2,1)S(1)} %get-tuple-element.140), channel_id=1, replica_groups=mesh['pair'=2,'core'=2,'tensor'=8] {'pair','tensor'}, dimensions={0} | all-to-all | bytes 524288 | tf_op jit(solution)/shard_map/all_to_all | solution.py:532
  127.6 2.2 %all_gather.3 = bf16[2,2,8,32,256]{4,3,2,1,0:T(8,128)(2,1)S(1)} all-gather(bf16[1,2,8,32,256]{4,3,2,1,0:T(8,128)(2,1)S(1)} %bitcast.35), channel_id=1, replica_groups=mesh['pair'=2,'core'=2,'tensor'=8] {'core'}, dimensions={0}, use_global_device_ids=true | all-gather | bytes 786432 | tf_op jit(solution)/shard_map/all_gather | solution.py:710
  129.9 6.9 %shard_map.200 = bf16[4,8,24,256]{3,2,1,0:T(8,128)(2,1)} custom-call(bf16[96,128]{1,0:T(8,128)(2,1)S(1)} %add_convert_fusion.pick_ref, bf16[4,8,32,256]{3,2,1,0:T(8,128)(2,1)S(1)} %bitcast.30, bf16[1,2048]{1,0:T(2,128)(2,1)S(1)} %broadcast_in_dim.253.gain_ref, bf16[352,2048]{1,0:T(8,128)(2,1)S(1)} %copy-done.1, bf16[352,2048]{1,0:T(8,128)(2,1)S(1)} %copy-done.2, ...), custom_call_target="tpu_custom_call" | custom-call | flops 1660944384 | bytes 17301504 | tf_op jit(solution)/shard_map/pallas_call | solution.py:497
  136.8 2.6 %all-to-all-start.4 = ((bf16[32,24,256]{2,1,0:T(8,128)(2,1)}), bf16[32,24,256]{2,1,0:T(8,128)(2,1)S(1)}, u32[]{:S(2)}, u32[]{:S(2)}) async-start(bf16[32,24,256]{2,1,0:T(8,128)(2,1)} %bitcast.12), calls=%async_computation.4 | async-start | bytes 786432 | tf_op jit(solution)/shard_map/all_to_all | solution.py:532
  140.8 12.1 %all-to-all-done.4 = bf16[32,24,256]{2,1,0:T(8,128)(2,1)S(1)} async-done(((bf16[32,24,256]{2,1,0:T(8,128)(2,1)}), bf16[32,24,256]{2,1,0:T(8,128)(2,1)S(1)}, u32[]{:S(2)}, u32[]{:S(2)}) %all-to-all-start.4) | async-done | bytes 393248 | tf_op jit(solution)/shard_map/all_to_all | solution.py:532
  152.9 0.9 shard_map.201
  (138 shorter events, 8.6 us)
Async XLA Ops:
  0.0 24.3 %copy-start.9 = (s32[32]{0:T(128)S(1)}, s32[32]{0:T(128)}, u32[]{:S(2)}) copy-start(s32[32]{0:T(128)} %param.28) | copy-start | bytes 388
  0.0 26.2 %copy-start.10 = (s32[12]{0:T(128)S(1)}, s32[12]{0:T(128)}, u32[]{:S(2)}) copy-start(s32[12]{0:T(128)} %param.26) | copy-start | bytes 148
  1.4 14.6 %all-to-all-start = ((bf16[8,32,256]{2,1,0:T(8,128)(2,1)}), bf16[8,32,256]{2,1,0:T(8,128)(2,1)S(1)}, u32[]{:S(2)}, u32[]{:S(2)}) async-start(bf16[8,32,256]{2,1,0:T(8,128)(2,1)} %broadcast_in_dim.231), calls=%async_computation | async-start | bytes 262144 | tf_op jit(solution)/shard_map/all_to_all | solution.py:532
  19.4 5.8 %collective-permute-start.3 = (bf16[32,1152]{1,0:T(8,128)(2,1)S(1)}, bf16[32,1152]{1,0:T(8,128)(2,1)S(1)}, u32[]{:S(2)}, u32[]{:S(2)}) collective-permute-start(bf16[32,1152]{1,0:T(8,128)(2,1)S(1)} %shard_map.190.refs_0_), channel_id=1, source_target_pairs={{0,4},{1,5},{2,6},{3,7},{4,0},{5,1},{6,2},{7,3},{8,12},{9,13},{10,... | collective-permute-start | bytes 221192 | tf_op jit(solution)/shard_map/ppermute | solution.py:537
  19.9 6.6 %collective-permute-start.2 = (bf16[32,1152]{1,0:T(8,128)(2,1)S(1)}, bf16[32,1152]{1,0:T(8,128)(2,1)S(1)}, u32[]{:S(2)}, u32[]{:S(2)}) collective-permute-start(bf16[32,1152]{1,0:T(8,128)(2,1)S(1)} %shard_map.190.refs_0_), channel_id=1, source_target_pairs={{0,3},{1,2},{2,1},{3,0},{4,7},{5,6},{6,5},{7,4},{8,11},{9,10},{10,... | collective-permute-start | bytes 221192 | tf_op jit(solution)/shard_map/ppermute | solution.py:537
  21.2 5.3 %collective-permute-start.1 = (bf16[32,1152]{1,0:T(8,128)(2,1)S(1)}, bf16[32,1152]{1,0:T(8,128)(2,1)S(1)}, u32[]{:S(2)}, u32[]{:S(2)}) collective-permute-start(bf16[32,1152]{1,0:T(8,128)(2,1)S(1)} %shard_map.190.refs_0_), channel_id=1, source_target_pairs={{0,2},{1,3},{2,0},{3,1},{4,6},{5,7},{6,4},{7,5},{8,10},{9,11},{10,... | collective-permute-start | bytes 221192 | tf_op jit(solution)/shard_map/ppermute | solution.py:537
  21.6 4.9 %collective-permute-start = (bf16[32,1152]{1,0:T(8,128)(2,1)S(1)}, bf16[32,1152]{1,0:T(8,128)(2,1)S(1)}, u32[]{:S(2)}, u32[]{:S(2)}) collective-permute-start(bf16[32,1152]{1,0:T(8,128)(2,1)S(1)} %shard_map.190.refs_0_), channel_id=1, source_target_pairs={{0,1},{1,0},{2,3},{3,2},{4,5},{5,4},{6,7},{7,6},{8,9},{9,8},{10,11... | collective-permute-start | bytes 221192 | tf_op jit(solution)/shard_map/ppermute | solution.py:537
  25.3 5.3 %collective-permute-start.6 = (bf16[32,1152]{1,0:T(8,128)(2,1)S(1)}, bf16[32,1152]{1,0:T(8,128)(2,1)S(1)}, u32[]{:S(2)}, u32[]{:S(2)}) collective-permute-start(bf16[32,1152]{1,0:T(8,128)(2,1)S(1)} %collective-permute-done.3.refs_0_), channel_id=1, source_target_pairs={{0,3},{1,2},{2,1},{3,0},{4,7},{5,6},{6,5},{7,4},{8,11},{9,10},{10,... | collective-permute-start | bytes 221192 | tf_op jit(solution)/shard_map/ppermute | solution.py:537
  26.8 14.1 %collective-permute-start.7 = (bf16[16,4736]{1,0:T(8,128)(2,1)S(1)}, bf16[16,4736]{1,0:T(8,128)(2,1)S(1)}, u32[]{:S(2)}, u32[]{:S(2)}) collective-permute-start(bf16[16,4736]{1,0:T(8,128)(2,1)S(1)} %get-tuple-element.91), channel_id=1, source_target_pairs={{0,8},{8,0},{16,24},{24,16},{1,9},{9,1},{17,25},{25,17},{2,10},{10... | collective-permute-start | bytes 454664 | tf_op jit(solution)/shard_map/ppermute | solution.py:544
  26.9 14.3 %collective-permute-start.8 = (bf16[16,4736]{1,0:T(8,128)(2,1)S(1)}, bf16[16,4736]{1,0:T(8,128)(2,1)S(1)}, u32[]{:S(2)}, u32[]{:S(2)}) collective-permute-start(bf16[16,4736]{1,0:T(8,128)(2,1)S(1)} %get-tuple-element.92), channel_id=1, source_target_pairs={{0,16},{8,24},{16,0},{24,8},{1,17},{9,25},{17,1},{25,9},{2,18},{10... | collective-permute-start | bytes 454664 | tf_op jit(solution)/shard_map/ppermute | solution.py:544
  28.5 12.9 %collective-permute-start.9 = (bf16[16,4736]{1,0:T(8,128)(2,1)S(1)}, bf16[16,4736]{1,0:T(8,128)(2,1)S(1)}, u32[]{:S(2)}, u32[]{:S(2)}) collective-permute-start(bf16[16,4736]{1,0:T(8,128)(2,1)S(1)} %get-tuple-element.93), channel_id=1, source_target_pairs={{0,24},{8,16},{16,8},{24,0},{1,25},{9,17},{17,9},{25,1},{2,26},{10... | collective-permute-start | bytes 454664 | tf_op jit(solution)/shard_map/ppermute | solution.py:544
  28.7 11.8 %collective-permute-start.5 = (bf16[32,1152]{1,0:T(8,128)(2,1)S(1)}, bf16[32,1152]{1,0:T(8,128)(2,1)S(1)}, u32[]{:S(2)}, u32[]{:S(2)}) collective-permute-start(bf16[32,1152]{1,0:T(8,128)(2,1)S(1)} %collective-permute-done.3.refs_0_), channel_id=1, source_target_pairs={{0,2},{1,3},{2,0},{3,1},{4,6},{5,7},{6,4},{7,5},{8,10},{9,11},{10,... | collective-permute-start | bytes 221192 | tf_op jit(solution)/shard_map/ppermute | solution.py:537
  30.5 10.1 %collective-permute-start.4 = (bf16[32,1152]{1,0:T(8,128)(2,1)S(1)}, bf16[32,1152]{1,0:T(8,128)(2,1)S(1)}, u32[]{:S(2)}, u32[]{:S(2)}) collective-permute-start(bf16[32,1152]{1,0:T(8,128)(2,1)S(1)} %collective-permute-done.3.refs_0_), channel_id=1, source_target_pairs={{0,1},{1,0},{2,3},{3,2},{4,5},{5,4},{6,7},{7,6},{8,9},{9,8},{10,11... | collective-permute-start | bytes 221192 | tf_op jit(solution)/shard_map/ppermute | solution.py:537
  42.2 6.5 %collective-permute-start.10 = (bf16[16,4736]{1,0:T(8,128)(2,1)S(1)}, bf16[16,4736]{1,0:T(8,128)(2,1)S(1)}, u32[]{:S(2)}, u32[]{:S(2)}) collective-permute-start(bf16[16,4736]{1,0:T(8,128)(2,1)S(1)} %get-tuple-element.99), channel_id=1, source_target_pairs={{0,8},{8,0},{16,24},{24,16},{1,9},{9,1},{17,25},{25,17},{2,10},{10... | collective-permute-start | bytes 454664 | tf_op jit(solution)/shard_map/ppermute | solution.py:544
  42.3 6.8 %collective-permute-start.11 = (bf16[16,4736]{1,0:T(8,128)(2,1)S(1)}, bf16[16,4736]{1,0:T(8,128)(2,1)S(1)}, u32[]{:S(2)}, u32[]{:S(2)}) collective-permute-start(bf16[16,4736]{1,0:T(8,128)(2,1)S(1)} %get-tuple-element.100), channel_id=1, source_target_pairs={{0,16},{8,24},{16,0},{24,8},{1,17},{9,25},{17,1},{25,9},{2,18},{10... | collective-permute-start | bytes 454664 | tf_op jit(solution)/shard_map/ppermute | solution.py:544
  43.9 7.6 %collective-permute-start.12 = (bf16[16,4736]{1,0:T(8,128)(2,1)S(1)}, bf16[16,4736]{1,0:T(8,128)(2,1)S(1)}, u32[]{:S(2)}, u32[]{:S(2)}) collective-permute-start(bf16[16,4736]{1,0:T(8,128)(2,1)S(1)} %get-tuple-element.101), channel_id=1, source_target_pairs={{0,24},{8,16},{16,8},{24,0},{1,25},{9,17},{17,9},{25,1},{2,26},{10... | collective-permute-start | bytes 454664 | tf_op jit(solution)/shard_map/ppermute | solution.py:544
  56.2 4.1 %collective-permute-start.16 = (bf16[16,4224]{1,0:T(8,128)(2,1)S(1)}, bf16[16,4224]{1,0:T(8,128)(2,1)S(1)}, u32[]{:S(2)}, u32[]{:S(2)}) collective-permute-start(bf16[16,4224]{1,0:T(8,128)(2,1)S(1)} %get-tuple-element.129), channel_id=1, source_target_pairs={{0,8},{8,0},{16,24},{24,16},{1,9},{9,1},{17,25},{25,17},{2,10},{10... | collective-permute-start | bytes 405512 | tf_op jit(solution)/shard_map/ppermute | solution.py:544
  56.6 12.8 %collective-permute-start.17 = (bf16[16,4224]{1,0:T(8,128)(2,1)S(1)}, bf16[16,4224]{1,0:T(8,128)(2,1)S(1)}, u32[]{:S(2)}, u32[]{:S(2)}) collective-permute-start(bf16[16,4224]{1,0:T(8,128)(2,1)S(1)} %get-tuple-element.130), channel_id=1, source_target_pairs={{0,16},{8,24},{16,0},{24,8},{1,17},{9,25},{17,1},{25,9},{2,18},{10... | collective-permute-start | bytes 405512 | tf_op jit(solution)/shard_map/ppermute | solution.py:544
  58.1 11.2 %collective-permute-start.18 = (bf16[16,4224]{1,0:T(8,128)(2,1)S(1)}, bf16[16,4224]{1,0:T(8,128)(2,1)S(1)}, u32[]{:S(2)}, u32[]{:S(2)}) collective-permute-start(bf16[16,4224]{1,0:T(8,128)(2,1)S(1)} %get-tuple-element.131), channel_id=1, source_target_pairs={{0,24},{8,16},{16,8},{24,0},{1,25},{9,17},{17,9},{25,1},{2,26},{10... | collective-permute-start | bytes 405512 | tf_op jit(solution)/shard_map/ppermute | solution.py:544
  58.2 11.2 %collective-permute-start.13 = (bf16[16,4224]{1,0:T(8,128)(2,1)S(1)}, bf16[16,4224]{1,0:T(8,128)(2,1)S(1)}, u32[]{:S(2)}, u32[]{:S(2)}) collective-permute-start(bf16[16,4224]{1,0:T(8,128)(2,1)S(1)} %get-tuple-element.125), channel_id=1, source_target_pairs={{0,8},{8,0},{16,24},{24,16},{1,9},{9,1},{17,25},{25,17},{2,10},{10... | collective-permute-start | bytes 405512 | tf_op jit(solution)/shard_map/ppermute | solution.py:544
  58.8 10.6 %collective-permute-start.14 = (bf16[16,4224]{1,0:T(8,128)(2,1)S(1)}, bf16[16,4224]{1,0:T(8,128)(2,1)S(1)}, u32[]{:S(2)}, u32[]{:S(2)}) collective-permute-start(bf16[16,4224]{1,0:T(8,128)(2,1)S(1)} %get-tuple-element.126), channel_id=1, source_target_pairs={{0,16},{8,24},{16,0},{24,8},{1,17},{9,25},{17,1},{25,9},{2,18},{10... | collective-permute-start | bytes 405512 | tf_op jit(solution)/shard_map/ppermute | solution.py:544
  60.3 10.0 %collective-permute-start.15 = (bf16[16,4224]{1,0:T(8,128)(2,1)S(1)}, bf16[16,4224]{1,0:T(8,128)(2,1)S(1)}, u32[]{:S(2)}, u32[]{:S(2)}) collective-permute-start(bf16[16,4224]{1,0:T(8,128)(2,1)S(1)} %get-tuple-element.127), channel_id=1, source_target_pairs={{0,24},{8,16},{16,8},{24,0},{1,25},{9,17},{17,9},{25,1},{2,26},{10... | collective-permute-start | bytes 405512 | tf_op jit(solution)/shard_map/ppermute | solution.py:544
  72.4 57.3 %slice-start = ((s8[5767168]{0:T(1024)(128)(4,1)}), s8[4194304]{0:T(1024)(128)(4,1)S(1)}, s32[]{:S(2)}) async-start(s8[5767168]{0:T(1024)(128)(4,1)} %bitcast.23), calls=%async_computation.5 | async-start | bytes 8388608
  72.4 57.3 %slice-start.2 = ((s8[5767168]{0:T(1024)(128)(4,1)}), s8[4194304]{0:T(1024)(128)(4,1)S(1)}, s32[]{:S(2)}) async-start(s8[5767168]{0:T(1024)(128)(4,1)} %bitcast.25), calls=%async_computation.7 | async-start | bytes 8388608
  72.5 57.3 %slice-start.4 = ((s8[5767168]{0:T(1024)(128)(4,1)}), s8[4194304]{0:T(1024)(128)(4,1)S(1)}, s32[]{:S(2)}) async-start(s8[5767168]{0:T(1024)(128)(4,1)} %bitcast.27), calls=%async_computation.9 | async-start | bytes 8388608
  94.1 35.7 %slice-start.1 = ((s8[5767168]{0:T(1024)(128)(4,1)}), s8[1572864]{0:T(1024)(128)(4,1)S(1)}, s32[]{:S(2)}) async-start(s8[5767168]{0:T(1024)(128)(4,1)} %bitcast.23), calls=%async_computation.6 | async-start | bytes 3145728
  94.1 35.7 %slice-start.3 = ((s8[5767168]{0:T(1024)(128)(4,1)}), s8[1572864]{0:T(1024)(128)(4,1)S(1)}, s32[]{:S(2)}) async-start(s8[5767168]{0:T(1024)(128)(4,1)} %bitcast.25), calls=%async_computation.8 | async-start | bytes 3145728
  94.1 35.7 %slice-start.5 = ((s8[5767168]{0:T(1024)(128)(4,1)}), s8[1572864]{0:T(1024)(128)(4,1)S(1)}, s32[]{:S(2)}) async-start(s8[5767168]{0:T(1024)(128)(4,1)} %bitcast.27), calls=%async_computation.10 | async-start | bytes 3145728
  94.4 35.4 %copy-start.1 = (bf16[352,2048]{1,0:T(8,128)(2,1)S(1)}, bf16[352,2048]{1,0:T(8,128)(2,1)}, u32[]{:S(2)}) copy-start(bf16[352,2048]{1,0:T(8,128)(2,1)} %shared_gate_ref.1) | copy-start | bytes 4325380
  94.4 35.4 %copy-start.2 = (bf16[352,2048]{1,0:T(8,128)(2,1)S(1)}, bf16[352,2048]{1,0:T(8,128)(2,1)}, u32[]{:S(2)}) copy-start(bf16[352,2048]{1,0:T(8,128)(2,1)} %shared_up_ref.1) | copy-start | bytes 4325380
  94.4 35.4 %copy-start.3 = (bf16[352,2048]{1,0:T(8,128)(2,1)S(1)}, bf16[352,2048]{1,0:T(8,128)(2,1)}, u32[]{:S(2)}) copy-start(bf16[352,2048]{1,0:T(8,128)(2,1)} %shared_down_ref.1) | copy-start | bytes 4325380
  136.8 16.1 %all-to-all-start.4 = ((bf16[32,24,256]{2,1,0:T(8,128)(2,1)}), bf16[32,24,256]{2,1,0:T(8,128)(2,1)S(1)}, u32[]{:S(2)}, u32[]{:S(2)}) async-start(bf16[32,24,256]{2,1,0:T(8,128)(2,1)} %bitcast.12), calls=%async_computation.4 | async-start | bytes 786432 | tf_op jit(solution)/shard_map/all_to_all | solution.py:532
  (7 other events, 110.8 us)

commit v5 on v4

--- a/solution.py
+++ b/solution.py
@@ -311,9 +311,32 @@
     )(in_hbm(cache), holder, *rows)
 
 
-def local_body(base_ref, unpick_ref, *refs):
-    first_hbm, back_refs = refs[:SHARES], refs[SHARES:-4]
-    out_ref, first_ref, out_mass_ref, sems = refs[-4:]
+def mass_rows(mass):
+    length = mass.shape[0]
+    diagonal = lax.broadcasted_iota(jnp.int32, (length, LAT), 0) == lax.broadcasted_iota(
+        jnp.int32, (length, LAT), 1
+    )
+    line = jnp.sum(jnp.where(diagonal, mass, 0.0), axis=0, keepdims=True)
+    row = lax.broadcasted_iota(jnp.int32, (MASS_ROWS, LAT), 0)
+    tail = jnp.zeros((MASS_ROWS, LAT), jnp.float32)
+    for k, part in enumerate(split_three(line)):
+        tail = jnp.where(row == k, part, tail)
+    return tail.astype(jnp.bfloat16)
+
+
+def mass_column(tail, length):
+    diagonal = lax.broadcasted_iota(jnp.int32, (length, LAT), 0) == lax.broadcasted_iota(
+        jnp.int32, (length, LAT), 1
+    )
+    tail = tail.astype(jnp.float32)
+    line = tail[0:1] + tail[1:2] + tail[2:3]
+    return jnp.sum(jnp.where(diagonal, line, 0.0), axis=1, keepdims=True)
+
+
+def local_body(unpick_ref, *refs):
+    first_hbm, refs = refs[:SHARES], refs[SHARES:]
+    back_refs, refs = refs[: -PIECES - 3], refs[-PIECES - 3 :]
+    out_refs, (first_ref, out_mass_ref, sems) = refs[:PIECES], refs[PIECES:]
     copies = [
         pltpu.make_async_copy(first_hbm[k], first_ref.at[k], sems.at[k]) for k in range(SHARES)
     ]
@@ -328,8 +351,8 @@
         return dot_nn(unpick, jnp.concatenate(rows, axis=0))
 
     extras = [returned(share, slice(HEADS * LAT, None)) for share in range(SHARES)]
-    shares, length = out_ref.shape[0], out_ref.shape[1] - MASS_ROWS
-    per_piece = shares // PIECES
+    cuts, length = out_refs[0].shape[0], out_refs[0].shape[1] - MASS_ROWS
+    each = min(length, requests)
     for h in range(H):
         share, head = divmod(h, HEADS)
         if head == 0:
@@ -347,79 +370,67 @@
         total = first_weight + group_weight
         out = (first_weight * first_ref[share, at, :LAT] + group_weight * group_out) / total
         out = out.astype(jnp.bfloat16)
-        each = min(length, requests)
         for k in range(requests // each):
-            sub, row = divmod(h % 2 * requests + k * each, length)
-            target = (h // 2 ^ base_ref[0]) * per_piece + sub
-            out_ref[target, row : row + each, :] = out[k * each : (k + 1) * each]
+            cut, row = divmod(h % 2 * requests + k * each, length)
+            out_refs[h // 2][cut, row : row + each, :] = out[k * each : (k + 1) * each]
         out_mass_ref[h * requests : (h + 1) * requests, :] = peak + jnp.log(total)
-    diagonal = lax.broadcasted_iota(jnp.int32, (length, LAT), 0) == lax.broadcasted_iota(
-        jnp.int32, (length, LAT), 1
-    )
-    row = lax.broadcasted_iota(jnp.int32, (MASS_ROWS, LAT), 0)
-    for share in range(shares):
-        masses = jnp.where(diagonal, out_mass_ref[share * length : (share + 1) * length, :], 0.0)
-        masses = jnp.sum(masses, axis=0, keepdims=True)
-        tail = jnp.zeros((MASS_ROWS, LAT), jnp.float32)
-        for k, part in enumerate(split_three(masses)):
-            tail = jnp.where(row == k, part, tail)
-        piece, sub = divmod(share, per_piece)
-        target = (piece ^ base_ref[0]) * per_piece + sub
-        out_ref[target, length:, :] = tail.astype(jnp.bfloat16)
-
-
-def local_join(base, unpick, first, back, shares):
+    for piece in range(PIECES):
+        for cut in range(cuts):
+            at = piece * 2 * requests + cut * length
+            out_refs[piece][cut, length:, :] = mass_rows(out_mass_ref[at : at + length, :])
+
+
+def local_join(unpick, first, back, cuts):
     count = SHARES * first[0].shape[0]
+    out = jax.ShapeDtypeStruct((cuts, count // PIECES // cuts + MASS_ROWS, LAT), jnp.bfloat16)
     return call(
         local_body,
-        jax.ShapeDtypeStruct((shares, count // shares + MASS_ROWS, LAT), jnp.bfloat16),
+        (out,) * PIECES,
         10,
         2 * unpick.shape[0] * unpick.shape[1] * H * LAT,
         4 * count * LAT,
-        in_specs=[pl.BlockSpec(memory_space=pltpu.SMEM), VMEM]
-        + [HBM] * SHARES
-        + [VMEM] * len(back),
-        out_specs=VMEM,
+        in_specs=[VMEM] + [HBM] * SHARES + [VMEM] * len(back),
+        out_specs=(VMEM,) * PIECES,
         scratch_shapes=[
             pltpu.VMEM((SHARES,) + first[0].shape, jnp.float32),
             pltpu.VMEM((count, 1), jnp.float32),
             pltpu.SemaphoreType.DMA((SHARES,)),
         ],
-    )(base, unpick, *[in_hbm(x) for x in first], *back)
-
-
-def join_body(parts_ref, out_ref):
-    sources, copies, length = parts_ref.shape[0], out_ref.shape[0], out_ref.shape[1]
-    diagonal = lax.broadcasted_iota(jnp.int32, (length, LAT), 0) == lax.broadcasted_iota(
-        jnp.int32, (length, LAT), 1
-    )
-    masses = []
-    for s in range(sources):
-        tail = parts_ref[s, length:, :].astype(jnp.float32)
-        mass = tail[0:1] + tail[1:2] + tail[2:3]
-        masses.append(jnp.sum(jnp.where(diagonal, mass, 0.0), axis=1, keepdims=True))
+    )(unpick, *[in_hbm(x) for x in first], *back)
+
+
+def join_body(further, *refs):
+    parts_refs, out_ref = refs[:-1], refs[-1]
+    length = parts_refs[0].shape[0] - MASS_ROWS
+    masses = [mass_column(ref[length:, :], length) for ref in parts_refs]
     peak = functools.reduce(jnp.maximum, masses)
     scales = [jnp.exp(mass - peak) for mass in masses]
     total = functools.reduce(jnp.add, scales)
     out = functools.reduce(
         jnp.add,
-        [scales[s] * parts_ref[s, :length, :].astype(jnp.float32) for s in range(sources)],
+        [scale * ref[:length, :].astype(jnp.float32) for scale, ref in zip(scales, parts_refs)],
     )
     out = (out / total).astype(jnp.bfloat16)
-    for c in range(copies):
-        out_ref[c] = out
-
-
-def join(parts):
-    sources, rows, _ = parts.shape
-    rows -= MASS_ROWS
-    return call(
-        join_body,
-        jax.ShapeDtypeStruct((sources, rows, LAT), jnp.bfloat16),
+    if further:
+        out_ref[:length, :] = out
+        out_ref[length:, :] = mass_rows(peak + jnp.log(total))
+    else:
+        for c in range(out_ref.shape[0]):
+            out_ref[c] = out
+
+
+def join(parts, copies=0):
+    rows = parts[0].shape[0]
+    shape = (copies, rows - MASS_ROWS, LAT) if copies else (rows, LAT)
+    return call(
+        functools.partial(join_body, not copies),
+        jax.ShapeDtypeStruct(shape, jnp.bfloat16),
         6,
-        3e10,
-        4 * sources * rows * LAT,
-    )(parts)
+        3e10 if copies else 2 * len(parts) * rows * LAT,
+        4 * len(parts) * rows * LAT,
+        in_specs=[VMEM] * len(parts),
+        out_specs=VMEM,
+    )(*parts)
 
 
 def output_body(rows_ref, weight_ref, hidden_ref, out_ref, copies_ref):
@@ -643,12 +654,10 @@
         .astype(jnp.float32)
     )
     if tensors == PIECES:
-        base = tensor_index
         pieces = [projected] + [turn(projected, k) for k in (1, 2, 3)]
         pieces.append(turn(projected, 4))
         pieces += [turn(pieces[4], k) for k in (1, 2, 3)]
     else:
-        base = jnp.zeros((), jnp.int32)
         copies = jnp.broadcast_to(projected[None], (tensors,) + projected.shape)
         queries = gather_pieces(exchange(copies, "tensor"))
         pieces = [queries[k] for k in range(PIECES)]
@@ -700,8 +709,15 @@
     back[1] = swap_owners(answered)
     first.append(own_attention(far, suffix_holder, root_columns, suffix_rows))
     back, gain = lax.optimization_barrier((back, mixture_gain[None]))
-    parts = local_join(base[None], unpick, first, sum(back, []), tensors)
-    attention = exchange(join(exchange(parts, "tensor")), "tensor")
+    parts = local_join(unpick, first, sum(back, []), tensors // PIECES)
+    if tensors == PIECES:
+        parts = [part[0] for part in parts]
+        crossing = join([parts[4]] + [turn(parts[4 + k], k) for k in (1, 2, 3)])
+        parts = [parts[0]] + [turn(parts[k], k) for k in (1, 2, 3)] + [turn(crossing, 4)]
+    else:
+        parts = exchange(jnp.concatenate(parts, axis=0), "tensor")
+        parts = [parts[k] for k in range(tensors)]
+    attention = exchange(join(parts, tensors), "tensor")
     mid, copies = output_projection(
         attention.reshape(-1, LAT), out_weight, hidden, owners // 2 * tensors
     )

time: 154 us -> 145 us (0.942)
  blocking collectives: 55.6 us -> 32.2 us
  starting transfers between devices: 24.9 us -> 34.2 us
  waiting for transfers between devices: 22.8 us -> 27.6 us
    all_to_all x3 -> x2, blocking collectives: 53.4 us -> 29.8 us  [exchange(): return lax.all_to_all(x, axis, 0, 0, tiled=True)]
    ppermute x7 -> x14, starting transfers between devices: 7.14 us -> 16.4 us  [turn(): return lax.ppermute(x, 'tensor', [(i, i ^ k) for i in range(count)])]
    ppermute x7 -> x14, waiting for transfers between devices: 1.22 us -> 6.02 us  [turn(): return lax.ppermute(x, 'tensor', [(i, i ^ k) for i in range(count)])]
  transfers between devices with their start and end apart: 21 -> 28, of which waited for: 7 -> 10; matrix products, arithmetic and copies ran while one was open for 3% -> 3% of each run, Pallas kernels for 15% -> 16%
where the time goes in v5:
time: 145 us
  Pallas kernels  42.9 us (30%)
  starting transfers between devices  34.2 us (24%)
  blocking collectives  32.2 us (22%)
  waiting for transfers between devices  27.6 us (19%)
  local copies, waits for them, and re-layouts  4.72 us (3%)
  other arithmetic  2.42 us (2%)
    all_to_all x2, blocking collectives, exchange(): return lax.all_to_all(x, axis, 0, 0, tiled=True)  29.8 us
    pallas_call x2, Pallas kernels, own_attention(): call(own_body, pltpu.HBM((count, LAT + LANES), jnp.float32), 44, 2 * coun...  18.1 us
    all_to_all x2, waiting for transfers between devices, exchange(): return lax.all_to_all(x, axis, 0, 0, tiled=True)  17.9 us
    ppermute x14, starting transfers between devices, turn(): return lax.ppermute(x, 'tensor', [(i, i ^ k) for i in range(count)])  16.4 us
    all_to_all x2, starting transfers between devices, exchange(): return lax.all_to_all(x, axis, 0, 0, tiled=True)  9.85 us
    pallas_call x2, Pallas kernels, group_attention(): call(functools.partial(group_body, owners), (out,) * owners, 40, 2 * owne...  9.28 us
    ppermute x12, starting transfers between devices, swap_owners(): out[k] = lax.ppermute(arrays[k], OWNER, [(i, i ^ k) for i in range(count)])  7.94 us
    pallas_call x1, Pallas kernels, expert(): call(expert_body, jax.ShapeDtypeStruct((owners, PIECES, slots + requests...  6.86 us
  transfers between devices with their start and end apart: 28, of which 10 were waited for; matrix products, arithmetic and copies ran while one was open for 3% of the time, Pallas kernels for 16%

profile of v5, /device:TPU:0, one launch (start us, length us, event | category | flops | bytes accessed | tf_op | source)
XLA Modules:
  0.0 144.6 jit_solution(12639173411843529018)
XLA Ops:
  0.0 1.4 broadcast_in_dim.228
  1.4 7.3 %all-to-all-start = ((bf16[8,32,256]{2,1,0:T(8,128)(2,1)}), bf16[8,32,256]{2,1,0:T(8,128)(2,1)S(1)}, u32[]{:S(2)}, u32[]{:S(2)}) async-start(bf16[8,32,256]{2,1,0:T(8,128)(2,1)} %broadcast_in_dim.228), calls=%async_computation | async-start | bytes 262144 | tf_op jit(solution)/shard_map/all_to_all | solution.py:543
  10.2 5.8 %all-to-all-done.rows_ref = bf16[8,32,256]{2,1,0:T(8,128)(2,1)S(1)} async-done(((bf16[8,32,256]{2,1,0:T(8,128)(2,1)}), bf16[8,32,256]{2,1,0:T(8,128)(2,1)S(1)}, u32[]{:S(2)}, u32[]{:S(2)}) %all-to-all-start) | async-done | bytes 131104 | tf_op jit(solution)/shard_map/all_to_all | solution.py:543
  16.0 3.4 %shard_map.190.refs_0_ = bf16[32,1152]{1,0:T(8,128)(2,1)S(1)} custom-call(bf16[8,32,256]{2,1,0:T(8,128)(2,1)S(1)} %all-to-all-done.rows_ref, bf16[1,2048]{1,0:T(2,128)(2,1)S(1)} %broadcast_in_dim.229.gain_ref, bf16[1152,2048]{1,0:T(8,128)(2,1)} %weight_hbm.1), custom_call_target="tpu_custom_call" | custom-call | flops 150994944 | bytes 4718592 | tf_op jit(solution)/shard_map/pallas_call | solution.py:101
  19.9 1.3 collective-permute-start.2
  21.6 1.8 %collective-permute-start = (bf16[32,1152]{1,0:T(8,128)(2,1)S(1)}, bf16[32,1152]{1,0:T(8,128)(2,1)S(1)}, u32[]{:S(2)}, u32[]{:S(2)}) collective-permute-start(bf16[32,1152]{1,0:T(8,128)(2,1)S(1)} %shard_map.190.refs_0_), channel_id=1, source_target_pairs={{0,1},{1,0},{2,3},{3,2},{4,5},{5,4},{6,7},{7,6},{8,9},{9,8},{10,11... | collective-permute-start | bytes 221192 | tf_op jit(solution)/shard_map/ppermute | solution.py:548
  25.2 1.0 collective-permute-start.6
  26.9 1.6 %collective-permute-start.8 = (bf16[16,4736]{1,0:T(8,128)(2,1)S(1)}, bf16[16,4736]{1,0:T(8,128)(2,1)S(1)}, u32[]{:S(2)}, u32[]{:S(2)}) collective-permute-start(bf16[16,4736]{1,0:T(8,128)(2,1)S(1)} %get-tuple-element.100), channel_id=1, source_target_pairs={{0,16},{8,24},{16,0},{24,8},{1,17},{9,25},{17,1},{25,9},{2,18},{10... | collective-permute-start | bytes 454664 | tf_op jit(solution)/shard_map/ppermute | solution.py:555
  28.7 1.4 collective-permute-start.5
  31.3 9.0 %shard_map.191.refs_0_ = f32[256,640]{1,0:T(8,128)} custom-call(s32[1,2048]{1,0:T(1,128)S(1)} %select_n.114.holder_ref, bf16[576,4096]{1,0:T(8,128)(2,1)} %bitcast.54, bf16[2048,576]{1,0:T(8,128)(2,1)} %bitcast.56, bf16[32,1152]{1,0:T(8,128)(2,1)S(1)} %shard_map.190.refs_0_, bf16[32,1152]{1,0:T(8,128)(2,1)S(1)} %collective-permute-done.refs_1_, ...), custom_call_target="tpu_custom_call" | custom-call | flops 2852126720 | bytes 7077888 | tf_op jit(solution)/shard_map/pallas_call | solution.py:215
  42.3 1.6 %collective-permute-start.11 = (bf16[16,4736]{1,0:T(8,128)(2,1)S(1)}, bf16[16,4736]{1,0:T(8,128)(2,1)S(1)}, u32[]{:S(2)}, u32[]{:S(2)}) collective-permute-start(bf16[16,4736]{1,0:T(8,128)(2,1)S(1)} %get-tuple-element.108), channel_id=1, source_target_pairs={{0,16},{8,24},{16,0},{24,8},{1,17},{9,25},{17,1},{25,9},{2,18},{10... | collective-permute-start | bytes 454664 | tf_op jit(solution)/shard_map/ppermute | solution.py:555
  44.2 4.6 %shard_map.194 = (bf16[16,4224]{1,0:T(8,128)(2,1)S(1)}, bf16[16,4224]{1,0:T(8,128)(2,1)S(1)}, bf16[16,4224]{1,0:T(8,128)(2,1)S(1)}, bf16[16,4224]{1,0:T(8,128)(2,1)S(1)}) custom-call(bf16[12,576,128]{2,1,0:T(8,128)(2,1)} %bitcast.58, f32[1,1536]{1,0:T(1,128)S(1)} %bitcast.41, bf16[16,4736]{1,0:T(8,128)(2,1)S(1)} %get-tuple-element.110.refs_0_, ...), custom_call_target="tpu_custom_call" | custom-call | flops 1711276032 | bytes 1769472 | tf_op jit(solution)/shard_map/pallas_call | solution.py:298
  49.1 2.3 %collective-permute-done.12.refs_3_ = bf16[16,4736]{1,0:T(8,128)(2,1)S(1)} collective-permute-done((bf16[16,4736]{1,0:T(8,128)(2,1)S(1)}, bf16[16,4736]{1,0:T(8,128)(2,1)S(1)}, u32[]{:S(2)}, u32[]{:S(2)}) %collective-permute-start.12) | collective-permute-done | bytes 151584 | tf_op jit(solution)/shard_map/ppermute | solution.py:555
  51.5 4.7 %shard_map.195 = (bf16[16,4224]{1,0:T(8,128)(2,1)S(1)}, bf16[16,4224]{1,0:T(8,128)(2,1)S(1)}, bf16[16,4224]{1,0:T(8,128)(2,1)S(1)}, bf16[16,4224]{1,0:T(8,128)(2,1)S(1)}) custom-call(bf16[12,576,128]{2,1,0:T(8,128)(2,1)} %bitcast.59, f32[1,1536]{1,0:T(1,128)S(1)} %bitcast.42, bf16[16,4736]{1,0:T(8,128)(2,1)S(1)} %get-tuple-element.118.refs_0_, ...), custom_call_target="tpu_custom_call" | custom-call | flops 1711276032 | bytes 1769472 | tf_op jit(solution)/shard_map/pallas_call | solution.py:298
  56.6 1.6 %collective-permute-start.17 = (bf16[16,4224]{1,0:T(8,128)(2,1)S(1)}, bf16[16,4224]{1,0:T(8,128)(2,1)S(1)}, u32[]{:S(2)}, u32[]{:S(2)}) collective-permute-start(bf16[16,4224]{1,0:T(8,128)(2,1)S(1)} %get-tuple-element.138), channel_id=1, source_target_pairs={{0,16},{8,24},{16,0},{24,8},{1,17},{9,25},{17,1},{25,9},{2,18},{10... | collective-permute-start | bytes 405512 | tf_op jit(solution)/shard_map/ppermute | solution.py:555
  58.8 1.5 %collective-permute-start.14 = (bf16[16,4224]{1,0:T(8,128)(2,1)S(1)}, bf16[16,4224]{1,0:T(8,128)(2,1)S(1)}, u32[]{:S(2)}, u32[]{:S(2)}) collective-permute-start(bf16[16,4224]{1,0:T(8,128)(2,1)S(1)} %get-tuple-element.134), channel_id=1, source_target_pairs={{0,16},{8,24},{16,0},{24,8},{1,17},{9,25},{17,1},{25,9},{2,18},{10... | collective-permute-start | bytes 405512 | tf_op jit(solution)/shard_map/ppermute | solution.py:555
  60.3 9.0 %shard_map.196.refs_1_ = f32[256,640]{1,0:T(8,128)} custom-call(s32[1,2048]{1,0:T(1,128)S(1)} %select_n.114.holder_ref, bf16[576,4096]{1,0:T(8,128)(2,1)} %bitcast.55, bf16[2048,576]{1,0:T(8,128)(2,1)} %bitcast.57, bf16[32,1152]{1,0:T(8,128)(2,1)S(1)} %collective-permute-done.3.refs_0_, bf16[32,1152]{1,0:T(8,128)(2,1)S(1)} %collective-permute-done.4.refs_1_, ...), custom_call_target="tpu_custom_call" | custom-call | flops 2852126720 | bytes 7077888 | tf_op jit(solution)/shard_map/pallas_call | solution.py:215
  69.4 0.9 collective-permute-done.15.refs_5_
  70.3 2.1 %shard_map.197 = (bf16[1,72,512]{2,1,0:T(8,128)(2,1)S(1)}, bf16[1,72,512]{2,1,0:T(8,128)(2,1)S(1)}, bf16[1,72,512]{2,1,0:T(8,128)(2,1)S(1)}, bf16[1,72,512]{2,1,...) custom-call(bf16[32,64]{1,0:T(8,128)(2,1)S(1)} %and_convert_fusion.u, ...), custom_call_target="tpu_custom_call" | custom-call | flops 33554432 | bytes 1048576 | tf_op jit(solution)/shard_map/pallas_call | solution.py:386
  72.4 1.3 collective-permute-start.22
  74.0 2.0 %collective-permute-start.24 = (bf16[72,512]{1,0:T(8,128)(2,1)S(1)}, bf16[72,512]{1,0:T(8,128)(2,1)S(1)}, u32[]{:S(2)}, u32[]{:S(2)}) collective-permute-start(bf16[72,512]{1,0:T(8,128)(2,1)S(1)} %bitcast.47), channel_id=1, source_target_pairs={{0,3},{1,2},{2,1},{3,0},{4,7},{5,6},{6,5},{7,4},{8,11},{9,10},{10,... | collective-permute-start | bytes 221192 | tf_op jit(solution)/shard_map/ppermute | solution.py:548
  76.0 1.2 collective-permute-start.19
  77.5 2.0 %collective-permute-start.21 = (bf16[72,512]{1,0:T(8,128)(2,1)S(1)}, bf16[72,512]{1,0:T(8,128)(2,1)S(1)}, u32[]{:S(2)}, u32[]{:S(2)}) collective-permute-start(bf16[72,512]{1,0:T(8,128)(2,1)S(1)} %bitcast.44), channel_id=1, source_target_pairs={{0,3},{1,2},{2,1},{3,0},{4,7},{5,6},{6,5},{7,4},{8,11},{9,10},{10,... | collective-permute-start | bytes 221192 | tf_op jit(solution)/shard_map/ppermute | solution.py:548
  80.6 2.2 %collective-permute-start.25 = (bf16[72,512]{1,0:T(8,128)(2,1)S(1)}, bf16[72,512]{1,0:T(8,128)(2,1)S(1)}, u32[]{:S(2)}, u32[]{:S(2)}) collective-permute-start(bf16[72,512]{1,0:T(8,128)(2,1)S(1)} %shard_map.198), channel_id=1, source_target_pairs={{0,4},{1,5},{2,6},{3,7},{4,0},{5,1},{6,2},{7,3},{8,12},{9,13},{10,... | collective-permute-start | bytes 221192 | tf_op jit(solution)/shard_map/ppermute | solution.py:548
  83.1 3.6 %collective-permute-done.25.refs_4_ = bf16[72,512]{1,0:T(8,128)(2,1)S(1)} collective-permute-done((bf16[72,512]{1,0:T(8,128)(2,1)S(1)}, bf16[72,512]{1,0:T(8,128)(2,1)S(1)}, u32[]{:S(2)}, u32[]{:S(2)}) %collective-permute-start.25) | collective-permute-done | bytes 73760 | tf_op jit(solution)/shard_map/ppermute | solution.py:548
  87.0 16.8 %all_to_all.20 = bf16[8,64,512]{2,1,0:T(8,128)(2,1)S(1)} all-to-all(bf16[8,64,512]{2,1,0:T(8,128)(2,1)S(1)} %shard_map.199), channel_id=1, replica_groups=mesh['pair'=2,'core'=2,'tensor'=8] {'tensor'}, dimensions={0} | all-to-all | bytes 1048576 | tf_op jit(solution)/shard_map/all_to_all | solution.py:543
  103.8 1.3 shard_map.200
  105.2 13.0 %all_to_all.21 = bf16[16,32,256]{2,1,0:T(8,128)(2,1)S(1)} all-to-all(bf16[16,32,256]{2,1,0:T(8,128)(2,1)S(1)} %get-tuple-element.156), channel_id=1, replica_groups=mesh['pair'=2,'core'=2,'tensor'=8] {'pair','tensor'}, dimensions={0} | all-to-all | bytes 524288 | tf_op jit(solution)/shard_map/all_to_all | solution.py:543
  118.2 2.4 %all_gather.3 = bf16[2,2,8,32,256]{4,3,2,1,0:T(8,128)(2,1)S(1)} all-gather(bf16[1,2,8,32,256]{4,3,2,1,0:T(8,128)(2,1)S(1)} %bitcast.50), channel_id=1, replica_groups=mesh['pair'=2,'core'=2,'tensor'=8] {'core'}, dimensions={0}, use_global_device_ids=true | all-gather | bytes 786432 | tf_op jit(solution)/shard_map/all_gather | solution.py:726
  120.7 6.9 %shard_map.201 = bf16[4,8,24,256]{3,2,1,0:T(8,128)(2,1)} custom-call(bf16[96,128]{1,0:T(8,128)(2,1)S(1)} %add_convert_fusion.pick_ref, bf16[4,8,32,256]{3,2,1,0:T(8,128)(2,1)S(1)} %bitcast.37, bf16[1,2048]{1,0:T(2,128)(2,1)S(1)} %broadcast_in_dim.249.gain_ref, bf16[352,2048]{1,0:T(8,128)(2,1)S(1)} %copy-done.1, bf16[352,2048]{1,0:T(8,128)(2,1)S(1)} %copy-done.2, ...), custom_call_target="tpu_custom_call" | custom-call | flops 1660944384 | bytes 17301504 | tf_op jit(solution)/shard_map/pallas_call | solution.py:508
  127.6 2.6 %all-to-all-start.3 = ((bf16[32,24,256]{2,1,0:T(8,128)(2,1)}), bf16[32,24,256]{2,1,0:T(8,128)(2,1)S(1)}, u32[]{:S(2)}, u32[]{:S(2)}) async-start(bf16[32,24,256]{2,1,0:T(8,128)(2,1)} %bitcast.19), calls=%async_computation.3 | async-start | bytes 786432 | tf_op jit(solution)/shard_map/all_to_all | solution.py:543
  131.6 12.1 %all-to-all-done.3 = bf16[32,24,256]{2,1,0:T(8,128)(2,1)S(1)} async-done(((bf16[32,24,256]{2,1,0:T(8,128)(2,1)}), bf16[32,24,256]{2,1,0:T(8,128)(2,1)S(1)}, u32[]{:S(2)}, u32[]{:S(2)}) %all-to-all-start.3) | async-done | bytes 393248 | tf_op jit(solution)/shard_map/all_to_all | solution.py:543
  (152 shorter events, 14.3 us)
Async XLA Ops:
  1.4 14.6 %all-to-all-start = ((bf16[8,32,256]{2,1,0:T(8,128)(2,1)}), bf16[8,32,256]{2,1,0:T(8,128)(2,1)S(1)}, u32[]{:S(2)}, u32[]{:S(2)}) async-start(bf16[8,32,256]{2,1,0:T(8,128)(2,1)} %broadcast_in_dim.228), calls=%async_computation | async-start | bytes 262144 | tf_op jit(solution)/shard_map/all_to_all | solution.py:543
  19.4 5.8 %collective-permute-start.3 = (bf16[32,1152]{1,0:T(8,128)(2,1)S(1)}, bf16[32,1152]{1,0:T(8,128)(2,1)S(1)}, u32[]{:S(2)}, u32[]{:S(2)}) collective-permute-start(bf16[32,1152]{1,0:T(8,128)(2,1)S(1)} %shard_map.190.refs_0_), channel_id=1, source_target_pairs={{0,4},{1,5},{2,6},{3,7},{4,0},{5,1},{6,2},{7,3},{8,12},{9,13},{10,... | collective-permute-start | bytes 221192 | tf_op jit(solution)/shard_map/ppermute | solution.py:548
  19.9 6.6 %collective-permute-start.2 = (bf16[32,1152]{1,0:T(8,128)(2,1)S(1)}, bf16[32,1152]{1,0:T(8,128)(2,1)S(1)}, u32[]{:S(2)}, u32[]{:S(2)}) collective-permute-start(bf16[32,1152]{1,0:T(8,128)(2,1)S(1)} %shard_map.190.refs_0_), channel_id=1, source_target_pairs={{0,3},{1,2},{2,1},{3,0},{4,7},{5,6},{6,5},{7,4},{8,11},{9,10},{10,... | collective-permute-start | bytes 221192 | tf_op jit(solution)/shard_map/ppermute | solution.py:548
  21.1 5.3 %collective-permute-start.1 = (bf16[32,1152]{1,0:T(8,128)(2,1)S(1)}, bf16[32,1152]{1,0:T(8,128)(2,1)S(1)}, u32[]{:S(2)}, u32[]{:S(2)}) collective-permute-start(bf16[32,1152]{1,0:T(8,128)(2,1)S(1)} %shard_map.190.refs_0_), channel_id=1, source_target_pairs={{0,2},{1,3},{2,0},{3,1},{4,6},{5,7},{6,4},{7,5},{8,10},{9,11},{10,... | collective-permute-start | bytes 221192 | tf_op jit(solution)/shard_map/ppermute | solution.py:548
  21.6 4.9 %collective-permute-start = (bf16[32,1152]{1,0:T(8,128)(2,1)S(1)}, bf16[32,1152]{1,0:T(8,128)(2,1)S(1)}, u32[]{:S(2)}, u32[]{:S(2)}) collective-permute-start(bf16[32,1152]{1,0:T(8,128)(2,1)S(1)} %shard_map.190.refs_0_), channel_id=1, source_target_pairs={{0,1},{1,0},{2,3},{3,2},{4,5},{5,4},{6,7},{7,6},{8,9},{9,8},{10,11... | collective-permute-start | bytes 221192 | tf_op jit(solution)/shard_map/ppermute | solution.py:548
  25.2 5.3 %collective-permute-start.6 = (bf16[32,1152]{1,0:T(8,128)(2,1)S(1)}, bf16[32,1152]{1,0:T(8,128)(2,1)S(1)}, u32[]{:S(2)}, u32[]{:S(2)}) collective-permute-start(bf16[32,1152]{1,0:T(8,128)(2,1)S(1)} %collective-permute-done.3.refs_0_), channel_id=1, source_target_pairs={{0,3},{1,2},{2,1},{3,0},{4,7},{5,6},{6,5},{7,4},{8,11},{9,10},{10,... | collective-permute-start | bytes 221192 | tf_op jit(solution)/shard_map/ppermute | solution.py:548
  26.8 14.1 %collective-permute-start.7 = (bf16[16,4736]{1,0:T(8,128)(2,1)S(1)}, bf16[16,4736]{1,0:T(8,128)(2,1)S(1)}, u32[]{:S(2)}, u32[]{:S(2)}) collective-permute-start(bf16[16,4736]{1,0:T(8,128)(2,1)S(1)} %get-tuple-element.99), channel_id=1, source_target_pairs={{0,8},{8,0},{16,24},{24,16},{1,9},{9,1},{17,25},{25,17},{2,10},{10... | collective-permute-start | bytes 454664 | tf_op jit(solution)/shard_map/ppermute | solution.py:555
  26.9 14.3 %collective-permute-start.8 = (bf16[16,4736]{1,0:T(8,128)(2,1)S(1)}, bf16[16,4736]{1,0:T(8,128)(2,1)S(1)}, u32[]{:S(2)}, u32[]{:S(2)}) collective-permute-start(bf16[16,4736]{1,0:T(8,128)(2,1)S(1)} %get-tuple-element.100), channel_id=1, source_target_pairs={{0,16},{8,24},{16,0},{24,8},{1,17},{9,25},{17,1},{25,9},{2,18},{10... | collective-permute-start | bytes 454664 | tf_op jit(solution)/shard_map/ppermute | solution.py:555
  28.5 13.0 %collective-permute-start.9 = (bf16[16,4736]{1,0:T(8,128)(2,1)S(1)}, bf16[16,4736]{1,0:T(8,128)(2,1)S(1)}, u32[]{:S(2)}, u32[]{:S(2)}) collective-permute-start(bf16[16,4736]{1,0:T(8,128)(2,1)S(1)} %get-tuple-element.101), channel_id=1, source_target_pairs={{0,24},{8,16},{16,8},{24,0},{1,25},{9,17},{17,9},{25,1},{2,26},{10... | collective-permute-start | bytes 454664 | tf_op jit(solution)/shard_map/ppermute | solution.py:555
  28.7 11.9 %collective-permute-start.5 = (bf16[32,1152]{1,0:T(8,128)(2,1)S(1)}, bf16[32,1152]{1,0:T(8,128)(2,1)S(1)}, u32[]{:S(2)}, u32[]{:S(2)}) collective-permute-start(bf16[32,1152]{1,0:T(8,128)(2,1)S(1)} %collective-permute-done.3.refs_0_), channel_id=1, source_target_pairs={{0,2},{1,3},{2,0},{3,1},{4,6},{5,7},{6,4},{7,5},{8,10},{9,11},{10,... | collective-permute-start | bytes 221192 | tf_op jit(solution)/shard_map/ppermute | solution.py:548
  30.5 10.1 %collective-permute-start.4 = (bf16[32,1152]{1,0:T(8,128)(2,1)S(1)}, bf16[32,1152]{1,0:T(8,128)(2,1)S(1)}, u32[]{:S(2)}, u32[]{:S(2)}) collective-permute-start(bf16[32,1152]{1,0:T(8,128)(2,1)S(1)} %collective-permute-done.3.refs_0_), channel_id=1, source_target_pairs={{0,1},{1,0},{2,3},{3,2},{4,5},{5,4},{6,7},{7,6},{8,9},{9,8},{10,11... | collective-permute-start | bytes 221192 | tf_op jit(solution)/shard_map/ppermute | solution.py:548
  42.3 6.5 %collective-permute-start.10 = (bf16[16,4736]{1,0:T(8,128)(2,1)S(1)}, bf16[16,4736]{1,0:T(8,128)(2,1)S(1)}, u32[]{:S(2)}, u32[]{:S(2)}) collective-permute-start(bf16[16,4736]{1,0:T(8,128)(2,1)S(1)} %get-tuple-element.107), channel_id=1, source_target_pairs={{0,8},{8,0},{16,24},{24,16},{1,9},{9,1},{17,25},{25,17},{2,10},{10... | collective-permute-start | bytes 454664 | tf_op jit(solution)/shard_map/ppermute | solution.py:555
  42.3 6.8 %collective-permute-start.11 = (bf16[16,4736]{1,0:T(8,128)(2,1)S(1)}, bf16[16,4736]{1,0:T(8,128)(2,1)S(1)}, u32[]{:S(2)}, u32[]{:S(2)}) collective-permute-start(bf16[16,4736]{1,0:T(8,128)(2,1)S(1)} %get-tuple-element.108), channel_id=1, source_target_pairs={{0,16},{8,24},{16,0},{24,8},{1,17},{9,25},{17,1},{25,9},{2,18},{10... | collective-permute-start | bytes 454664 | tf_op jit(solution)/shard_map/ppermute | solution.py:555
  43.9 7.6 %collective-permute-start.12 = (bf16[16,4736]{1,0:T(8,128)(2,1)S(1)}, bf16[16,4736]{1,0:T(8,128)(2,1)S(1)}, u32[]{:S(2)}, u32[]{:S(2)}) collective-permute-start(bf16[16,4736]{1,0:T(8,128)(2,1)S(1)} %get-tuple-element.109), channel_id=1, source_target_pairs={{0,24},{8,16},{16,8},{24,0},{1,25},{9,17},{17,9},{25,1},{2,26},{10... | collective-permute-start | bytes 454664 | tf_op jit(solution)/shard_map/ppermute | solution.py:555
  56.2 4.1 %collective-permute-start.16 = (bf16[16,4224]{1,0:T(8,128)(2,1)S(1)}, bf16[16,4224]{1,0:T(8,128)(2,1)S(1)}, u32[]{:S(2)}, u32[]{:S(2)}) collective-permute-start(bf16[16,4224]{1,0:T(8,128)(2,1)S(1)} %get-tuple-element.137), channel_id=1, source_target_pairs={{0,8},{8,0},{16,24},{24,16},{1,9},{9,1},{17,25},{25,17},{2,10},{10... | collective-permute-start | bytes 405512 | tf_op jit(solution)/shard_map/ppermute | solution.py:555
  56.6 12.8 %collective-permute-start.17 = (bf16[16,4224]{1,0:T(8,128)(2,1)S(1)}, bf16[16,4224]{1,0:T(8,128)(2,1)S(1)}, u32[]{:S(2)}, u32[]{:S(2)}) collective-permute-start(bf16[16,4224]{1,0:T(8,128)(2,1)S(1)} %get-tuple-element.138), channel_id=1, source_target_pairs={{0,16},{8,24},{16,0},{24,8},{1,17},{9,25},{17,1},{25,9},{2,18},{10... | collective-permute-start | bytes 405512 | tf_op jit(solution)/shard_map/ppermute | solution.py:555
  58.2 11.2 %collective-permute-start.18 = (bf16[16,4224]{1,0:T(8,128)(2,1)S(1)}, bf16[16,4224]{1,0:T(8,128)(2,1)S(1)}, u32[]{:S(2)}, u32[]{:S(2)}) collective-permute-start(bf16[16,4224]{1,0:T(8,128)(2,1)S(1)} %get-tuple-element.139), channel_id=1, source_target_pairs={{0,24},{8,16},{16,8},{24,0},{1,25},{9,17},{17,9},{25,1},{2,26},{10... | collective-permute-start | bytes 405512 | tf_op jit(solution)/shard_map/ppermute | solution.py:555
  58.2 11.2 %collective-permute-start.13 = (bf16[16,4224]{1,0:T(8,128)(2,1)S(1)}, bf16[16,4224]{1,0:T(8,128)(2,1)S(1)}, u32[]{:S(2)}, u32[]{:S(2)}) collective-permute-start(bf16[16,4224]{1,0:T(8,128)(2,1)S(1)} %get-tuple-element.133), channel_id=1, source_target_pairs={{0,8},{8,0},{16,24},{24,16},{1,9},{9,1},{17,25},{25,17},{2,10},{10... | collective-permute-start | bytes 405512 | tf_op jit(solution)/shard_map/ppermute | solution.py:555
  58.8 10.6 %collective-permute-start.14 = (bf16[16,4224]{1,0:T(8,128)(2,1)S(1)}, bf16[16,4224]{1,0:T(8,128)(2,1)S(1)}, u32[]{:S(2)}, u32[]{:S(2)}) collective-permute-start(bf16[16,4224]{1,0:T(8,128)(2,1)S(1)} %get-tuple-element.134), channel_id=1, source_target_pairs={{0,16},{8,24},{16,0},{24,8},{1,17},{9,25},{17,1},{25,9},{2,18},{10... | collective-permute-start | bytes 405512 | tf_op jit(solution)/shard_map/ppermute | solution.py:555
  60.3 10.0 %collective-permute-start.15 = (bf16[16,4224]{1,0:T(8,128)(2,1)S(1)}, bf16[16,4224]{1,0:T(8,128)(2,1)S(1)}, u32[]{:S(2)}, u32[]{:S(2)}) collective-permute-start(bf16[16,4224]{1,0:T(8,128)(2,1)S(1)} %get-tuple-element.135), channel_id=1, source_target_pairs={{0,24},{8,16},{16,8},{24,0},{1,25},{9,17},{17,9},{25,1},{2,26},{10... | collective-permute-start | bytes 405512 | tf_op jit(solution)/shard_map/ppermute | solution.py:555
  72.4 5.1 %collective-permute-start.22 = (bf16[72,512]{1,0:T(8,128)(2,1)S(1)}, bf16[72,512]{1,0:T(8,128)(2,1)S(1)}, u32[]{:S(2)}, u32[]{:S(2)}) collective-permute-start(bf16[72,512]{1,0:T(8,128)(2,1)S(1)} %bitcast.49), channel_id=1, source_target_pairs={{0,1},{1,0},{2,3},{3,2},{4,5},{5,4},{6,7},{7,6},{8,9},{9,8},{10,11... | collective-permute-start | bytes 221192 | tf_op jit(solution)/shard_map/ppermute | solution.py:548
  73.7 5.8 %collective-permute-start.23 = (bf16[72,512]{1,0:T(8,128)(2,1)S(1)}, bf16[72,512]{1,0:T(8,128)(2,1)S(1)}, u32[]{:S(2)}, u32[]{:S(2)}) collective-permute-start(bf16[72,512]{1,0:T(8,128)(2,1)S(1)} %bitcast.48), channel_id=1, source_target_pairs={{0,2},{1,3},{2,0},{3,1},{4,6},{5,7},{6,4},{7,5},{8,10},{9,11},{10,... | collective-permute-start | bytes 221192 | tf_op jit(solution)/shard_map/ppermute | solution.py:548
  74.0 6.4 %collective-permute-start.24 = (bf16[72,512]{1,0:T(8,128)(2,1)S(1)}, bf16[72,512]{1,0:T(8,128)(2,1)S(1)}, u32[]{:S(2)}, u32[]{:S(2)}) collective-permute-start(bf16[72,512]{1,0:T(8,128)(2,1)S(1)} %bitcast.47), channel_id=1, source_target_pairs={{0,3},{1,2},{2,1},{3,0},{4,7},{5,6},{6,5},{7,4},{8,11},{9,10},{10,... | collective-permute-start | bytes 221192 | tf_op jit(solution)/shard_map/ppermute | solution.py:548
  76.0 6.9 %collective-permute-start.19 = (bf16[72,512]{1,0:T(8,128)(2,1)S(1)}, bf16[72,512]{1,0:T(8,128)(2,1)S(1)}, u32[]{:S(2)}, u32[]{:S(2)}) collective-permute-start(bf16[72,512]{1,0:T(8,128)(2,1)S(1)} %bitcast.46), channel_id=1, source_target_pairs={{0,1},{1,0},{2,3},{3,2},{4,5},{5,4},{6,7},{7,6},{8,9},{9,8},{10,11... | collective-permute-start | bytes 221192 | tf_op jit(solution)/shard_map/ppermute | solution.py:548
  77.2 5.6 %collective-permute-start.20 = (bf16[72,512]{1,0:T(8,128)(2,1)S(1)}, bf16[72,512]{1,0:T(8,128)(2,1)S(1)}, u32[]{:S(2)}, u32[]{:S(2)}) collective-permute-start(bf16[72,512]{1,0:T(8,128)(2,1)S(1)} %bitcast.45), channel_id=1, source_target_pairs={{0,2},{1,3},{2,0},{3,1},{4,6},{5,7},{6,4},{7,5},{8,10},{9,11},{10,... | collective-permute-start | bytes 221192 | tf_op jit(solution)/shard_map/ppermute | solution.py:548
  77.5 5.6 %collective-permute-start.21 = (bf16[72,512]{1,0:T(8,128)(2,1)S(1)}, bf16[72,512]{1,0:T(8,128)(2,1)S(1)}, u32[]{:S(2)}, u32[]{:S(2)}) collective-permute-start(bf16[72,512]{1,0:T(8,128)(2,1)S(1)} %bitcast.44), channel_id=1, source_target_pairs={{0,3},{1,2},{2,1},{3,0},{4,7},{5,6},{6,5},{7,4},{8,11},{9,10},{10,... | collective-permute-start | bytes 221192 | tf_op jit(solution)/shard_map/ppermute | solution.py:548
  80.6 6.1 %collective-permute-start.25 = (bf16[72,512]{1,0:T(8,128)(2,1)S(1)}, bf16[72,512]{1,0:T(8,128)(2,1)S(1)}, u32[]{:S(2)}, u32[]{:S(2)}) collective-permute-start(bf16[72,512]{1,0:T(8,128)(2,1)S(1)} %shard_map.198), channel_id=1, source_target_pairs={{0,4},{1,5},{2,6},{3,7},{4,0},{5,1},{6,2},{7,3},{8,12},{9,13},{10,... | collective-permute-start | bytes 221192 | tf_op jit(solution)/shard_map/ppermute | solution.py:548
  86.7 33.9 %slice-start = ((s8[5767168]{0:T(1024)(128)(4,1)}), s8[4194304]{0:T(1024)(128)(4,1)S(1)}, s32[]{:S(2)}) async-start(s8[5767168]{0:T(1024)(128)(4,1)} %bitcast.30), calls=%async_computation.4 | async-start | bytes 8388608
  86.7 33.9 %slice-start.2 = ((s8[5767168]{0:T(1024)(128)(4,1)}), s8[4194304]{0:T(1024)(128)(4,1)S(1)}, s32[]{:S(2)}) async-start(s8[5767168]{0:T(1024)(128)(4,1)} %bitcast.32), calls=%async_computation.6 | async-start | bytes 8388608
  86.7 33.9 %slice-start.4 = ((s8[5767168]{0:T(1024)(128)(4,1)}), s8[4194304]{0:T(1024)(128)(4,1)S(1)}, s32[]{:S(2)}) async-start(s8[5767168]{0:T(1024)(128)(4,1)} %bitcast.34), calls=%async_computation.8 | async-start | bytes 8388608
  86.7 33.8 %slice-start.1 = ((s8[5767168]{0:T(1024)(128)(4,1)}), s8[1572864]{0:T(1024)(128)(4,1)S(1)}, s32[]{:S(2)}) async-start(s8[5767168]{0:T(1024)(128)(4,1)} %bitcast.30), calls=%async_computation.5 | async-start | bytes 3145728
  127.6 16.1 %all-to-all-start.3 = ((bf16[32,24,256]{2,1,0:T(8,128)(2,1)}), bf16[32,24,256]{2,1,0:T(8,128)(2,1)S(1)}, u32[]{:S(2)}, u32[]{:S(2)}) async-start(bf16[32,24,256]{2,1,0:T(8,128)(2,1)} %bitcast.19), calls=%async_computation.3 | async-start | bytes 786432 | tf_op jit(solution)/shard_map/all_to_all | solution.py:543
  (14 other events, 327.8 us)

commit v6 on v5

--- a/solution.py
+++ b/solution.py
@@ -77,7 +77,8 @@
     return (rows * lax.rsqrt(square + epsilon) * gain.astype(jnp.float32)).astype(jnp.bfloat16)
 
 
-def project_body(rows_ref, gain_ref, weight_hbm, out_ref, weight_ref, sems):
+def project_body(base_ref, gain_ref, weight_hbm, *refs):
+    rows_refs, (out_ref, rows_ref, weight_ref, sems) = refs[:PIECES], refs[PIECES:]
     steps, each, width = weight_ref.shape
     copies = [
         pltpu.make_async_copy(
@@ -87,15 +88,21 @@
     ]
     for copy in copies:
         copy.start()
-    normed = normalised(lambda k: rows_ref[k], gain_ref[...], width)
+    part = width // PIECES
+    for k in range(PIECES):
+        at = pl.multiple_of((k ^ base_ref[0]) * part, part)
+        rows_ref[:, pl.ds(at, part)] = rows_refs[k][...]
+    normed = normalised(
+        lambda k: rows_ref[:, k * part : (k + 1) * part], gain_ref[...], width
+    )
     for step in range(steps):
         copies[step].wait()
         out = dot_nt(normed, weight_ref[step]).astype(jnp.bfloat16)
         out_ref[:, step * each : (step + 1) * each] = out
 
 
-def project(rows, gain, weight):
-    pieces, requests, part = rows.shape
+def project(base, rows, gain, weight):
+    requests, _ = rows[0].shape
     columns, width = weight.shape
     steps = 3 if columns % (3 * LANES) == 0 else 1
     return call(
@@ -104,13 +111,14 @@
         16,
         2 * requests * columns * width,
         2 * columns * width,
-        in_specs=[VMEM, VMEM, HBM],
+        in_specs=[pl.BlockSpec(memory_space=pltpu.SMEM), VMEM, HBM] + [VMEM] * PIECES,
         out_specs=VMEM,
         scratch_shapes=[
+            pltpu.VMEM((requests, width), jnp.bfloat16),
             pltpu.VMEM((steps, columns // steps, width), jnp.bfloat16),
             pltpu.SemaphoreType.DMA((steps,)),
         ],
-    )(rows, gain, in_hbm(weight))
+    )(base[None], gain, in_hbm(weight), *rows)
 
 
 def pick_body(pick_ref, extra_ref, *refs):
@@ -426,42 +434,69 @@
         functools.partial(join_body, not copies),
         jax.ShapeDtypeStruct(shape, jnp.bfloat16),
         6,
-        3e10 if copies else 2 * len(parts) * rows * LAT,
+        2 * len(parts) * rows * LAT,
         4 * len(parts) * rows * LAT,
         in_specs=[VMEM] * len(parts),
         out_specs=VMEM,
     )(*parts)
 
 
-def output_body(rows_ref, weight_ref, hidden_ref, out_ref, copies_ref):
-    requests = hidden_ref.shape[0]
-    total = hidden_ref[...].astype(jnp.float32)
-    for h in range(H):
-        total = total + dot_nt(
-            rows_ref[h * requests : (h + 1) * requests, :],
-            weight_ref[:, h * LAT : (h + 1) * LAT],
-        )
-    out = total.astype(jnp.bfloat16)
-    out_ref[...] = out
-    for c in range(copies_ref.shape[0]):
-        copies_ref[c] = out
-
-
-def output_projection(rows, weight, hidden, copies):
+def output_body(share, base_ref, weight_hbm, start_ref, *refs):
+    count = PIECES // SHARES
+    rows_refs, out_refs = refs[:count], refs[count:-2]
+    weight_ref, sems = refs[-2:]
+    requests, _ = start_ref.shape
+    width = weight_ref.shape[2]
+    copies = []
+    for k in range(count):
+        piece = share * count + k ^ base_ref[0]
+        copy = pltpu.make_async_copy(
+            weight_hbm.at[:, pl.ds(pl.multiple_of(piece * width, width), width)],
+            weight_ref.at[k],
+            sems.at[k],
+        )
+        copy.start()
+        copies.append(copy)
+    total = start_ref[...].astype(jnp.float32)
+    for k in range(count):
+        copies[k].wait()
+        for j in range(2):
+            total = total + dot_nt(
+                rows_refs[k][j * requests : (j + 1) * requests, :],
+                weight_ref[k, :, j * LAT : (j + 1) * LAT],
+            )
+    if share < SHARES - 1:
+        out_refs[0][...] = total
+    else:
+        out = total.astype(jnp.bfloat16)
+        out_refs[0][...] = out
+        for c in range(out_refs[1].shape[0]):
+            out_refs[1][c] = out
+
+
+def output_projection(share, base, rows, weight, start, copies):
     features, width = weight.shape
-    requests = hidden.shape[0]
+    last = share == SHARES - 1
+    if last:
+        out = (
+            jax.ShapeDtypeStruct(start.shape, jnp.bfloat16),
+            jax.ShapeDtypeStruct((copies,) + start.shape, jnp.bfloat16),
+        )
+    else:
+        out = jax.ShapeDtypeStruct(start.shape, jnp.float32)
     return call(
-        output_body,
-        (
-            jax.ShapeDtypeStruct(hidden.shape, jnp.bfloat16),
-            jax.ShapeDtypeStruct((copies,) + hidden.shape, jnp.bfloat16),
-        ),
+        functools.partial(output_body, share),
+        out,
         8,
-        2 * requests * features * width,
-        2 * features * width,
-        in_specs=[VMEM] * 3,
-        out_specs=(VMEM, VMEM),
-    )(rows, weight, hidden)
+        3e10 if last else 2 * start.shape[0] * features * width // SHARES,
+        2 * features * width // SHARES,
+        in_specs=[pl.BlockSpec(memory_space=pltpu.SMEM), HBM, VMEM] + [VMEM] * len(rows),
+        out_specs=(VMEM, VMEM) if last else VMEM,
+        scratch_shapes=[
+            pltpu.VMEM((len(rows), features, width // PIECES), jnp.bfloat16),
+            pltpu.SemaphoreType.DMA((len(rows),)),
+        ],
+    )(base[None], in_hbm(weight), start, *rows)
 
 
 def gated(rows, gate, up):
@@ -546,6 +581,12 @@
 def turn(x, k):
     count = lax.axis_size("tensor")
     return lax.ppermute(x, "tensor", [(i, i ^ k) for i in range(count)])
+
+
+def gather_by_turns(x):
+    near = [x] + [turn(x, k) for k in (1, 2, 3)]
+    crossed = turn(x, 4)
+    return near + [crossed] + [turn(crossed, k) for k in (1, 2, 3)]
 
 
 def swap_owners(arrays):
@@ -616,9 +657,16 @@
         group_columns = group_cache.reshape(-1, KVW).T[None]
     else:
         group_columns = jnp.swapaxes(group_cache, 1, 2)
-    rows = exchange(jnp.broadcast_to(hidden[None], (tensors,) + hidden.shape), "tensor")
-
-    projected = project(gather_pieces(rows), attention_gain[None], query_weight)
+    by_turns = tensors == PIECES
+    base = tensor_index if by_turns else jnp.zeros((), jnp.int32)
+    if by_turns:
+        rows = gather_by_turns(hidden)
+    else:
+        copies = jnp.broadcast_to(hidden[None], (tensors,) + hidden.shape)
+        rows = gather_pieces(exchange(copies, "tensor"))
+        rows = [rows[k] for k in range(PIECES)]
+
+    projected = project(base, rows, attention_gain[None], query_weight)
     projected, group_of, group_length, suffix_length, routes, route_weight = (
         lax.optimization_barrier(
             (projected, group_of, group_length, suffix_length, routes, route_weight)
@@ -653,10 +701,8 @@
         .reshape(1, -1)
         .astype(jnp.float32)
     )
-    if tensors == PIECES:
-        pieces = [projected] + [turn(projected, k) for k in (1, 2, 3)]
-        pieces.append(turn(projected, 4))
-        pieces += [turn(pieces[4], k) for k in (1, 2, 3)]
+    if by_turns:
+        pieces = gather_by_turns(projected)
     else:
         copies = jnp.broadcast_to(projected[None], (tensors,) + projected.shape)
         queries = gather_pieces(exchange(copies, "tensor"))
@@ -710,17 +756,22 @@
     first.append(own_attention(far, suffix_holder, root_columns, suffix_rows))
     back, gain = lax.optimization_barrier((back, mixture_gain[None]))
     parts = local_join(unpick, first, sum(back, []), tensors // PIECES)
-    if tensors == PIECES:
+    if by_turns:
         parts = [part[0] for part in parts]
         crossing = join([parts[4]] + [turn(parts[4 + k], k) for k in (1, 2, 3)])
         parts = [parts[0]] + [turn(parts[k], k) for k in (1, 2, 3)] + [turn(crossing, 4)]
     else:
         parts = exchange(jnp.concatenate(parts, axis=0), "tensor")
         parts = [parts[k] for k in range(tensors)]
-    attention = exchange(join(parts, tensors), "tensor")
-    mid, copies = output_projection(
-        attention.reshape(-1, LAT), out_weight, hidden, owners // 2 * tensors
-    )
+    if by_turns:
+        attention = gather_by_turns(join(parts, 1)[0])
+    else:
+        attention = exchange(join(parts, tensors), "tensor").reshape(PIECES, -1, LAT)
+        attention = [attention[k] for k in range(PIECES)]
+    half = PIECES // SHARES
+    total = output_projection(0, base, attention[:half], out_weight, hidden, 0)
+    rest, total = lax.optimization_barrier((attention[half:], total))
+    mid, copies = output_projection(1, base, rest, out_weight, total, pairs * tensors)
 
     half = exchange(copies, ("pair", "tensor"))
     both = lax.all_gather(half.reshape((pairs, tensors) + mid.shape), "core")

time: 145 us -> 143 us (0.986)
  blocking collectives: 32.2 us -> 15.2 us
  starting transfers between devices: 34.2 us -> 46.6 us
  Pallas kernels: 42.9 us -> 47.4 us
    ppermute x14 -> x28, starting transfers between devices: 16.4 us -> 36.1 us  [turn(): return lax.ppermute(x, 'tensor', [(i, i ^ k) for i in range(count)])]
    all_to_all x2 -> x1, blocking collectives: 29.8 us -> 12.8 us  [exchange(): return lax.all_to_all(x, axis, 0, 0, tiled=True)]
    all_to_all x2 -> x1, starting transfers between devices: 9.85 us -> 2.59 us  [exchange(): return lax.all_to_all(x, axis, 0, 0, tiled=True)]
    all_to_all x2 -> x1, waiting for transfers between devices: 17.9 us -> 12.1 us  [exchange(): return lax.all_to_all(x, axis, 0, 0, tiled=True)]
    ppermute x14 -> x28, waiting for transfers between devices: 6.02 us -> 10.7 us  [turn(): return lax.ppermute(x, 'tensor', [(i, i ^ k) for i in range(count)])]
    pallas_call x1 -> x2, Pallas kernels: 1.35 us -> 5.8 us  [output_projection(): call(functools.partial(output_body, share), out, 8, 30000000000.0 if last...]
  transfers between devices with their start and end apart: 28 -> 41, of which waited for: 10 -> 14; matrix products, arithmetic and copies ran while one was open for 3% -> 3% of each run, Pallas kernels for 16% -> 18%
where the time goes in v6:
time: 143 us
  Pallas kernels  47.4 us (33%)
  starting transfers between devices  46.6 us (33%)
  waiting for transfers between devices  26.4 us (18%)
  blocking collectives  15.2 us (11%)
  local copies, waits for them, and re-layouts  4.06 us (3%)
  other arithmetic  2.42 us (2%)
    ppermute x28, starting transfers between devices, turn(): return lax.ppermute(x, 'tensor', [(i, i ^ k) for i in range(count)])  36.1 us
    pallas_call x2, Pallas kernels, own_attention(): call(own_body, pltpu.HBM((count, LAT + LANES), jnp.float32), 44, 2 * coun...  18 us
    all_to_all x1, blocking collectives, exchange(): return lax.all_to_all(x, axis, 0, 0, tiled=True)  12.8 us
    all_to_all x1, waiting for transfers between devices, exchange(): return lax.all_to_all(x, axis, 0, 0, tiled=True)  12.1 us
    ppermute x28, waiting for transfers between devices, turn(): return lax.ppermute(x, 'tensor', [(i, i ^ k) for i in range(count)])  10.7 us
    pallas_call x2, Pallas kernels, group_attention(): call(functools.partial(group_body, owners), (out,) * owners, 40, 2 * owne...  9.29 us
    ppermute x12, starting transfers between devices, swap_owners(): out[k] = lax.ppermute(arrays[k], OWNER, [(i, i ^ k) for i in range(count)])  7.95 us
    pallas_call x1, Pallas kernels, expert(): call(expert_body, jax.ShapeDtypeStruct((owners, PIECES, slots + requests...  6.86 us
  transfers between devices with their start and end apart: 41, of which 14 were waited for; matrix products, arithmetic and copies ran while one was open for 3% of the time, Pallas kernels for 18%

profile of v6, /device:TPU:0, one launch (start us, length us, event | category | flops | bytes accessed | tf_op | source)
XLA Modules:
  0.0 142.7 jit_solution(8074161113722706044)
XLA Ops:
  0.0 4.1 %collective-permute-start.3 = (bf16[32,256]{1,0:T(8,128)(2,1)}, bf16[32,256]{1,0:T(8,128)(2,1)S(1)}, u32[]{:S(2)}, u32[]{:S(2)}) collective-permute-start(bf16[32,256]{1,0:T(8,128)(2,1)} %start_ref.1), channel_id=1, source_target_pairs={{0,4},{1,5},{2,6},{3,7},{4,0},{5,1},{6,2},{7,3},{8,12},{9,13},{10,... | collective-permute-start | bytes 49160 | tf_op jit(solution)/shard_map/ppermute | solution.py:583
  4.1 2.5 %collective-permute-start.2 = (bf16[32,256]{1,0:T(8,128)(2,1)}, bf16[32,256]{1,0:T(8,128)(2,1)S(1)}, u32[]{:S(2)}, u32[]{:S(2)}) collective-permute-start(bf16[32,256]{1,0:T(8,128)(2,1)} %start_ref.1), channel_id=1, source_target_pairs={{0,3},{1,2},{2,1},{3,0},{4,7},{5,6},{6,5},{7,4},{8,11},{9,10},{10,... | collective-permute-start | bytes 49160 | tf_op jit(solution)/shard_map/ppermute | solution.py:583
  8.4 2.6 %collective-permute-start.6 = (bf16[32,256]{1,0:T(8,128)(2,1)S(1)}, bf16[32,256]{1,0:T(8,128)(2,1)S(1)}, u32[]{:S(2)}, u32[]{:S(2)}) collective-permute-start(bf16[32,256]{1,0:T(8,128)(2,1)S(1)} %collective-permute-done.3.refs_4_), channel_id=1, source_target_pairs={{0,3},{1,2},{2,1},{3,0},{4,7},{5,6},{6,5},{7,4},{8,11},{9,10},{10,... | collective-permute-start | bytes 49160 | tf_op jit(solution)/shard_map/ppermute | solution.py:583
  13.1 1.6 %collective-permute-done.5.refs_6_ = bf16[32,256]{1,0:T(8,128)(2,1)S(1)} collective-permute-done((bf16[32,256]{1,0:T(8,128)(2,1)S(1)}, bf16[32,256]{1,0:T(8,128)(2,1)S(1)}, u32[]{:S(2)}, u32[]{:S(2)}) %collective-permute-start.5) | collective-permute-done | bytes 16416 | tf_op jit(solution)/shard_map/ppermute | solution.py:583
  15.8 3.4 %shard_map.190.refs_0_ = bf16[32,1152]{1,0:T(8,128)(2,1)S(1)} custom-call(s32[1]{0:T(128)} %bitcast.base_ref, bf16[1,2048]{1,0:T(2,128)(2,1)S(1)} %broadcast_in_dim.228.gain_ref, bf16[1152,2048]{1,0:T(8,128)(2,1)} %weight_hbm.3, bf16[32,256]{1,0:T(8,128)(2,1)S(1)} %copy-done.3, bf16[32,256]{1,0:T(8,128)(2,1)S(1)} %collective-permute-done.refs_1_, ...), custom_call_target="tpu_custom_call" | custom-call | flops 150994944 | bytes 4718592 | tf_op jit(solution)/shard_map/pallas_call | solution.py:108
  19.9 1.6 %collective-permute-start.9 = (bf16[32,1152]{1,0:T(8,128)(2,1)S(1)}, bf16[32,1152]{1,0:T(8,128)(2,1)S(1)}, u32[]{:S(2)}, u32[]{:S(2)}) collective-permute-start(bf16[32,1152]{1,0:T(8,128)(2,1)S(1)} %shard_map.190.refs_0_), channel_id=1, source_target_pairs={{0,3},{1,2},{2,1},{3,0},{4,7},{5,6},{6,5},{7,4},{8,11},{9,10},{10,... | collective-permute-start | bytes 221192 | tf_op jit(solution)/shard_map/ppermute | solution.py:583
  21.9 1.5 %collective-permute-start.7 = (bf16[32,1152]{1,0:T(8,128)(2,1)S(1)}, bf16[32,1152]{1,0:T(8,128)(2,1)S(1)}, u32[]{:S(2)}, u32[]{:S(2)}) collective-permute-start(bf16[32,1152]{1,0:T(8,128)(2,1)S(1)} %shard_map.190.refs_0_), channel_id=1, source_target_pairs={{0,1},{1,0},{2,3},{3,2},{4,5},{5,4},{6,7},{7,6},{8,9},{9,8},{10,11... | collective-permute-start | bytes 221192 | tf_op jit(solution)/shard_map/ppermute | solution.py:583
  27.3 1.6 %collective-permute-start.15 = (bf16[16,4736]{1,0:T(8,128)(2,1)S(1)}, bf16[16,4736]{1,0:T(8,128)(2,1)S(1)}, u32[]{:S(2)}, u32[]{:S(2)}) collective-permute-start(bf16[16,4736]{1,0:T(8,128)(2,1)S(1)} %get-tuple-element.105), channel_id=1, source_target_pairs={{0,16},{8,24},{16,0},{24,8},{1,17},{9,25},{17,1},{25,9},{2,18},{10... | collective-permute-start | bytes 454664 | tf_op jit(solution)/shard_map/ppermute | solution.py:596
  30.1 1.5 %collective-permute-start.11 = (bf16[32,1152]{1,0:T(8,128)(2,1)S(1)}, bf16[32,1152]{1,0:T(8,128)(2,1)S(1)}, u32[]{:S(2)}, u32[]{:S(2)}) collective-permute-start(bf16[32,1152]{1,0:T(8,128)(2,1)S(1)} %collective-permute-done.10.refs_0_), channel_id=1, source_target_pairs={{0,1},{1,0},{2,3},{3,2},{4,5},{5,4},{6,7},{7,6},{8,9},{9,8},{10,11... | collective-permute-start | bytes 221192 | tf_op jit(solution)/shard_map/ppermute | solution.py:583
  31.6 9.0 %shard_map.191.refs_0_ = f32[256,640]{1,0:T(8,128)} custom-call(s32[1,2048]{1,0:T(1,128)S(1)} %select_n.114.holder_ref, bf16[576,4096]{1,0:T(8,128)(2,1)} %bitcast.59, bf16[2048,576]{1,0:T(8,128)(2,1)} %bitcast.61, bf16[32,1152]{1,0:T(8,128)(2,1)S(1)} %shard_map.190.refs_0_, bf16[32,1152]{1,0:T(8,128)(2,1)S(1)} %collective-permute-done.7.refs_1_, ...), custom_call_target="tpu_custom_call" | custom-call | flops 2852126720 | bytes 7077888 | tf_op jit(solution)/shard_map/pallas_call | solution.py:223
  42.6 1.6 %collective-permute-start.18 = (bf16[16,4736]{1,0:T(8,128)(2,1)S(1)}, bf16[16,4736]{1,0:T(8,128)(2,1)S(1)}, u32[]{:S(2)}, u32[]{:S(2)}) collective-permute-start(bf16[16,4736]{1,0:T(8,128)(2,1)S(1)} %get-tuple-element.113), channel_id=1, source_target_pairs={{0,16},{8,24},{16,0},{24,8},{1,17},{9,25},{17,1},{25,9},{2,18},{10... | collective-permute-start | bytes 454664 | tf_op jit(solution)/shard_map/ppermute | solution.py:596
  44.5 4.6 %shard_map.194 = (bf16[16,4224]{1,0:T(8,128)(2,1)S(1)}, bf16[16,4224]{1,0:T(8,128)(2,1)S(1)}, bf16[16,4224]{1,0:T(8,128)(2,1)S(1)}, bf16[16,4224]{1,0:T(8,128)(2,1)S(1)}) custom-call(bf16[12,576,128]{2,1,0:T(8,128)(2,1)} %bitcast.63, f32[1,1536]{1,0:T(1,128)S(1)} %bitcast.47, bf16[16,4736]{1,0:T(8,128)(2,1)S(1)} %get-tuple-element.115.refs_0_, ...), custom_call_target="tpu_custom_call" | custom-call | flops 1711276032 | bytes 1769472 | tf_op jit(solution)/shard_map/pallas_call | solution.py:306
  49.4 2.3 %collective-permute-done.19.refs_3_ = bf16[16,4736]{1,0:T(8,128)(2,1)S(1)} collective-permute-done((bf16[16,4736]{1,0:T(8,128)(2,1)S(1)}, bf16[16,4736]{1,0:T(8,128)(2,1)S(1)}, u32[]{:S(2)}, u32[]{:S(2)}) %collective-permute-start.19) | collective-permute-done | bytes 151584 | tf_op jit(solution)/shard_map/ppermute | solution.py:596
  51.8 4.7 %shard_map.195 = (bf16[16,4224]{1,0:T(8,128)(2,1)S(1)}, bf16[16,4224]{1,0:T(8,128)(2,1)S(1)}, bf16[16,4224]{1,0:T(8,128)(2,1)S(1)}, bf16[16,4224]{1,0:T(8,128)(2,1)S(1)}) custom-call(bf16[12,576,128]{2,1,0:T(8,128)(2,1)} %bitcast.64, f32[1,1536]{1,0:T(1,128)S(1)} %bitcast.48, bf16[16,4736]{1,0:T(8,128)(2,1)S(1)} %get-tuple-element.123.refs_0_, ...), custom_call_target="tpu_custom_call" | custom-call | flops 1711276032 | bytes 1769472 | tf_op jit(solution)/shard_map/pallas_call | solution.py:306
  56.9 1.6 %collective-permute-start.24 = (bf16[16,4224]{1,0:T(8,128)(2,1)S(1)}, bf16[16,4224]{1,0:T(8,128)(2,1)S(1)}, u32[]{:S(2)}, u32[]{:S(2)}) collective-permute-start(bf16[16,4224]{1,0:T(8,128)(2,1)S(1)} %get-tuple-element.143), channel_id=1, source_target_pairs={{0,16},{8,24},{16,0},{24,8},{1,17},{9,25},{17,1},{25,9},{2,18},{10... | collective-permute-start | bytes 405512 | tf_op jit(solution)/shard_map/ppermute | solution.py:596
  59.1 1.5 %collective-permute-start.21 = (bf16[16,4224]{1,0:T(8,128)(2,1)S(1)}, bf16[16,4224]{1,0:T(8,128)(2,1)S(1)}, u32[]{:S(2)}, u32[]{:S(2)}) collective-permute-start(bf16[16,4224]{1,0:T(8,128)(2,1)S(1)} %get-tuple-element.139), channel_id=1, source_target_pairs={{0,16},{8,24},{16,0},{24,8},{1,17},{9,25},{17,1},{25,9},{2,18},{10... | collective-permute-start | bytes 405512 | tf_op jit(solution)/shard_map/ppermute | solution.py:596
  60.6 9.0 %shard_map.196.refs_1_ = f32[256,640]{1,0:T(8,128)} custom-call(s32[1,2048]{1,0:T(1,128)S(1)} %select_n.114.holder_ref, bf16[576,4096]{1,0:T(8,128)(2,1)} %bitcast.60, bf16[2048,576]{1,0:T(8,128)(2,1)} %bitcast.62, bf16[32,1152]{1,0:T(8,128)(2,1)S(1)} %collective-permute-done.10.refs_0_, bf16[32,1152]{1,0:T(8,128)(2,1)S(1)} %collective-permute-done.11.refs_1_, ...), custom_call_target="tpu_custom_call" | custom-call | flops 2852126720 | bytes 7077888 | tf_op jit(solution)/shard_map/pallas_call | solution.py:223
  70.6 2.1 %shard_map.197 = (bf16[1,72,512]{2,1,0:T(8,128)(2,1)S(1)}, bf16[1,72,512]{2,1,0:T(8,128)(2,1)S(1)}, bf16[1,72,512]{2,1,0:T(8,128)(2,1)S(1)}, bf16[1,72,512]{2,1,...) custom-call(bf16[32,64]{1,0:T(8,128)(2,1)S(1)} %and_convert_fusion.u, ...), custom_call_target="tpu_custom_call" | custom-call | flops 33554432 | bytes 1048576 | tf_op jit(solution)/shard_map/pallas_call | solution.py:394
  73.4 1.9 %collective-permute-start.30 = (bf16[72,512]{1,0:T(8,128)(2,1)S(1)}, bf16[72,512]{1,0:T(8,128)(2,1)S(1)}, u32[]{:S(2)}, u32[]{:S(2)}) collective-permute-start(bf16[72,512]{1,0:T(8,128)(2,1)S(1)} %bitcast.53), channel_id=1, source_target_pairs={{0,2},{1,3},{2,0},{3,1},{4,6},{5,7},{6,4},{7,5},{8,10},{9,11},{10,... | collective-permute-start | bytes 221192 | tf_op jit(solution)/shard_map/ppermute | solution.py:583
  76.8 1.9 %collective-permute-start.27 = (bf16[72,512]{1,0:T(8,128)(2,1)S(1)}, bf16[72,512]{1,0:T(8,128)(2,1)S(1)}, u32[]{:S(2)}, u32[]{:S(2)}) collective-permute-start(bf16[72,512]{1,0:T(8,128)(2,1)S(1)} %bitcast.50), channel_id=1, source_target_pairs={{0,2},{1,3},{2,0},{3,1},{4,6},{5,7},{6,4},{7,5},{8,10},{9,11},{10,... | collective-permute-start | bytes 221192 | tf_op jit(solution)/shard_map/ppermute | solution.py:583
  79.8 1.5 %collective-permute-done.31.refs_3_ = bf16[72,512]{1,0:T(8,128)(2,1)S(1)} collective-permute-done((bf16[72,512]{1,0:T(8,128)(2,1)S(1)}, bf16[72,512]{1,0:T(8,128)(2,1)S(1)}, u32[]{:S(2)}, u32[]{:S(2)}) %collective-permute-start.31) | collective-permute-done | bytes 73760 | tf_op jit(solution)/shard_map/ppermute | solution.py:583
  81.5 1.8 %collective-permute-start.32 = (bf16[72,512]{1,0:T(8,128)(2,1)S(1)}, bf16[72,512]{1,0:T(8,128)(2,1)S(1)}, u32[]{:S(2)}, u32[]{:S(2)}) collective-permute-start(bf16[72,512]{1,0:T(8,128)(2,1)S(1)} %shard_map.198), channel_id=1, source_target_pairs={{0,4},{1,5},{2,6},{3,7},{4,0},{5,1},{6,2},{7,3},{8,12},{9,13},{10,... | collective-permute-start | bytes 221192 | tf_op jit(solution)/shard_map/ppermute | solution.py:583
  83.3 1.5 %collective-permute-done.28.refs_3_ = bf16[72,512]{1,0:T(8,128)(2,1)S(1)} collective-permute-done((bf16[72,512]{1,0:T(8,128)(2,1)S(1)}, bf16[72,512]{1,0:T(8,128)(2,1)S(1)}, u32[]{:S(2)}, u32[]{:S(2)}) %collective-permute-start.28) | collective-permute-done | bytes 73760 | tf_op jit(solution)/shard_map/ppermute | solution.py:583
  84.8 2.8 %collective-permute-done.32.refs_4_ = bf16[72,512]{1,0:T(8,128)(2,1)S(1)} collective-permute-done((bf16[72,512]{1,0:T(8,128)(2,1)S(1)}, bf16[72,512]{1,0:T(8,128)(2,1)S(1)}, u32[]{:S(2)}, u32[]{:S(2)}) %collective-permute-start.32) | collective-permute-done | bytes 73760 | tf_op jit(solution)/shard_map/ppermute | solution.py:583
  88.9 2.2 %collective-permute-start.39 = (bf16[64,512]{1,0:T(8,128)(2,1)S(1)}, bf16[64,512]{1,0:T(8,128)(2,1)S(1)}, u32[]{:S(2)}, u32[]{:S(2)}) collective-permute-start(bf16[64,512]{1,0:T(8,128)(2,1)S(1)} %bitcast.40), channel_id=1, source_target_pairs={{0,3},{1,2},{2,1},{3,0},{4,7},{5,6},{6,5},{7,4},{8,11},{9,10},{10,... | collective-permute-start | bytes 196616 | tf_op jit(solution)/shard_map/ppermute | solution.py:583
  96.8 2.6 %shard_map.200.start_ref = f32[32,256]{1,0:T(8,128)S(1)} custom-call(s32[1]{0:T(128)} %bitcast.base_ref, bf16[256,8192]{1,0:T(8,128)(2,1)} %weight_hbm.5, bf16[32,256]{1,0:T(8,128)(2,1)S(1)} %copy-done.4, bf16[64,512]{1,0:T(8,128)(2,1)S(1)} %bitcast.43, bf16[64,512]{1,0:T(8,128)(2,1)S(1)} %collective-permute-done.37.refs_1_, ...), custom_call_target="tpu_custom_call" | custom-call | flops 67108864 | bytes 2097152 | tf_op jit(solution)/shard_map/pallas_call | solution.py:487
  100.2 3.2 %shard_map.201 = (bf16[32,256]{1,0:T(8,128)(2,1)S(1)}, bf16[16,32,256]{2,1,0:T(8,128)(2,1)S(1)}) custom-call(s32[1]{0:T(128)} %bitcast.base_ref, bf16[256,8192]{1,0:T(8,128)(2,1)} %weight_hbm.5, f32[32,256]{1,0:T(8,128)S(1)} %shard_map.200.start_ref, bf16[64,512]{1,0:T(8,128)(2,1)S(1)} %collective-permute-done.33.refs_0_, ...), custom_call_target="tpu_custom_call" | custom-call | flops 30000001024 | bytes 2097152 | tf_op jit(solution)/shard_map/pallas_call | solution.py:487
  103.5 12.8 %all_to_all.10 = bf16[16,32,256]{2,1,0:T(8,128)(2,1)S(1)} all-to-all(bf16[16,32,256]{2,1,0:T(8,128)(2,1)S(1)} %get-tuple-element.166), channel_id=1, replica_groups=mesh['pair'=2,'core'=2,'tensor'=8] {'pair','tensor'}, dimensions={0} | all-to-all | bytes 524288 | tf_op jit(solution)/shard_map/all_to_all | solution.py:578
  116.2 2.4 %all_gather.3 = bf16[2,2,8,32,256]{4,3,2,1,0:T(8,128)(2,1)S(1)} all-gather(bf16[1,2,8,32,256]{4,3,2,1,0:T(8,128)(2,1)S(1)} %bitcast.55), channel_id=1, replica_groups=mesh['pair'=2,'core'=2,'tensor'=8] {'core'}, dimensions={0}, use_global_device_ids=true | all-gather | bytes 786432 | tf_op jit(solution)/shard_map/all_gather | solution.py:777
  118.7 6.9 %shard_map.202 = bf16[4,8,24,256]{3,2,1,0:T(8,128)(2,1)} custom-call(bf16[96,128]{1,0:T(8,128)(2,1)S(1)} %add_convert_fusion.pick_ref, bf16[4,8,32,256]{3,2,1,0:T(8,128)(2,1)S(1)} %bitcast.37, bf16[1,2048]{1,0:T(2,128)(2,1)S(1)} %broadcast_in_dim.248.gain_ref, bf16[352,2048]{1,0:T(8,128)(2,1)S(1)} %copy-done, bf16[352,2048]{1,0:T(8,128)(2,1)S(1)} %copy-done.1, ...), custom_call_target="tpu_custom_call" | custom-call | flops 1660944384 | bytes 17301504 | tf_op jit(solution)/shard_map/pallas_call | solution.py:543
  125.6 2.6 %all-to-all-start.1 = ((bf16[32,24,256]{2,1,0:T(8,128)(2,1)}), bf16[32,24,256]{2,1,0:T(8,128)(2,1)S(1)}, u32[]{:S(2)}, u32[]{:S(2)}) async-start(bf16[32,24,256]{2,1,0:T(8,128)(2,1)} %bitcast.20), calls=%async_computation.1 | async-start | bytes 786432 | tf_op jit(solution)/shard_map/all_to_all | solution.py:578
  129.6 12.1 %all-to-all-done.1 = bf16[32,24,256]{2,1,0:T(8,128)(2,1)S(1)} async-done(((bf16[32,24,256]{2,1,0:T(8,128)(2,1)}), bf16[32,24,256]{2,1,0:T(8,128)(2,1)S(1)}, u32[]{:S(2)}, u32[]{:S(2)}) %all-to-all-start.1) | async-done | bytes 393248 | tf_op jit(solution)/shard_map/all_to_all | solution.py:578
  (177 shorter events, 29.0 us)
Async XLA Ops:
  0.0 8.3 %collective-permute-start.3 = (bf16[32,256]{1,0:T(8,128)(2,1)}, bf16[32,256]{1,0:T(8,128)(2,1)S(1)}, u32[]{:S(2)}, u32[]{:S(2)}) collective-permute-start(bf16[32,256]{1,0:T(8,128)(2,1)} %start_ref.1), channel_id=1, source_target_pairs={{0,4},{1,5},{2,6},{3,7},{4,0},{5,1},{6,2},{7,3},{8,12},{9,13},{10,... | collective-permute-start | bytes 49160 | tf_op jit(solution)/shard_map/ppermute | solution.py:583
  4.1 7.3 %collective-permute-start.2 = (bf16[32,256]{1,0:T(8,128)(2,1)}, bf16[32,256]{1,0:T(8,128)(2,1)S(1)}, u32[]{:S(2)}, u32[]{:S(2)}) collective-permute-start(bf16[32,256]{1,0:T(8,128)(2,1)} %start_ref.1), channel_id=1, source_target_pairs={{0,3},{1,2},{2,1},{3,0},{4,7},{5,6},{6,5},{7,4},{8,11},{9,10},{10,... | collective-permute-start | bytes 49160 | tf_op jit(solution)/shard_map/ppermute | solution.py:583
  6.6 6.1 %collective-permute-start.1 = (bf16[32,256]{1,0:T(8,128)(2,1)}, bf16[32,256]{1,0:T(8,128)(2,1)S(1)}, u32[]{:S(2)}, u32[]{:S(2)}) collective-permute-start(bf16[32,256]{1,0:T(8,128)(2,1)} %start_ref.1), channel_id=1, source_target_pairs={{0,2},{1,3},{2,0},{3,1},{4,6},{5,7},{6,4},{7,5},{8,10},{9,11},{10,... | collective-permute-start | bytes 49160 | tf_op jit(solution)/shard_map/ppermute | solution.py:583
  7.1 5.6 %collective-permute-start = (bf16[32,256]{1,0:T(8,128)(2,1)}, bf16[32,256]{1,0:T(8,128)(2,1)S(1)}, u32[]{:S(2)}, u32[]{:S(2)}) collective-permute-start(bf16[32,256]{1,0:T(8,128)(2,1)} %start_ref.1), channel_id=1, source_target_pairs={{0,1},{1,0},{2,3},{3,2},{4,5},{5,4},{6,7},{7,6},{8,9},{9,8},{10,11... | collective-permute-start | bytes 49160 | tf_op jit(solution)/shard_map/ppermute | solution.py:583
  19.9 6.5 %collective-permute-start.9 = (bf16[32,1152]{1,0:T(8,128)(2,1)S(1)}, bf16[32,1152]{1,0:T(8,128)(2,1)S(1)}, u32[]{:S(2)}, u32[]{:S(2)}) collective-permute-start(bf16[32,1152]{1,0:T(8,128)(2,1)S(1)} %shard_map.190.refs_0_), channel_id=1, source_target_pairs={{0,3},{1,2},{2,1},{3,0},{4,7},{5,6},{6,5},{7,4},{8,11},{9,10},{10,... | collective-permute-start | bytes 221192 | tf_op jit(solution)/shard_map/ppermute | solution.py:583
  24.7 5.4 %collective-permute-start.13 = (bf16[32,1152]{1,0:T(8,128)(2,1)S(1)}, bf16[32,1152]{1,0:T(8,128)(2,1)S(1)}, u32[]{:S(2)}, u32[]{:S(2)}) collective-permute-start(bf16[32,1152]{1,0:T(8,128)(2,1)S(1)} %collective-permute-done.10.refs_0_), channel_id=1, source_target_pairs={{0,3},{1,2},{2,1},{3,0},{4,7},{5,6},{6,5},{7,4},{8,11},{9,10},{10,... | collective-permute-start | bytes 221192 | tf_op jit(solution)/shard_map/ppermute | solution.py:583
  27.2 14.0 %collective-permute-start.14 = (bf16[16,4736]{1,0:T(8,128)(2,1)S(1)}, bf16[16,4736]{1,0:T(8,128)(2,1)S(1)}, u32[]{:S(2)}, u32[]{:S(2)}) collective-permute-start(bf16[16,4736]{1,0:T(8,128)(2,1)S(1)} %get-tuple-element.104), channel_id=1, source_target_pairs={{0,8},{8,0},{16,24},{24,16},{1,9},{9,1},{17,25},{25,17},{2,10},{10... | collective-permute-start | bytes 454664 | tf_op jit(solution)/shard_map/ppermute | solution.py:596
  27.3 14.2 %collective-permute-start.15 = (bf16[16,4736]{1,0:T(8,128)(2,1)S(1)}, bf16[16,4736]{1,0:T(8,128)(2,1)S(1)}, u32[]{:S(2)}, u32[]{:S(2)}) collective-permute-start(bf16[16,4736]{1,0:T(8,128)(2,1)S(1)} %get-tuple-element.105), channel_id=1, source_target_pairs={{0,16},{8,24},{16,0},{24,8},{1,17},{9,25},{17,1},{25,9},{2,18},{10... | collective-permute-start | bytes 454664 | tf_op jit(solution)/shard_map/ppermute | solution.py:596
  28.9 12.8 %collective-permute-start.16 = (bf16[16,4736]{1,0:T(8,128)(2,1)S(1)}, bf16[16,4736]{1,0:T(8,128)(2,1)S(1)}, u32[]{:S(2)}, u32[]{:S(2)}) collective-permute-start(bf16[16,4736]{1,0:T(8,128)(2,1)S(1)} %get-tuple-element.106), channel_id=1, source_target_pairs={{0,24},{8,16},{16,8},{24,0},{1,25},{9,17},{17,9},{25,1},{2,26},{10... | collective-permute-start | bytes 454664 | tf_op jit(solution)/shard_map/ppermute | solution.py:596
  29.1 11.7 %collective-permute-start.12 = (bf16[32,1152]{1,0:T(8,128)(2,1)S(1)}, bf16[32,1152]{1,0:T(8,128)(2,1)S(1)}, u32[]{:S(2)}, u32[]{:S(2)}) collective-permute-start(bf16[32,1152]{1,0:T(8,128)(2,1)S(1)} %collective-permute-done.10.refs_0_), channel_id=1, source_target_pairs={{0,2},{1,3},{2,0},{3,1},{4,6},{5,7},{6,4},{7,5},{8,10},{9,11},{10,... | collective-permute-start | bytes 221192 | tf_op jit(solution)/shard_map/ppermute | solution.py:583
  30.1 10.8 %collective-permute-start.11 = (bf16[32,1152]{1,0:T(8,128)(2,1)S(1)}, bf16[32,1152]{1,0:T(8,128)(2,1)S(1)}, u32[]{:S(2)}, u32[]{:S(2)}) collective-permute-start(bf16[32,1152]{1,0:T(8,128)(2,1)S(1)} %collective-permute-done.10.refs_0_), channel_id=1, source_target_pairs={{0,1},{1,0},{2,3},{3,2},{4,5},{5,4},{6,7},{7,6},{8,9},{9,8},{10,11... | collective-permute-start | bytes 221192 | tf_op jit(solution)/shard_map/ppermute | solution.py:583
  42.5 6.5 %collective-permute-start.17 = (bf16[16,4736]{1,0:T(8,128)(2,1)S(1)}, bf16[16,4736]{1,0:T(8,128)(2,1)S(1)}, u32[]{:S(2)}, u32[]{:S(2)}) collective-permute-start(bf16[16,4736]{1,0:T(8,128)(2,1)S(1)} %get-tuple-element.112), channel_id=1, source_target_pairs={{0,8},{8,0},{16,24},{24,16},{1,9},{9,1},{17,25},{25,17},{2,10},{10... | collective-permute-start | bytes 454664 | tf_op jit(solution)/shard_map/ppermute | solution.py:596
  42.6 6.8 %collective-permute-start.18 = (bf16[16,4736]{1,0:T(8,128)(2,1)S(1)}, bf16[16,4736]{1,0:T(8,128)(2,1)S(1)}, u32[]{:S(2)}, u32[]{:S(2)}) collective-permute-start(bf16[16,4736]{1,0:T(8,128)(2,1)S(1)} %get-tuple-element.113), channel_id=1, source_target_pairs={{0,16},{8,24},{16,0},{24,8},{1,17},{9,25},{17,1},{25,9},{2,18},{10... | collective-permute-start | bytes 454664 | tf_op jit(solution)/shard_map/ppermute | solution.py:596
  44.2 7.6 %collective-permute-start.19 = (bf16[16,4736]{1,0:T(8,128)(2,1)S(1)}, bf16[16,4736]{1,0:T(8,128)(2,1)S(1)}, u32[]{:S(2)}, u32[]{:S(2)}) collective-permute-start(bf16[16,4736]{1,0:T(8,128)(2,1)S(1)} %get-tuple-element.114), channel_id=1, source_target_pairs={{0,24},{8,16},{16,8},{24,0},{1,25},{9,17},{17,9},{25,1},{2,26},{10... | collective-permute-start | bytes 454664 | tf_op jit(solution)/shard_map/ppermute | solution.py:596
  56.9 12.8 %collective-permute-start.24 = (bf16[16,4224]{1,0:T(8,128)(2,1)S(1)}, bf16[16,4224]{1,0:T(8,128)(2,1)S(1)}, u32[]{:S(2)}, u32[]{:S(2)}) collective-permute-start(bf16[16,4224]{1,0:T(8,128)(2,1)S(1)} %get-tuple-element.143), channel_id=1, source_target_pairs={{0,16},{8,24},{16,0},{24,8},{1,17},{9,25},{17,1},{25,9},{2,18},{10... | collective-permute-start | bytes 405512 | tf_op jit(solution)/shard_map/ppermute | solution.py:596
  58.5 11.2 %collective-permute-start.25 = (bf16[16,4224]{1,0:T(8,128)(2,1)S(1)}, bf16[16,4224]{1,0:T(8,128)(2,1)S(1)}, u32[]{:S(2)}, u32[]{:S(2)}) collective-permute-start(bf16[16,4224]{1,0:T(8,128)(2,1)S(1)} %get-tuple-element.144), channel_id=1, source_target_pairs={{0,24},{8,16},{16,8},{24,0},{1,25},{9,17},{17,9},{25,1},{2,26},{10... | collective-permute-start | bytes 405512 | tf_op jit(solution)/shard_map/ppermute | solution.py:596
  58.5 11.1 %collective-permute-start.20 = (bf16[16,4224]{1,0:T(8,128)(2,1)S(1)}, bf16[16,4224]{1,0:T(8,128)(2,1)S(1)}, u32[]{:S(2)}, u32[]{:S(2)}) collective-permute-start(bf16[16,4224]{1,0:T(8,128)(2,1)S(1)} %get-tuple-element.138), channel_id=1, source_target_pairs={{0,8},{8,0},{16,24},{24,16},{1,9},{9,1},{17,25},{25,17},{2,10},{10... | collective-permute-start | bytes 405512 | tf_op jit(solution)/shard_map/ppermute | solution.py:596
  59.1 10.6 %collective-permute-start.21 = (bf16[16,4224]{1,0:T(8,128)(2,1)S(1)}, bf16[16,4224]{1,0:T(8,128)(2,1)S(1)}, u32[]{:S(2)}, u32[]{:S(2)}) collective-permute-start(bf16[16,4224]{1,0:T(8,128)(2,1)S(1)} %get-tuple-element.139), channel_id=1, source_target_pairs={{0,16},{8,24},{16,0},{24,8},{1,17},{9,25},{17,1},{25,9},{2,18},{10... | collective-permute-start | bytes 405512 | tf_op jit(solution)/shard_map/ppermute | solution.py:596
  60.6 10.0 %collective-permute-start.22 = (bf16[16,4224]{1,0:T(8,128)(2,1)S(1)}, bf16[16,4224]{1,0:T(8,128)(2,1)S(1)}, u32[]{:S(2)}, u32[]{:S(2)}) collective-permute-start(bf16[16,4224]{1,0:T(8,128)(2,1)S(1)} %get-tuple-element.140), channel_id=1, source_target_pairs={{0,24},{8,16},{16,8},{24,0},{1,25},{9,17},{17,9},{25,1},{2,26},{10... | collective-permute-start | bytes 405512 | tf_op jit(solution)/shard_map/ppermute | solution.py:596
  72.7 6.0 %collective-permute-start.29 = (bf16[72,512]{1,0:T(8,128)(2,1)S(1)}, bf16[72,512]{1,0:T(8,128)(2,1)S(1)}, u32[]{:S(2)}, u32[]{:S(2)}) collective-permute-start(bf16[72,512]{1,0:T(8,128)(2,1)S(1)} %bitcast.54), channel_id=1, source_target_pairs={{0,1},{1,0},{2,3},{3,2},{4,5},{5,4},{6,7},{7,6},{8,9},{9,8},{10,11... | collective-permute-start | bytes 221192 | tf_op jit(solution)/shard_map/ppermute | solution.py:583
  73.4 6.4 %collective-permute-start.30 = (bf16[72,512]{1,0:T(8,128)(2,1)S(1)}, bf16[72,512]{1,0:T(8,128)(2,1)S(1)}, u32[]{:S(2)}, u32[]{:S(2)}) collective-permute-start(bf16[72,512]{1,0:T(8,128)(2,1)S(1)} %bitcast.53), channel_id=1, source_target_pairs={{0,2},{1,3},{2,0},{3,1},{4,6},{5,7},{6,4},{7,5},{8,10},{9,11},{10,... | collective-permute-start | bytes 221192 | tf_op jit(solution)/shard_map/ppermute | solution.py:583
  75.3 6.0 %collective-permute-start.31 = (bf16[72,512]{1,0:T(8,128)(2,1)S(1)}, bf16[72,512]{1,0:T(8,128)(2,1)S(1)}, u32[]{:S(2)}, u32[]{:S(2)}) collective-permute-start(bf16[72,512]{1,0:T(8,128)(2,1)S(1)} %bitcast.52), channel_id=1, source_target_pairs={{0,3},{1,2},{2,1},{3,0},{4,7},{5,6},{6,5},{7,4},{8,11},{9,10},{10,... | collective-permute-start | bytes 221192 | tf_op jit(solution)/shard_map/ppermute | solution.py:583
  76.3 7.0 %collective-permute-start.26 = (bf16[72,512]{1,0:T(8,128)(2,1)S(1)}, bf16[72,512]{1,0:T(8,128)(2,1)S(1)}, u32[]{:S(2)}, u32[]{:S(2)}) collective-permute-start(bf16[72,512]{1,0:T(8,128)(2,1)S(1)} %bitcast.51), channel_id=1, source_target_pairs={{0,1},{1,0},{2,3},{3,2},{4,5},{5,4},{6,7},{7,6},{8,9},{9,8},{10,11... | collective-permute-start | bytes 221192 | tf_op jit(solution)/shard_map/ppermute | solution.py:583
  76.8 6.5 %collective-permute-start.27 = (bf16[72,512]{1,0:T(8,128)(2,1)S(1)}, bf16[72,512]{1,0:T(8,128)(2,1)S(1)}, u32[]{:S(2)}, u32[]{:S(2)}) collective-permute-start(bf16[72,512]{1,0:T(8,128)(2,1)S(1)} %bitcast.50), channel_id=1, source_target_pairs={{0,2},{1,3},{2,0},{3,1},{4,6},{5,7},{6,4},{7,5},{8,10},{9,11},{10,... | collective-permute-start | bytes 221192 | tf_op jit(solution)/shard_map/ppermute | solution.py:583
  78.8 6.0 %collective-permute-start.28 = (bf16[72,512]{1,0:T(8,128)(2,1)S(1)}, bf16[72,512]{1,0:T(8,128)(2,1)S(1)}, u32[]{:S(2)}, u32[]{:S(2)}) collective-permute-start(bf16[72,512]{1,0:T(8,128)(2,1)S(1)} %bitcast.49), channel_id=1, source_target_pairs={{0,3},{1,2},{2,1},{3,0},{4,7},{5,6},{6,5},{7,4},{8,11},{9,10},{10,... | collective-permute-start | bytes 221192 | tf_op jit(solution)/shard_map/ppermute | solution.py:583
  81.5 6.1 %collective-permute-start.32 = (bf16[72,512]{1,0:T(8,128)(2,1)S(1)}, bf16[72,512]{1,0:T(8,128)(2,1)S(1)}, u32[]{:S(2)}, u32[]{:S(2)}) collective-permute-start(bf16[72,512]{1,0:T(8,128)(2,1)S(1)} %shard_map.198), channel_id=1, source_target_pairs={{0,4},{1,5},{2,6},{3,7},{4,0},{5,1},{6,2},{7,3},{8,12},{9,13},{10,... | collective-permute-start | bytes 221192 | tf_op jit(solution)/shard_map/ppermute | solution.py:583
  87.8 5.5 %collective-permute-start.33 = (bf16[64,512]{1,0:T(8,128)(2,1)S(1)}, bf16[64,512]{1,0:T(8,128)(2,1)S(1)}, u32[]{:S(2)}, u32[]{:S(2)}) collective-permute-start(bf16[64,512]{1,0:T(8,128)(2,1)S(1)} %bitcast.39), channel_id=1, source_target_pairs={{0,4},{1,5},{2,6},{3,7},{4,0},{5,1},{6,2},{7,3},{8,12},{9,13},{10,... | collective-permute-start | bytes 196616 | tf_op jit(solution)/shard_map/ppermute | solution.py:583
  88.9 7.1 %collective-permute-start.39 = (bf16[64,512]{1,0:T(8,128)(2,1)S(1)}, bf16[64,512]{1,0:T(8,128)(2,1)S(1)}, u32[]{:S(2)}, u32[]{:S(2)}) collective-permute-start(bf16[64,512]{1,0:T(8,128)(2,1)S(1)} %bitcast.40), channel_id=1, source_target_pairs={{0,3},{1,2},{2,1},{3,0},{4,7},{5,6},{6,5},{7,4},{8,11},{9,10},{10,... | collective-permute-start | bytes 196616 | tf_op jit(solution)/shard_map/ppermute | solution.py:583
  91.1 5.7 %collective-permute-start.38 = (bf16[64,512]{1,0:T(8,128)(2,1)S(1)}, bf16[64,512]{1,0:T(8,128)(2,1)S(1)}, u32[]{:S(2)}, u32[]{:S(2)}) collective-permute-start(bf16[64,512]{1,0:T(8,128)(2,1)S(1)} %bitcast.41), channel_id=1, source_target_pairs={{0,2},{1,3},{2,0},{3,1},{4,6},{5,7},{6,4},{7,5},{8,10},{9,11},{10,... | collective-permute-start | bytes 196616 | tf_op jit(solution)/shard_map/ppermute | solution.py:583
  91.1 5.7 %collective-permute-start.37 = (bf16[64,512]{1,0:T(8,128)(2,1)S(1)}, bf16[64,512]{1,0:T(8,128)(2,1)S(1)}, u32[]{:S(2)}, u32[]{:S(2)}) collective-permute-start(bf16[64,512]{1,0:T(8,128)(2,1)S(1)} %bitcast.42), channel_id=1, source_target_pairs={{0,1},{1,0},{2,3},{3,2},{4,5},{5,4},{6,7},{7,6},{8,9},{9,8},{10,11... | collective-permute-start | bytes 196616 | tf_op jit(solution)/shard_map/ppermute | solution.py:583
  93.3 6.2 %collective-permute-start.36 = (bf16[64,512]{1,0:T(8,128)(2,1)S(1)}, bf16[64,512]{1,0:T(8,128)(2,1)S(1)}, u32[]{:S(2)}, u32[]{:S(2)}) collective-permute-start(bf16[64,512]{1,0:T(8,128)(2,1)S(1)} %collective-permute-done.33.refs_0_), channel_id=1, source_target_pairs={{0,3},{1,2},{2,1},{3,0},{4,7},{5,6},{6,5},{7,4},{8,11},{9,10},{10,... | collective-permute-start | bytes 196616 | tf_op jit(solution)/shard_map/ppermute | solution.py:583
  125.6 16.1 %all-to-all-start.1 = ((bf16[32,24,256]{2,1,0:T(8,128)(2,1)}), bf16[32,24,256]{2,1,0:T(8,128)(2,1)S(1)}, u32[]{:S(2)}, u32[]{:S(2)}) async-start(bf16[32,24,256]{2,1,0:T(8,128)(2,1)} %bitcast.20), calls=%async_computation.1 | async-start | bytes 786432 | tf_op jit(solution)/shard_map/all_to_all | solution.py:578
  (27 other events, 387.3 us)

commit v7 on v6

--- a/solution.py
+++ b/solution.py
@@ -441,15 +441,14 @@
     )(*parts)
 
 
-def output_body(share, base_ref, weight_hbm, start_ref, *refs):
-    count = PIECES // SHARES
+def output_body(first, count, base_ref, weight_hbm, start_ref, *refs):
     rows_refs, out_refs = refs[:count], refs[count:-2]
     weight_ref, sems = refs[-2:]
     requests, _ = start_ref.shape
     width = weight_ref.shape[2]
     copies = []
     for k in range(count):
-        piece = share * count + k ^ base_ref[0]
+        piece = (first + k) ^ base_ref[0]
         copy = pltpu.make_async_copy(
             weight_hbm.at[:, pl.ds(pl.multiple_of(piece * width, width), width)],
             weight_ref.at[k],
@@ -465,7 +464,7 @@
                 rows_refs[k][j * requests : (j + 1) * requests, :],
                 weight_ref[k, :, j * LAT : (j + 1) * LAT],
             )
-    if share < SHARES - 1:
+    if first + count < PIECES:
         out_refs[0][...] = total
     else:
         out = total.astype(jnp.bfloat16)
@@ -474,9 +473,9 @@
             out_refs[1][c] = out
 
 
-def output_projection(share, base, rows, weight, start, copies):
+def output_projection(first, base, rows, weight, start, copies):
     features, width = weight.shape
-    last = share == SHARES - 1
+    last = first + len(rows) == PIECES
     if last:
         out = (
             jax.ShapeDtypeStruct(start.shape, jnp.bfloat16),
@@ -485,11 +484,11 @@
     else:
         out = jax.ShapeDtypeStruct(start.shape, jnp.float32)
     return call(
-        functools.partial(output_body, share),
+        functools.partial(output_body, first, len(rows)),
         out,
         8,
-        3e10 if last else 2 * start.shape[0] * features * width // SHARES,
-        2 * features * width // SHARES,
+        3e10 if last else 2 * start.shape[0] * features * width // 2,
+        features * width,
         in_specs=[pl.BlockSpec(memory_space=pltpu.SMEM), HBM, VMEM] + [VMEM] * len(rows),
         out_specs=(VMEM, VMEM) if last else VMEM,
         scratch_shapes=[
@@ -709,8 +708,17 @@
         pieces = [queries[k] for k in range(PIECES)]
     near, far = pieces[: PIECES // 2], pieces[PIECES // 2 :]
     arrived = [swap_owners(pick_queries(pick, extra, near))]
+    root_columns, suffix_rows = root_cache.T, suffix_cache.reshape(-1, KVW)
+    near, far[0] = lax.optimization_barrier((near, far[0]))
+    first = [own_attention(near, suffix_holder, root_columns, suffix_rows)]
+    far, first = lax.optimization_barrier((far, first))
+    sent = pick_queries(pick, extra, far)
+    arrived[0], sent = lax.optimization_barrier((arrived[0], sent))
+    arrived.append(swap_owners(sent))
+    answered = group_attention(arrived[0], group_columns, group_holder)
+    asked_rows, answered = lax.optimization_barrier((arrived[0], answered))
     all_routes = jnp.stack(
-        [x[:, HEADS * KVW + 1 : HEADS * KVW + 1 + named.shape[1]] for x in arrived[0]]
+        [x[:, HEADS * KVW + 1 : HEADS * KVW + 1 + named.shape[1]] for x in asked_rows]
     ).reshape(1, owners, requests, fanout)
     turned = owner_range[:, None] ^ owner_index == owner_range[None, :]
     all_routes = jnp.sum(
@@ -737,22 +745,11 @@
     expert_pick = jnp.concatenate(
         [expert_pick.reshape(owners * expert_slots, owners * requests), shared_pick], axis=0
     ).astype(jnp.bfloat16)
-    root_columns, suffix_rows = root_cache.T, suffix_cache.reshape(-1, KVW)
-    near, far[0] = lax.optimization_barrier((near, far[0]))
-    first = [own_attention(near, suffix_holder, root_columns, suffix_rows)]
-    far, first = lax.optimization_barrier((far, first))
-    sent = pick_queries(pick, extra, far)
-    arrived[0], sent = lax.optimization_barrier((arrived[0], sent))
-    arrived.append(swap_owners(sent))
-    back = []
-    for share in arrived:
-        if back:
-            share, answered = lax.optimization_barrier((share, answered))
-            back[0] = swap_owners(answered)
-        answered = group_attention(share, group_columns, group_holder)
-        back.append(swap_owners(answered))
-    far, answered, expert_pick = lax.optimization_barrier((far, answered, expert_pick))
-    back[1] = swap_owners(answered)
+    share, answered, expert_pick = lax.optimization_barrier((arrived[1], answered, expert_pick))
+    back = [swap_owners(answered)]
+    answered = group_attention(share, group_columns, group_holder)
+    far, answered = lax.optimization_barrier((far, answered))
+    back.append(swap_owners(answered))
     first.append(own_attention(far, suffix_holder, root_columns, suffix_rows))
     back, gain = lax.optimization_barrier((back, mixture_gain[None]))
     parts = local_join(unpick, first, sum(back, []), tensors // PIECES)
@@ -768,10 +765,10 @@
     else:
         attention = exchange(join(parts, tensors), "tensor").reshape(PIECES, -1, LAT)
         attention = [attention[k] for k in range(PIECES)]
-    half = PIECES // SHARES
-    total = output_projection(0, base, attention[:half], out_weight, hidden, 0)
-    rest, total = lax.optimization_barrier((attention[half:], total))
-    mid, copies = output_projection(1, base, rest, out_weight, total, pairs * tensors)
+    early = PIECES // 2 + 1
+    total = output_projection(0, base, attention[:early], out_weight, hidden, 0)
+    rest, total = lax.optimization_barrier((attention[early:], total))
+    mid, copies = output_projection(early, base, rest, out_weight, total, pairs * tensors)
 
     half = exchange(copies, ("pair", "tensor"))
     both = lax.all_gather(half.reshape((pairs, tensors) + mid.shape), "core")

time: 143 us -> 140 us (0.979)
  waiting for transfers between devices: 26.4 us -> 23.4 us
    ppermute x12, waiting for transfers between devices: 3.67 us -> 1.1 us  [swap_owners(): out[k] = lax.ppermute(arrays[k], OWNER, [(i, i ^ k) for i in range(count)])]
  transfers between devices with their start and end apart: 41 -> 41, of which waited for: 14 -> 11; matrix products, arithmetic and copies ran while one was open for 3% -> 5% of each run, Pallas kernels for 18% -> 22%
where the time goes in v7:
time: 140 us
  Pallas kernels  47.1 us (34%)
  starting transfers between devices  46.4 us (33%)
  waiting for transfers between devices  23.4 us (17%)
  blocking collectives  15.2 us (11%)
  local copies, waits for them, and re-layouts  4.73 us (3%)
  other arithmetic  2.43 us (2%)
    ppermute x28, starting transfers between devices, turn(): return lax.ppermute(x, 'tensor', [(i, i ^ k) for i in range(count)])  36 us
    pallas_call x2, Pallas kernels, own_attention(): call(own_body, pltpu.HBM((count, LAT + LANES), jnp.float32), 44, 2 * coun...  18.1 us
    all_to_all x1, blocking collectives, exchange(): return lax.all_to_all(x, axis, 0, 0, tiled=True)  12.8 us
    all_to_all x1, waiting for transfers between devices, exchange(): return lax.all_to_all(x, axis, 0, 0, tiled=True)  12.1 us
    ppermute x28, waiting for transfers between devices, turn(): return lax.ppermute(x, 'tensor', [(i, i ^ k) for i in range(count)])  10.2 us
    pallas_call x2, Pallas kernels, group_attention(): call(functools.partial(group_body, owners), (out,) * owners, 40, 2 * owne...  9.28 us
    ppermute x12, starting transfers between devices, swap_owners(): out[k] = lax.ppermute(arrays[k], OWNER, [(i, i ^ k) for i in range(count)])  7.87 us
    pallas_call x1, Pallas kernels, expert(): call(expert_body, jax.ShapeDtypeStruct((owners, PIECES, slots + requests...  6.84 us
  transfers between devices with their start and end apart: 41, of which 11 were waited for; matrix products, arithmetic and copies ran while one was open for 5% of the time, Pallas kernels for 22%

profile of v7, /device:TPU:0, one launch (start us, length us, event | category | flops | bytes accessed | tf_op | source)
XLA Modules:
  0.0 139.9 jit_solution(11085798015200658293)
XLA Ops:
  0.0 4.1 %collective-permute-start.3 = (bf16[32,256]{1,0:T(8,128)(2,1)}, bf16[32,256]{1,0:T(8,128)(2,1)S(1)}, u32[]{:S(2)}, u32[]{:S(2)}) collective-permute-start(bf16[32,256]{1,0:T(8,128)(2,1)} %start_ref.1), channel_id=1, source_target_pairs={{0,4},{1,5},{2,6},{3,7},{4,0},{5,1},{6,2},{7,3},{8,12},{9,13},{10,... | collective-permute-start | bytes 49160 | tf_op jit(solution)/shard_map/ppermute | solution.py:582
  4.1 2.5 %collective-permute-start.2 = (bf16[32,256]{1,0:T(8,128)(2,1)}, bf16[32,256]{1,0:T(8,128)(2,1)S(1)}, u32[]{:S(2)}, u32[]{:S(2)}) collective-permute-start(bf16[32,256]{1,0:T(8,128)(2,1)} %start_ref.1), channel_id=1, source_target_pairs={{0,3},{1,2},{2,1},{3,0},{4,7},{5,6},{6,5},{7,4},{8,11},{9,10},{10,... | collective-permute-start | bytes 49160 | tf_op jit(solution)/shard_map/ppermute | solution.py:582
  8.4 2.6 %collective-permute-start.6 = (bf16[32,256]{1,0:T(8,128)(2,1)S(1)}, bf16[32,256]{1,0:T(8,128)(2,1)S(1)}, u32[]{:S(2)}, u32[]{:S(2)}) collective-permute-start(bf16[32,256]{1,0:T(8,128)(2,1)S(1)} %collective-permute-done.3.refs_4_), channel_id=1, source_target_pairs={{0,3},{1,2},{2,1},{3,0},{4,7},{5,6},{6,5},{7,4},{8,11},{9,10},{10,... | collective-permute-start | bytes 49160 | tf_op jit(solution)/shard_map/ppermute | solution.py:582
  15.8 3.4 %shard_map.190.refs_0_ = bf16[32,1152]{1,0:T(8,128)(2,1)S(1)} custom-call(s32[1]{0:T(128)} %bitcast.base_ref, bf16[1,2048]{1,0:T(2,128)(2,1)S(1)} %broadcast_in_dim.228.gain_ref, bf16[1152,2048]{1,0:T(8,128)(2,1)} %weight_hbm.3, bf16[32,256]{1,0:T(8,128)(2,1)S(1)} %copy-done.3, bf16[32,256]{1,0:T(8,128)(2,1)S(1)} %collective-permute-done.refs_1_, ...), custom_call_target="tpu_custom_call" | custom-call | flops 150994944 | bytes 4718592 | tf_op jit(solution)/shard_map/pallas_call | solution.py:108
  19.9 1.6 %collective-permute-start.9 = (bf16[32,1152]{1,0:T(8,128)(2,1)S(1)}, bf16[32,1152]{1,0:T(8,128)(2,1)S(1)}, u32[]{:S(2)}, u32[]{:S(2)}) collective-permute-start(bf16[32,1152]{1,0:T(8,128)(2,1)S(1)} %shard_map.190.refs_0_), channel_id=1, source_target_pairs={{0,3},{1,2},{2,1},{3,0},{4,7},{5,6},{6,5},{7,4},{8,11},{9,10},{10,... | collective-permute-start | bytes 221192 | tf_op jit(solution)/shard_map/ppermute | solution.py:582
  21.9 1.5 %collective-permute-start.7 = (bf16[32,1152]{1,0:T(8,128)(2,1)S(1)}, bf16[32,1152]{1,0:T(8,128)(2,1)S(1)}, u32[]{:S(2)}, u32[]{:S(2)}) collective-permute-start(bf16[32,1152]{1,0:T(8,128)(2,1)S(1)} %shard_map.190.refs_0_), channel_id=1, source_target_pairs={{0,1},{1,0},{2,3},{3,2},{4,5},{5,4},{6,7},{7,6},{8,9},{9,8},{10,11... | collective-permute-start | bytes 221192 | tf_op jit(solution)/shard_map/ppermute | solution.py:582
  24.7 1.4 %collective-permute-start.16 = (bf16[32,1152]{1,0:T(8,128)(2,1)S(1)}, bf16[32,1152]{1,0:T(8,128)(2,1)S(1)}, u32[]{:S(2)}, u32[]{:S(2)}) collective-permute-start(bf16[32,1152]{1,0:T(8,128)(2,1)S(1)} %collective-permute-done.13.refs_0_), channel_id=1, source_target_pairs={{0,3},{1,2},{2,1},{3,0},{4,7},{5,6},{6,5},{7,4},{8,11},{9,10},{10,... | collective-permute-start | bytes 221192 | tf_op jit(solution)/shard_map/ppermute | solution.py:582
  27.3 1.6 %collective-permute-start.11 = (bf16[16,4736]{1,0:T(8,128)(2,1)S(1)}, bf16[16,4736]{1,0:T(8,128)(2,1)S(1)}, u32[]{:S(2)}, u32[]{:S(2)}) collective-permute-start(bf16[16,4736]{1,0:T(8,128)(2,1)S(1)} %get-tuple-element.101), channel_id=1, source_target_pairs={{0,16},{8,24},{16,0},{24,8},{1,17},{9,25},{17,1},{25,9},{2,18},{10... | collective-permute-start | bytes 454664 | tf_op jit(solution)/shard_map/ppermute | solution.py:595
  30.1 1.5 %collective-permute-start.14 = (bf16[32,1152]{1,0:T(8,128)(2,1)S(1)}, bf16[32,1152]{1,0:T(8,128)(2,1)S(1)}, u32[]{:S(2)}, u32[]{:S(2)}) collective-permute-start(bf16[32,1152]{1,0:T(8,128)(2,1)S(1)} %collective-permute-done.13.refs_0_), channel_id=1, source_target_pairs={{0,1},{1,0},{2,3},{3,2},{4,5},{5,4},{6,7},{7,6},{8,9},{9,8},{10,11... | collective-permute-start | bytes 221192 | tf_op jit(solution)/shard_map/ppermute | solution.py:582
  31.6 9.0 %shard_map.192.refs_0_ = f32[256,640]{1,0:T(8,128)} custom-call(s32[1,2048]{1,0:T(1,128)S(1)} %select_n.119.holder_ref, bf16[576,4096]{1,0:T(8,128)(2,1)} %bitcast.59, bf16[2048,576]{1,0:T(8,128)(2,1)} %bitcast.61, bf16[32,1152]{1,0:T(8,128)(2,1)S(1)} %shard_map.190.refs_0_, bf16[32,1152]{1,0:T(8,128)(2,1)S(1)} %collective-permute-done.7.refs_1_, ...), custom_call_target="tpu_custom_call" | custom-call | flops 2852126720 | bytes 7077888 | tf_op jit(solution)/shard_map/pallas_call | solution.py:223
  41.0 1.6 %collective-permute-start.18 = (bf16[16,4736]{1,0:T(8,128)(2,1)S(1)}, bf16[16,4736]{1,0:T(8,128)(2,1)S(1)}, u32[]{:S(2)}, u32[]{:S(2)}) collective-permute-start(bf16[16,4736]{1,0:T(8,128)(2,1)S(1)} %get-tuple-element.119), channel_id=1, source_target_pairs={{0,16},{8,24},{16,0},{24,8},{1,17},{9,25},{17,1},{25,9},{2,18},{10... | collective-permute-start | bytes 454664 | tf_op jit(solution)/shard_map/ppermute | solution.py:595
  42.9 4.5 %shard_map.194 = (bf16[16,4224]{1,0:T(8,128)(2,1)S(1)}, bf16[16,4224]{1,0:T(8,128)(2,1)S(1)}, bf16[16,4224]{1,0:T(8,128)(2,1)S(1)}, bf16[16,4224]{1,0:T(8,128)(2,1)S(1)}) custom-call(bf16[12,576,128]{2,1,0:T(8,128)(2,1)} %bitcast.63, f32[1,1536]{1,0:T(1,128)S(1)} %bitcast.47, bf16[16,4736]{1,0:T(8,128)(2,1)S(1)} %get-tuple-element.134.refs_0_, ...), custom_call_target="tpu_custom_call" | custom-call | flops 1711276032 | bytes 1769472 | tf_op jit(solution)/shard_map/pallas_call | solution.py:306
  50.5 1.5 %collective-permute-start.21 = (bf16[16,4224]{1,0:T(8,128)(2,1)S(1)}, bf16[16,4224]{1,0:T(8,128)(2,1)S(1)}, u32[]{:S(2)}, u32[]{:S(2)}) collective-permute-start(bf16[16,4224]{1,0:T(8,128)(2,1)S(1)} %get-tuple-element.154), channel_id=1, source_target_pairs={{0,16},{8,24},{16,0},{24,8},{1,17},{9,25},{17,1},{25,9},{2,18},{10... | collective-permute-start | bytes 405512 | tf_op jit(solution)/shard_map/ppermute | solution.py:595
  52.1 4.7 %shard_map.195 = (bf16[16,4224]{1,0:T(8,128)(2,1)S(1)}, bf16[16,4224]{1,0:T(8,128)(2,1)S(1)}, bf16[16,4224]{1,0:T(8,128)(2,1)S(1)}, bf16[16,4224]{1,0:T(8,128)(2,1)S(1)}) custom-call(bf16[12,576,128]{2,1,0:T(8,128)(2,1)} %bitcast.64, f32[1,1536]{1,0:T(1,128)S(1)} %bitcast.48, bf16[16,4736]{1,0:T(8,128)(2,1)S(1)} %get-tuple-element.140.refs_0_, ...), custom_call_target="tpu_custom_call" | custom-call | flops 1711276032 | bytes 1769472 | tf_op jit(solution)/shard_map/pallas_call | solution.py:306
  57.4 1.5 %collective-permute-start.24 = (bf16[16,4224]{1,0:T(8,128)(2,1)S(1)}, bf16[16,4224]{1,0:T(8,128)(2,1)S(1)}, u32[]{:S(2)}, u32[]{:S(2)}) collective-permute-start(bf16[16,4224]{1,0:T(8,128)(2,1)S(1)} %get-tuple-element.158), channel_id=1, source_target_pairs={{0,16},{8,24},{16,0},{24,8},{1,17},{9,25},{17,1},{25,9},{2,18},{10... | collective-permute-start | bytes 405512 | tf_op jit(solution)/shard_map/ppermute | solution.py:595
  59.0 9.0 %shard_map.196.refs_1_ = f32[256,640]{1,0:T(8,128)} custom-call(s32[1,2048]{1,0:T(1,128)S(1)} %select_n.119.holder_ref, bf16[576,4096]{1,0:T(8,128)(2,1)} %bitcast.60, bf16[2048,576]{1,0:T(8,128)(2,1)} %bitcast.62, bf16[32,1152]{1,0:T(8,128)(2,1)S(1)} %collective-permute-done.13.refs_0_, bf16[32,1152]{1,0:T(8,128)(2,1)S(1)} %collective-permute-done.14.refs_1_, ...), custom_call_target="tpu_custom_call" | custom-call | flops 2852126720 | bytes 7077888 | tf_op jit(solution)/shard_map/pallas_call | solution.py:223
  68.0 2.1 %shard_map.197 = (bf16[1,72,512]{2,1,0:T(8,128)(2,1)S(1)}, bf16[1,72,512]{2,1,0:T(8,128)(2,1)S(1)}, bf16[1,72,512]{2,1,0:T(8,128)(2,1)S(1)}, bf16[1,72,512]{2,1,...) custom-call(bf16[32,64]{1,0:T(8,128)(2,1)S(1)} %and_convert_fusion.u, ...), custom_call_target="tpu_custom_call" | custom-call | flops 33554432 | bytes 1048576 | tf_op jit(solution)/shard_map/pallas_call | solution.py:394
  70.8 2.1 %collective-permute-start.30 = (bf16[72,512]{1,0:T(8,128)(2,1)S(1)}, bf16[72,512]{1,0:T(8,128)(2,1)S(1)}, u32[]{:S(2)}, u32[]{:S(2)}) collective-permute-start(bf16[72,512]{1,0:T(8,128)(2,1)S(1)} %bitcast.53), channel_id=1, source_target_pairs={{0,2},{1,3},{2,0},{3,1},{4,6},{5,7},{6,4},{7,5},{8,10},{9,11},{10,... | collective-permute-start | bytes 221192 | tf_op jit(solution)/shard_map/ppermute | solution.py:582
  74.3 2.0 %collective-permute-start.27 = (bf16[72,512]{1,0:T(8,128)(2,1)S(1)}, bf16[72,512]{1,0:T(8,128)(2,1)S(1)}, u32[]{:S(2)}, u32[]{:S(2)}) collective-permute-start(bf16[72,512]{1,0:T(8,128)(2,1)S(1)} %bitcast.50), channel_id=1, source_target_pairs={{0,2},{1,3},{2,0},{3,1},{4,6},{5,7},{6,4},{7,5},{8,10},{9,11},{10,... | collective-permute-start | bytes 221192 | tf_op jit(solution)/shard_map/ppermute | solution.py:582
  77.2 1.6 %collective-permute-done.31.refs_3_ = bf16[72,512]{1,0:T(8,128)(2,1)S(1)} collective-permute-done((bf16[72,512]{1,0:T(8,128)(2,1)S(1)}, bf16[72,512]{1,0:T(8,128)(2,1)S(1)}, u32[]{:S(2)}, u32[]{:S(2)}) %collective-permute-start.31) | collective-permute-done | bytes 73760 | tf_op jit(solution)/shard_map/ppermute | solution.py:582
  79.0 1.8 %collective-permute-start.32 = (bf16[72,512]{1,0:T(8,128)(2,1)S(1)}, bf16[72,512]{1,0:T(8,128)(2,1)S(1)}, u32[]{:S(2)}, u32[]{:S(2)}) collective-permute-start(bf16[72,512]{1,0:T(8,128)(2,1)S(1)} %shard_map.198), channel_id=1, source_target_pairs={{0,4},{1,5},{2,6},{3,7},{4,0},{5,1},{6,2},{7,3},{8,12},{9,13},{10,... | collective-permute-start | bytes 221192 | tf_op jit(solution)/shard_map/ppermute | solution.py:582
  80.8 1.6 %collective-permute-done.28.refs_3_ = bf16[72,512]{1,0:T(8,128)(2,1)S(1)} collective-permute-done((bf16[72,512]{1,0:T(8,128)(2,1)S(1)}, bf16[72,512]{1,0:T(8,128)(2,1)S(1)}, u32[]{:S(2)}, u32[]{:S(2)}) %collective-permute-start.28) | collective-permute-done | bytes 73760 | tf_op jit(solution)/shard_map/ppermute | solution.py:582
  82.4 2.8 %collective-permute-done.32.refs_4_ = bf16[72,512]{1,0:T(8,128)(2,1)S(1)} collective-permute-done((bf16[72,512]{1,0:T(8,128)(2,1)S(1)}, bf16[72,512]{1,0:T(8,128)(2,1)S(1)}, u32[]{:S(2)}, u32[]{:S(2)}) %collective-permute-start.32) | collective-permute-done | bytes 73760 | tf_op jit(solution)/shard_map/ppermute | solution.py:582
  86.4 2.1 %collective-permute-start.39 = (bf16[64,512]{1,0:T(8,128)(2,1)S(1)}, bf16[64,512]{1,0:T(8,128)(2,1)S(1)}, u32[]{:S(2)}, u32[]{:S(2)}) collective-permute-start(bf16[64,512]{1,0:T(8,128)(2,1)S(1)} %bitcast.40), channel_id=1, source_target_pairs={{0,3},{1,2},{2,1},{3,0},{4,7},{5,6},{6,5},{7,4},{8,11},{9,10},{10,... | collective-permute-start | bytes 196616 | tf_op jit(solution)/shard_map/ppermute | solution.py:582
  91.9 1.7 %collective-permute-start.35 = (bf16[64,512]{1,0:T(8,128)(2,1)S(1)}, bf16[64,512]{1,0:T(8,128)(2,1)S(1)}, u32[]{:S(2)}, u32[]{:S(2)}) collective-permute-start(bf16[64,512]{1,0:T(8,128)(2,1)S(1)} %collective-permute-done.33.refs_4_), channel_id=1, source_target_pairs={{0,2},{1,3},{2,0},{3,1},{4,6},{5,7},{6,4},{7,5},{8,10},{9,11},{10,... | collective-permute-start | bytes 196616 | tf_op jit(solution)/shard_map/ppermute | solution.py:582
  94.4 2.7 %shard_map.200.start_ref = f32[32,256]{1,0:T(8,128)S(1)} custom-call(s32[1]{0:T(128)} %bitcast.base_ref, bf16[256,8192]{1,0:T(8,128)(2,1)} %weight_hbm.5, bf16[32,256]{1,0:T(8,128)(2,1)S(1)} %copy-done.4, bf16[64,512]{1,0:T(8,128)(2,1)S(1)} %bitcast.43, bf16[64,512]{1,0:T(8,128)(2,1)S(1)} %collective-permute-done.37.refs_1_, ...), custom_call_target="tpu_custom_call" | custom-call | flops 67108864 | bytes 2097152 | tf_op jit(solution)/shard_map/pallas_call | solution.py:486
  97.9 2.8 %shard_map.201 = (bf16[32,256]{1,0:T(8,128)(2,1)S(1)}, bf16[16,32,256]{2,1,0:T(8,128)(2,1)S(1)}) custom-call(s32[1]{0:T(128)} %bitcast.base_ref, bf16[256,8192]{1,0:T(8,128)(2,1)} %weight_hbm.5, f32[32,256]{1,0:T(8,128)S(1)} %shard_map.200.start_ref, bf16[64,512]{1,0:T(8,128)(2,1)S(1)} %collective-permute-done.34.refs_0_, ...), custom_call_target="tpu_custom_call" | custom-call | flops 30000001024 | bytes 2097152 | tf_op jit(solution)/shard_map/pallas_call | solution.py:486
  100.7 12.8 %all_to_all.10 = bf16[16,32,256]{2,1,0:T(8,128)(2,1)S(1)} all-to-all(bf16[16,32,256]{2,1,0:T(8,128)(2,1)S(1)} %get-tuple-element.180), channel_id=1, replica_groups=mesh['pair'=2,'core'=2,'tensor'=8] {'pair','tensor'}, dimensions={0} | all-to-all | bytes 524288 | tf_op jit(solution)/shard_map/all_to_all | solution.py:577
  113.5 2.4 %all_gather.3 = bf16[2,2,8,32,256]{4,3,2,1,0:T(8,128)(2,1)S(1)} all-gather(bf16[1,2,8,32,256]{4,3,2,1,0:T(8,128)(2,1)S(1)} %bitcast.55), channel_id=1, replica_groups=mesh['pair'=2,'core'=2,'tensor'=8] {'core'}, dimensions={0}, use_global_device_ids=true | all-gather | bytes 786432 | tf_op jit(solution)/shard_map/all_gather | solution.py:774
  116.0 6.8 %shard_map.202 = bf16[4,8,24,256]{3,2,1,0:T(8,128)(2,1)} custom-call(bf16[96,128]{1,0:T(8,128)(2,1)S(1)} %add_convert_fusion.pick_ref, bf16[4,8,32,256]{3,2,1,0:T(8,128)(2,1)S(1)} %bitcast.37, bf16[1,2048]{1,0:T(2,128)(2,1)S(1)} %broadcast_in_dim.248.gain_ref, bf16[352,2048]{1,0:T(8,128)(2,1)S(1)} %copy-done, bf16[352,2048]{1,0:T(8,128)(2,1)S(1)} %copy-done.1, ...), custom_call_target="tpu_custom_call" | custom-call | flops 1660944384 | bytes 17301504 | tf_op jit(solution)/shard_map/pallas_call | solution.py:542
  122.8 2.6 %all-to-all-start.1 = ((bf16[32,24,256]{2,1,0:T(8,128)(2,1)}), bf16[32,24,256]{2,1,0:T(8,128)(2,1)S(1)}, u32[]{:S(2)}, u32[]{:S(2)}) async-start(bf16[32,24,256]{2,1,0:T(8,128)(2,1)} %bitcast.20), calls=%async_computation.1 | async-start | bytes 786432 | tf_op jit(solution)/shard_map/all_to_all | solution.py:577
  126.9 12.1 %all-to-all-done.1 = bf16[32,24,256]{2,1,0:T(8,128)(2,1)S(1)} async-done(((bf16[32,24,256]{2,1,0:T(8,128)(2,1)}), bf16[32,24,256]{2,1,0:T(8,128)(2,1)S(1)}, u32[]{:S(2)}, u32[]{:S(2)}) %all-to-all-start.1) | async-done | bytes 393248 | tf_op jit(solution)/shard_map/all_to_all | solution.py:577
  (175 shorter events, 27.1 us)
Async XLA Ops:
  0.0 8.3 %collective-permute-start.3 = (bf16[32,256]{1,0:T(8,128)(2,1)}, bf16[32,256]{1,0:T(8,128)(2,1)S(1)}, u32[]{:S(2)}, u32[]{:S(2)}) collective-permute-start(bf16[32,256]{1,0:T(8,128)(2,1)} %start_ref.1), channel_id=1, source_target_pairs={{0,4},{1,5},{2,6},{3,7},{4,0},{5,1},{6,2},{7,3},{8,12},{9,13},{10,... | collective-permute-start | bytes 49160 | tf_op jit(solution)/shard_map/ppermute | solution.py:582
  4.1 7.3 %collective-permute-start.2 = (bf16[32,256]{1,0:T(8,128)(2,1)}, bf16[32,256]{1,0:T(8,128)(2,1)S(1)}, u32[]{:S(2)}, u32[]{:S(2)}) collective-permute-start(bf16[32,256]{1,0:T(8,128)(2,1)} %start_ref.1), channel_id=1, source_target_pairs={{0,3},{1,2},{2,1},{3,0},{4,7},{5,6},{6,5},{7,4},{8,11},{9,10},{10,... | collective-permute-start | bytes 49160 | tf_op jit(solution)/shard_map/ppermute | solution.py:582
  6.6 6.8 %collective-permute-start.1 = (bf16[32,256]{1,0:T(8,128)(2,1)}, bf16[32,256]{1,0:T(8,128)(2,1)S(1)}, u32[]{:S(2)}, u32[]{:S(2)}) collective-permute-start(bf16[32,256]{1,0:T(8,128)(2,1)} %start_ref.1), channel_id=1, source_target_pairs={{0,2},{1,3},{2,0},{3,1},{4,6},{5,7},{6,4},{7,5},{8,10},{9,11},{10,... | collective-permute-start | bytes 49160 | tf_op jit(solution)/shard_map/ppermute | solution.py:582
  7.1 6.3 %collective-permute-start = (bf16[32,256]{1,0:T(8,128)(2,1)}, bf16[32,256]{1,0:T(8,128)(2,1)S(1)}, u32[]{:S(2)}, u32[]{:S(2)}) collective-permute-start(bf16[32,256]{1,0:T(8,128)(2,1)} %start_ref.1), channel_id=1, source_target_pairs={{0,1},{1,0},{2,3},{3,2},{4,5},{5,4},{6,7},{7,6},{8,9},{9,8},{10,11... | collective-permute-start | bytes 49160 | tf_op jit(solution)/shard_map/ppermute | solution.py:582
  19.9 6.5 %collective-permute-start.9 = (bf16[32,1152]{1,0:T(8,128)(2,1)S(1)}, bf16[32,1152]{1,0:T(8,128)(2,1)S(1)}, u32[]{:S(2)}, u32[]{:S(2)}) collective-permute-start(bf16[32,1152]{1,0:T(8,128)(2,1)S(1)} %shard_map.190.refs_0_), channel_id=1, source_target_pairs={{0,3},{1,2},{2,1},{3,0},{4,7},{5,6},{6,5},{7,4},{8,11},{9,10},{10,... | collective-permute-start | bytes 221192 | tf_op jit(solution)/shard_map/ppermute | solution.py:582
  27.2 13.7 %collective-permute-start.10 = (bf16[16,4736]{1,0:T(8,128)(2,1)S(1)}, bf16[16,4736]{1,0:T(8,128)(2,1)S(1)}, u32[]{:S(2)}, u32[]{:S(2)}) collective-permute-start(bf16[16,4736]{1,0:T(8,128)(2,1)S(1)} %get-tuple-element.100), channel_id=1, source_target_pairs={{0,8},{8,0},{16,24},{24,16},{1,9},{9,1},{17,25},{25,17},{2,10},{10... | collective-permute-start | bytes 454664 | tf_op jit(solution)/shard_map/ppermute | solution.py:595
  27.3 13.7 %collective-permute-start.11 = (bf16[16,4736]{1,0:T(8,128)(2,1)S(1)}, bf16[16,4736]{1,0:T(8,128)(2,1)S(1)}, u32[]{:S(2)}, u32[]{:S(2)}) collective-permute-start(bf16[16,4736]{1,0:T(8,128)(2,1)S(1)} %get-tuple-element.101), channel_id=1, source_target_pairs={{0,16},{8,24},{16,0},{24,8},{1,17},{9,25},{17,1},{25,9},{2,18},{10... | collective-permute-start | bytes 454664 | tf_op jit(solution)/shard_map/ppermute | solution.py:595
  28.9 12.1 %collective-permute-start.12 = (bf16[16,4736]{1,0:T(8,128)(2,1)S(1)}, bf16[16,4736]{1,0:T(8,128)(2,1)S(1)}, u32[]{:S(2)}, u32[]{:S(2)}) collective-permute-start(bf16[16,4736]{1,0:T(8,128)(2,1)S(1)} %get-tuple-element.102), channel_id=1, source_target_pairs={{0,24},{8,16},{16,8},{24,0},{1,25},{9,17},{17,9},{25,1},{2,26},{10... | collective-permute-start | bytes 454664 | tf_op jit(solution)/shard_map/ppermute | solution.py:595
  29.1 11.5 %collective-permute-start.15 = (bf16[32,1152]{1,0:T(8,128)(2,1)S(1)}, bf16[32,1152]{1,0:T(8,128)(2,1)S(1)}, u32[]{:S(2)}, u32[]{:S(2)}) collective-permute-start(bf16[32,1152]{1,0:T(8,128)(2,1)S(1)} %collective-permute-done.13.refs_0_), channel_id=1, source_target_pairs={{0,2},{1,3},{2,0},{3,1},{4,6},{5,7},{6,4},{7,5},{8,10},{9,11},{10,... | collective-permute-start | bytes 221192 | tf_op jit(solution)/shard_map/ppermute | solution.py:582
  30.1 10.5 %collective-permute-start.14 = (bf16[32,1152]{1,0:T(8,128)(2,1)S(1)}, bf16[32,1152]{1,0:T(8,128)(2,1)S(1)}, u32[]{:S(2)}, u32[]{:S(2)}) collective-permute-start(bf16[32,1152]{1,0:T(8,128)(2,1)S(1)} %collective-permute-done.13.refs_0_), channel_id=1, source_target_pairs={{0,1},{1,0},{2,3},{3,2},{4,5},{5,4},{6,7},{7,6},{8,9},{9,8},{10,11... | collective-permute-start | bytes 221192 | tf_op jit(solution)/shard_map/ppermute | solution.py:582
  41.0 8.1 %collective-permute-start.17 = (bf16[16,4736]{1,0:T(8,128)(2,1)S(1)}, bf16[16,4736]{1,0:T(8,128)(2,1)S(1)}, u32[]{:S(2)}, u32[]{:S(2)}) collective-permute-start(bf16[16,4736]{1,0:T(8,128)(2,1)S(1)} %get-tuple-element.118), channel_id=1, source_target_pairs={{0,8},{8,0},{16,24},{24,16},{1,9},{9,1},{17,25},{25,17},{2,10},{10... | collective-permute-start | bytes 454664 | tf_op jit(solution)/shard_map/ppermute | solution.py:595
  41.0 8.1 %collective-permute-start.18 = (bf16[16,4736]{1,0:T(8,128)(2,1)S(1)}, bf16[16,4736]{1,0:T(8,128)(2,1)S(1)}, u32[]{:S(2)}, u32[]{:S(2)}) collective-permute-start(bf16[16,4736]{1,0:T(8,128)(2,1)S(1)} %get-tuple-element.119), channel_id=1, source_target_pairs={{0,16},{8,24},{16,0},{24,8},{1,17},{9,25},{17,1},{25,9},{2,18},{10... | collective-permute-start | bytes 454664 | tf_op jit(solution)/shard_map/ppermute | solution.py:595
  42.6 7.6 %collective-permute-start.19 = (bf16[16,4736]{1,0:T(8,128)(2,1)S(1)}, bf16[16,4736]{1,0:T(8,128)(2,1)S(1)}, u32[]{:S(2)}, u32[]{:S(2)}) collective-permute-start(bf16[16,4736]{1,0:T(8,128)(2,1)S(1)} %get-tuple-element.120), channel_id=1, source_target_pairs={{0,24},{8,16},{16,8},{24,0},{1,25},{9,17},{17,9},{25,1},{2,26},{10... | collective-permute-start | bytes 454664 | tf_op jit(solution)/shard_map/ppermute | solution.py:595
  50.2 8.8 %collective-permute-start.20 = (bf16[16,4224]{1,0:T(8,128)(2,1)S(1)}, bf16[16,4224]{1,0:T(8,128)(2,1)S(1)}, u32[]{:S(2)}, u32[]{:S(2)}) collective-permute-start(bf16[16,4224]{1,0:T(8,128)(2,1)S(1)} %get-tuple-element.153), channel_id=1, source_target_pairs={{0,8},{8,0},{16,24},{24,16},{1,9},{9,1},{17,25},{25,17},{2,10},{10... | collective-permute-start | bytes 405512 | tf_op jit(solution)/shard_map/ppermute | solution.py:595
  50.5 17.5 %collective-permute-start.21 = (bf16[16,4224]{1,0:T(8,128)(2,1)S(1)}, bf16[16,4224]{1,0:T(8,128)(2,1)S(1)}, u32[]{:S(2)}, u32[]{:S(2)}) collective-permute-start(bf16[16,4224]{1,0:T(8,128)(2,1)S(1)} %get-tuple-element.154), channel_id=1, source_target_pairs={{0,16},{8,24},{16,0},{24,8},{1,17},{9,25},{17,1},{25,9},{2,18},{10... | collective-permute-start | bytes 405512 | tf_op jit(solution)/shard_map/ppermute | solution.py:595
  52.0 16.0 %collective-permute-start.22 = (bf16[16,4224]{1,0:T(8,128)(2,1)S(1)}, bf16[16,4224]{1,0:T(8,128)(2,1)S(1)}, u32[]{:S(2)}, u32[]{:S(2)}) collective-permute-start(bf16[16,4224]{1,0:T(8,128)(2,1)S(1)} %get-tuple-element.155), channel_id=1, source_target_pairs={{0,24},{8,16},{16,8},{24,0},{1,25},{9,17},{17,9},{25,1},{2,26},{10... | collective-permute-start | bytes 405512 | tf_op jit(solution)/shard_map/ppermute | solution.py:595
  56.8 11.2 %collective-permute-start.23 = (bf16[16,4224]{1,0:T(8,128)(2,1)S(1)}, bf16[16,4224]{1,0:T(8,128)(2,1)S(1)}, u32[]{:S(2)}, u32[]{:S(2)}) collective-permute-start(bf16[16,4224]{1,0:T(8,128)(2,1)S(1)} %get-tuple-element.157), channel_id=1, source_target_pairs={{0,8},{8,0},{16,24},{24,16},{1,9},{9,1},{17,25},{25,17},{2,10},{10... | collective-permute-start | bytes 405512 | tf_op jit(solution)/shard_map/ppermute | solution.py:595
  57.4 10.6 %collective-permute-start.24 = (bf16[16,4224]{1,0:T(8,128)(2,1)S(1)}, bf16[16,4224]{1,0:T(8,128)(2,1)S(1)}, u32[]{:S(2)}, u32[]{:S(2)}) collective-permute-start(bf16[16,4224]{1,0:T(8,128)(2,1)S(1)} %get-tuple-element.158), channel_id=1, source_target_pairs={{0,16},{8,24},{16,0},{24,8},{1,17},{9,25},{17,1},{25,9},{2,18},{10... | collective-permute-start | bytes 405512 | tf_op jit(solution)/shard_map/ppermute | solution.py:595
  59.0 9.1 %collective-permute-start.25 = (bf16[16,4224]{1,0:T(8,128)(2,1)S(1)}, bf16[16,4224]{1,0:T(8,128)(2,1)S(1)}, u32[]{:S(2)}, u32[]{:S(2)}) collective-permute-start(bf16[16,4224]{1,0:T(8,128)(2,1)S(1)} %get-tuple-element.159), channel_id=1, source_target_pairs={{0,24},{8,16},{16,8},{24,0},{1,25},{9,17},{17,9},{25,1},{2,26},{10... | collective-permute-start | bytes 405512 | tf_op jit(solution)/shard_map/ppermute | solution.py:595
  70.1 6.2 %collective-permute-start.29 = (bf16[72,512]{1,0:T(8,128)(2,1)S(1)}, bf16[72,512]{1,0:T(8,128)(2,1)S(1)}, u32[]{:S(2)}, u32[]{:S(2)}) collective-permute-start(bf16[72,512]{1,0:T(8,128)(2,1)S(1)} %bitcast.54), channel_id=1, source_target_pairs={{0,1},{1,0},{2,3},{3,2},{4,5},{5,4},{6,7},{7,6},{8,9},{9,8},{10,11... | collective-permute-start | bytes 221192 | tf_op jit(solution)/shard_map/ppermute | solution.py:582
  70.8 6.4 %collective-permute-start.30 = (bf16[72,512]{1,0:T(8,128)(2,1)S(1)}, bf16[72,512]{1,0:T(8,128)(2,1)S(1)}, u32[]{:S(2)}, u32[]{:S(2)}) collective-permute-start(bf16[72,512]{1,0:T(8,128)(2,1)S(1)} %bitcast.53), channel_id=1, source_target_pairs={{0,2},{1,3},{2,0},{3,1},{4,6},{5,7},{6,4},{7,5},{8,10},{9,11},{10,... | collective-permute-start | bytes 221192 | tf_op jit(solution)/shard_map/ppermute | solution.py:582
  72.9 6.0 %collective-permute-start.31 = (bf16[72,512]{1,0:T(8,128)(2,1)S(1)}, bf16[72,512]{1,0:T(8,128)(2,1)S(1)}, u32[]{:S(2)}, u32[]{:S(2)}) collective-permute-start(bf16[72,512]{1,0:T(8,128)(2,1)S(1)} %bitcast.52), channel_id=1, source_target_pairs={{0,3},{1,2},{2,1},{3,0},{4,7},{5,6},{6,5},{7,4},{8,11},{9,10},{10,... | collective-permute-start | bytes 221192 | tf_op jit(solution)/shard_map/ppermute | solution.py:582
  73.7 7.1 %collective-permute-start.26 = (bf16[72,512]{1,0:T(8,128)(2,1)S(1)}, bf16[72,512]{1,0:T(8,128)(2,1)S(1)}, u32[]{:S(2)}, u32[]{:S(2)}) collective-permute-start(bf16[72,512]{1,0:T(8,128)(2,1)S(1)} %bitcast.51), channel_id=1, source_target_pairs={{0,1},{1,0},{2,3},{3,2},{4,5},{5,4},{6,7},{7,6},{8,9},{9,8},{10,11... | collective-permute-start | bytes 221192 | tf_op jit(solution)/shard_map/ppermute | solution.py:582
  74.3 6.5 %collective-permute-start.27 = (bf16[72,512]{1,0:T(8,128)(2,1)S(1)}, bf16[72,512]{1,0:T(8,128)(2,1)S(1)}, u32[]{:S(2)}, u32[]{:S(2)}) collective-permute-start(bf16[72,512]{1,0:T(8,128)(2,1)S(1)} %bitcast.50), channel_id=1, source_target_pairs={{0,2},{1,3},{2,0},{3,1},{4,6},{5,7},{6,4},{7,5},{8,10},{9,11},{10,... | collective-permute-start | bytes 221192 | tf_op jit(solution)/shard_map/ppermute | solution.py:582
  76.3 6.0 %collective-permute-start.28 = (bf16[72,512]{1,0:T(8,128)(2,1)S(1)}, bf16[72,512]{1,0:T(8,128)(2,1)S(1)}, u32[]{:S(2)}, u32[]{:S(2)}) collective-permute-start(bf16[72,512]{1,0:T(8,128)(2,1)S(1)} %bitcast.49), channel_id=1, source_target_pairs={{0,3},{1,2},{2,1},{3,0},{4,7},{5,6},{6,5},{7,4},{8,11},{9,10},{10,... | collective-permute-start | bytes 221192 | tf_op jit(solution)/shard_map/ppermute | solution.py:582
  79.0 6.1 %collective-permute-start.32 = (bf16[72,512]{1,0:T(8,128)(2,1)S(1)}, bf16[72,512]{1,0:T(8,128)(2,1)S(1)}, u32[]{:S(2)}, u32[]{:S(2)}) collective-permute-start(bf16[72,512]{1,0:T(8,128)(2,1)S(1)} %shard_map.198), channel_id=1, source_target_pairs={{0,4},{1,5},{2,6},{3,7},{4,0},{5,1},{6,2},{7,3},{8,12},{9,13},{10,... | collective-permute-start | bytes 221192 | tf_op jit(solution)/shard_map/ppermute | solution.py:582
  85.4 5.5 %collective-permute-start.33 = (bf16[64,512]{1,0:T(8,128)(2,1)S(1)}, bf16[64,512]{1,0:T(8,128)(2,1)S(1)}, u32[]{:S(2)}, u32[]{:S(2)}) collective-permute-start(bf16[64,512]{1,0:T(8,128)(2,1)S(1)} %bitcast.39), channel_id=1, source_target_pairs={{0,4},{1,5},{2,6},{3,7},{4,0},{5,1},{6,2},{7,3},{8,12},{9,13},{10,... | collective-permute-start | bytes 196616 | tf_op jit(solution)/shard_map/ppermute | solution.py:582
  86.4 7.3 %collective-permute-start.39 = (bf16[64,512]{1,0:T(8,128)(2,1)S(1)}, bf16[64,512]{1,0:T(8,128)(2,1)S(1)}, u32[]{:S(2)}, u32[]{:S(2)}) collective-permute-start(bf16[64,512]{1,0:T(8,128)(2,1)S(1)} %bitcast.40), channel_id=1, source_target_pairs={{0,3},{1,2},{2,1},{3,0},{4,7},{5,6},{6,5},{7,4},{8,11},{9,10},{10,... | collective-permute-start | bytes 196616 | tf_op jit(solution)/shard_map/ppermute | solution.py:582
  88.4 5.9 %collective-permute-start.38 = (bf16[64,512]{1,0:T(8,128)(2,1)S(1)}, bf16[64,512]{1,0:T(8,128)(2,1)S(1)}, u32[]{:S(2)}, u32[]{:S(2)}) collective-permute-start(bf16[64,512]{1,0:T(8,128)(2,1)S(1)} %bitcast.41), channel_id=1, source_target_pairs={{0,2},{1,3},{2,0},{3,1},{4,6},{5,7},{6,4},{7,5},{8,10},{9,11},{10,... | collective-permute-start | bytes 196616 | tf_op jit(solution)/shard_map/ppermute | solution.py:582
  88.4 5.9 %collective-permute-start.37 = (bf16[64,512]{1,0:T(8,128)(2,1)S(1)}, bf16[64,512]{1,0:T(8,128)(2,1)S(1)}, u32[]{:S(2)}, u32[]{:S(2)}) collective-permute-start(bf16[64,512]{1,0:T(8,128)(2,1)S(1)} %bitcast.42), channel_id=1, source_target_pairs={{0,1},{1,0},{2,3},{3,2},{4,5},{5,4},{6,7},{7,6},{8,9},{9,8},{10,11... | collective-permute-start | bytes 196616 | tf_op jit(solution)/shard_map/ppermute | solution.py:582
  90.9 6.4 %collective-permute-start.36 = (bf16[64,512]{1,0:T(8,128)(2,1)S(1)}, bf16[64,512]{1,0:T(8,128)(2,1)S(1)}, u32[]{:S(2)}, u32[]{:S(2)}) collective-permute-start(bf16[64,512]{1,0:T(8,128)(2,1)S(1)} %collective-permute-done.33.refs_4_), channel_id=1, source_target_pairs={{0,3},{1,2},{2,1},{3,0},{4,7},{5,6},{6,5},{7,4},{8,11},{9,10},{10,... | collective-permute-start | bytes 196616 | tf_op jit(solution)/shard_map/ppermute | solution.py:582
  122.8 16.1 %all-to-all-start.1 = ((bf16[32,24,256]{2,1,0:T(8,128)(2,1)}), bf16[32,24,256]{2,1,0:T(8,128)(2,1)S(1)}, u32[]{:S(2)}, u32[]{:S(2)}) async-start(bf16[32,24,256]{2,1,0:T(8,128)(2,1)} %bitcast.20), calls=%async_computation.1 | async-start | bytes 786432 | tf_op jit(solution)/shard_map/all_to_all | solution.py:577
  (26 other events, 375.3 us)
